TPU v7x, 128 devices: a whole 4x4x4 slice. The times are simulated.
128 devices in a mesh: dp: 8 (over x, y_lo), seq: 16 (over z, y_hi, core).
Axes of the slice: x: 4, y: 4 (y_hi: 2, y_lo: 2; y = y_hi * 2 + y_lo), z: 4, core: 2. Of those that a mesh axis runs over, the one named last changes fastest.
Arguments:
- tokens: bfloat16 [8, 4096, 768], P('dp', 'seq'), may hold values from -6 to 6
- tile_coords: int32 [8, 2, 4096], P('dp', None, 'seq'), may hold values from 0 to 255
- slide_lengths: int32 [8, 4], P('dp'), may hold values from 1 to 3072, 4096 in all within a row
- norm_gain: float32 [768], replicated, may hold values from 0.25 to 1.75
- norm_bias: float32 [768], replicated, may hold values from -3 to 3
- w_qkv: bfloat16 [768, 2304], replicated, may hold values from -3 to 3
- w_out: bfloat16 [768, 768], replicated, may hold values from -0.21875 to 0.21875
- cotangent: bfloat16 [8, 4096, 768], P('dp', 'seq'), may hold values from -6 to 6
Outputs:
- layer_out: bfloat16 [8, 4096, 768], P('dp', 'seq')
- d_tokens: bfloat16 [8, 4096, 768], P('dp', 'seq')
- d_w_qkv: float32 [768, 2304], replicated
- d_w_out: float32 [768, 768], replicated
- d_gain: float32 [768], replicated
- d_bias: float32 [768], replicated
Inputs may be any that keep to these rules, and one draw needn't show every extreme that they name: `slide_lengths`: every slide has 1 to 3072 tiles, the largest exactly that many, and the lengths of a sequence add up to 4096.
All inputs are finite; a program needn't handle non-finite values.
Results may differ from a plain program's by a relative error of at most 0.035.
The roundings to bfloat16 on the way count: a program that leaves them out, or rounds other values in their place, can miss the bound.
Values may be sent and summed in bfloat16 or wider, within the bound.
No kernel may reach another device: no remote copies, remote signals or barrier semaphores. Data moves between devices by JAX's collectives and lax.ppermute only.
A program may use at most 128 MiB of HBM per device.

v0:
```python
import jax
import jax.numpy as jnp
import numpy as np
from jax import lax
from jax.sharding import PartitionSpec as P

HEADS = 16
GROUP = 4


NEG = -1e30


def partner_2(block, axis, bit):
    count = lax.axis_size(axis)
    route = []
    for low in range(count):
        high = low | 1 << bit
        if high != low and high < count:
            route += [(low, high), (high, low)]
    return lax.ppermute(block, axis, route)


def embed_positions(coords, model_width):
    quarter = model_width // 4
    frequency = 1.0 / 10000.0 ** (jnp.arange(quarter, dtype=jnp.float32) / quarter)
    row_angle = coords[0].astype(jnp.float32)[:, None] * frequency[None, :]
    col_angle = coords[1].astype(jnp.float32)[:, None] * frequency[None, :]
    return jnp.concatenate(
        [jnp.sin(row_angle), jnp.cos(row_angle), jnp.sin(col_angle), jnp.cos(col_angle)], axis=1
    )


def slide_index(lengths, positions):
    ends = jnp.cumsum(lengths, dtype=jnp.int32)
    return jnp.sum((positions[:, None] >= ends[None, :]).astype(jnp.int32), axis=1, dtype=jnp.int32)


def head_marker(dilation):
    return np.arange(dilation)[:, None] == (np.arange(HEADS) % dilation)[None, :]


def pick_heads(block_rows, dilation):
    row_count, model_width = block_rows.shape
    shaped = block_rows.reshape(row_count // dilation, dilation, HEADS, model_width // HEADS)
    chosen = jnp.where(
        head_marker(dilation)[None, :, :, None], shaped, jnp.zeros((), block_rows.dtype)
    )
    return jnp.sum(chosen, axis=1, dtype=block_rows.dtype).reshape(
        row_count // dilation, model_width
    )


def spread_heads(returned, dilation):
    lead, row_count, model_width = returned.shape
    shaped = returned.reshape(lead, row_count, 1, HEADS, model_width // HEADS)
    placed = jnp.where(head_marker(dilation)[None, None, :, :, None], shaped, 0.0)
    return placed.reshape(lead, row_count * dilation, model_width)


def group_marker(dilation, offset, count):
    return np.arange(dilation)[:, None] == ((offset + np.arange(count)) % dilation)[None, :]


def pick_group(block, dilation, offset):
    if dilation == 1:
        return block
    row_count, count, tail = block.shape
    shaped = block.reshape(row_count // dilation, dilation, count, tail)
    chosen = jnp.where(
        group_marker(dilation, offset, count)[None, :, :, None], shaped, jnp.zeros((), block.dtype)
    )
    return jnp.sum(chosen, axis=1, dtype=block.dtype)


def spread_group(picked, dilation, offset, fill_value):
    if dilation == 1:
        return picked
    row_count, count, tail = picked.shape
    placed = jnp.where(
        group_marker(dilation, offset, count)[None, :, :, None], picked[:, None], fill_value
    )
    return placed.reshape(row_count * dilation, count, tail)


def group_residues(dilation, offset, count):
    return jnp.asarray((offset + np.arange(count)) % dilation, dtype=jnp.int32)


def per_device(tokens, tile_coords, slide_lengths, norm_gain, norm_bias, w_qkv, w_out, cotangent):
    tok_rows = tokens[0]
    tok_count, model_width = tok_rows.shape
    head_dim = model_width // HEADS
    scale = head_dim ** (-0.5)
    seq_count = lax.axis_size("seq")
    seq_index = lax.axis_index("seq")
    lengths = slide_lengths[0]
    local_pos = seq_index * tok_count + jnp.arange(tok_count, dtype=jnp.int32)
    mid_start = seq_index // GROUP * GROUP * tok_count
    group_size = 8
    group_width = group_size * head_dim

    def slide_of(base, residues):
        spots = base[:, None] + residues[None, :]
        return slide_index(lengths, spots.reshape(-1)).reshape(spots.shape)

    def masked_scores(q_lv, k_lv, q_ids, k_ids):
        scores = jnp.einsum("qgd,kgd->gqk", q_lv, k_lv, preferred_element_type=jnp.float32) * scale
        return jnp.where(q_ids.T[:, :, None] == k_ids.T[:, None, :], scores, NEG)

    def view_group(block_rows, offset):
        piece = block_rows[:, offset * head_dim : offset * head_dim + group_width]
        return piece.reshape(block_rows.shape[0], group_size, head_dim)

    inputs = tok_rows.astype(jnp.float32) + embed_positions(tile_coords[0], model_width)
    row_mean = jnp.mean(inputs, axis=1, keepdims=True)
    centred = inputs - row_mean
    row_var = jnp.mean(centred * centred, axis=1, keepdims=True)
    inv_std = lax.rsqrt(row_var + 1e-05)
    unit_rows = centred * inv_std
    normed = (unit_rows * norm_gain + norm_bias).astype(jnp.bfloat16)
    projected_qkv = jnp.dot(normed, w_qkv, preferred_element_type=jnp.float32).astype(jnp.bfloat16)
    q_flat = projected_qkv[:, :model_width]
    k_flat = projected_qkv[:, model_width : 2 * model_width]
    v_flat = projected_qkv[:, 2 * model_width :]
    mid_keys = jnp.stack([pick_heads(k_flat, GROUP), pick_heads(v_flat, GROUP)])
    far_keys = jnp.stack([pick_heads(k_flat, seq_count), pick_heads(v_flat, seq_count)])
    mid_all = mid_keys
    for bit_number in range(GROUP.bit_length() - 1):
        partner = partner_2(mid_all, "seq", bit_number)
        upper = jnp.right_shift(seq_index, bit_number) & 1 == 1
        mid_all = jnp.where(
            upper,
            jnp.concatenate([partner, mid_all], axis=1),
            jnp.concatenate([mid_all, partner], axis=1),
        )
    far_all = lax.all_gather(far_keys, "seq", axis=1, tiled=True)
    mid_count = mid_all.shape[1]
    far_count = far_all.shape[1]
    mid_pos = mid_start + GROUP * jnp.arange(mid_count, dtype=jnp.int32)
    far_pos = seq_count * jnp.arange(far_count, dtype=jnp.int32)

    def prepare(offset):
        q_group = view_group(q_flat, offset)
        key_sets = (
            (1, view_group(k_flat, offset), view_group(v_flat, offset), local_pos),
            (GROUP, view_group(mid_all[0], offset), view_group(mid_all[1], offset), mid_pos),
            (seq_count, view_group(far_all[0], offset), view_group(far_all[1], offset), far_pos),
        )
        prepared = []
        for dilation, k_lv, v_lv, key_base in key_sets:
            residues = group_residues(dilation, offset, group_size)
            q_base = seq_index * tok_count + dilation * jnp.arange(
                tok_count // dilation, dtype=jnp.int32
            )
            q_lv = pick_group(q_group, dilation, offset)
            prepared.append(
                (
                    dilation,
                    q_lv,
                    k_lv,
                    v_lv,
                    slide_of(q_base, residues),
                    slide_of(key_base, residues),
                )
            )
        return prepared

    def group_backward(offset, prepared, d_group, output, log_total):
        deltas = jnp.sum(d_group.astype(jnp.float32) * output.astype(jnp.float32), axis=2)
        d_query = jnp.zeros((tok_count, group_size, head_dim), jnp.float32)
        key_grads = []
        for level_number, view_item in enumerate(prepared):
            dilation, q_lv, k_lv, v_lv, q_ids, k_ids = view_item
            scores = masked_scores(q_lv, k_lv, q_ids, k_ids)
            level_lse = pick_group(log_total[:, :, None], dilation, offset)[:, :, 0]
            shares = jnp.exp(scores - level_lse.T[:, :, None])
            d_lv = pick_group(d_group, dilation, offset)
            d_shares = jnp.einsum("qgd,kgd->gqk", d_lv, v_lv, preferred_element_type=jnp.float32)
            level_delta = pick_group(deltas[:, :, None], dilation, offset)[:, :, 0]
            d_scores = (shares * (d_shares - level_delta.T[:, :, None])).astype(jnp.bfloat16)
            dq_part = (
                jnp.einsum("gqk,kgd->qgd", d_scores, k_lv, preferred_element_type=jnp.float32)
                * scale
            )
            d_query = d_query + spread_group(dq_part, dilation, offset, 0.0)
            dv_part = jnp.einsum(
                "gqk,qgd->kgd",
                shares.astype(jnp.bfloat16),
                d_lv,
                preferred_element_type=jnp.float32,
            )
            dk_part = (
                jnp.einsum("gqk,qgd->kgd", d_scores, q_lv, preferred_element_type=jnp.float32)
                * scale
            )
            key_grads.append(dk_part.reshape(dk_part.shape[0], group_width))
            key_grads.append(dv_part.reshape(dv_part.shape[0], group_width))
        return [d_query.reshape(tok_count, group_width)] + key_grads

    offsets = list(range(0, HEADS, group_size))
    prepared_all = [prepare(offset) for offset in offsets]
    group_outputs = []
    group_lse = []
    for offset, prepared in zip(offsets, prepared_all):
        highest = None
        for (
            group_dilation,
            group_q_lv,
            group_k_lv,
            group_v_lv,
            group_q_ids,
            group_k_ids,
        ) in prepared:
            group_scores = masked_scores(group_q_lv, group_k_lv, group_q_ids, group_k_ids)
            spread = spread_group(
                jnp.max(group_scores, axis=2).T[:, :, None], group_dilation, offset, NEG
            )[:, :, 0]
            highest = spread if highest is None else jnp.maximum(highest, spread)
        weighted = jnp.zeros((tok_count, group_size, head_dim), jnp.float32)
        totals = jnp.zeros((tok_count, group_size), jnp.float32)
        for (
            group_dilation,
            group_q_lv,
            group_k_lv,
            group_v_lv,
            group_q_ids,
            group_k_ids,
        ) in prepared:
            group_scores = masked_scores(group_q_lv, group_k_lv, group_q_ids, group_k_ids)
            level_top = pick_group(highest[:, :, None], group_dilation, offset)[:, :, 0]
            group_shares = jnp.exp(group_scores - level_top.T[:, :, None])
            totals = (
                totals
                + spread_group(
                    jnp.sum(group_shares, axis=2).T[:, :, None], group_dilation, offset, 0.0
                )[:, :, 0]
            )
            level_part = jnp.einsum(
                "gqk,kgd->qgd",
                group_shares.astype(jnp.bfloat16),
                group_v_lv,
                preferred_element_type=jnp.float32,
            )
            weighted = weighted + spread_group(level_part, group_dilation, offset, 0.0)
        group_output = (weighted / totals[:, :, None]).astype(jnp.bfloat16)
        output = group_output
        log_total = highest + jnp.log(totals)
        group_outputs.append(output)
        group_lse.append(log_total)
    attended = jnp.concatenate(
        [output.reshape(tok_count, group_width) for output in group_outputs], axis=1
    )
    projected = jnp.dot(attended, w_out, preferred_element_type=jnp.float32)
    layer_out = (inputs + projected).astype(jnp.bfloat16)
    d_out = cotangent[0]
    d_w_out = jnp.einsum("td,te->de", attended, d_out, preferred_element_type=jnp.float32)
    d_attended = jnp.einsum("te,de->td", d_out, w_out, preferred_element_type=jnp.float32).astype(
        jnp.bfloat16
    )
    group_grads = []
    for offset, prepared, output, log_total in zip(offsets, prepared_all, group_outputs, group_lse):
        group_grads.append(
            group_backward(offset, prepared, view_group(d_attended, offset), output, log_total)
        )
    joined = [
        jnp.concatenate([grads[slot] for grads in group_grads], axis=1)
        for slot in range(len(group_grads[0]))
    ]
    d_query, dk_local, dv_local, dk_mid, dv_mid, dk_far, dv_far = joined
    mid_grads = jnp.stack([dk_mid, dv_mid])
    far_grads = jnp.stack([dk_far, dv_far])
    for bit_number in reversed(range(GROUP.bit_length() - 1)):
        half_rows = mid_grads.shape[1] // 2
        lower_half = mid_grads[:, :half_rows]
        upper_half = mid_grads[:, half_rows:]
        upper = jnp.right_shift(seq_index, bit_number) & 1 == 1
        kept_half = jnp.where(upper, upper_half, lower_half)
        sent_half = jnp.where(upper, lower_half, upper_half)
        mid_grads = kept_half + partner_2(sent_half.astype(jnp.bfloat16), "seq", bit_number).astype(
            sent_half.dtype
        )
    far_back = lax.psum_scatter(
        far_grads.astype(jnp.bfloat16), "seq", scatter_dimension=1, tiled=True
    ).astype(jnp.float32)
    mid_spread = spread_heads(mid_grads, GROUP)
    far_spread = spread_heads(far_back, seq_count)
    d_key = dk_local + mid_spread[0] + far_spread[0]
    d_value = dv_local + mid_spread[1] + far_spread[1]
    d_qkv = jnp.concatenate([d_query, d_key, d_value], axis=1).astype(jnp.bfloat16)
    d_w_qkv = jnp.einsum("td,te->de", normed, d_qkv, preferred_element_type=jnp.float32)
    d_normed = jnp.einsum("te,de->td", d_qkv, w_qkv, preferred_element_type=jnp.float32)
    d_gain = jnp.sum(d_normed * unit_rows, axis=0)
    d_bias = jnp.sum(d_normed, axis=0)
    d_unit = d_normed * norm_gain
    d_inputs = inv_std * (
        d_unit
        - jnp.mean(d_unit, axis=1, keepdims=True)
        - unit_rows * jnp.mean(d_unit * unit_rows, axis=1, keepdims=True)
    )
    d_tokens = (d_out.astype(jnp.float32) + d_inputs).astype(jnp.bfloat16)
    summed_grads = lax.psum((d_w_qkv, d_w_out, d_gain, d_bias), ("dp", "seq"))
    return (
        layer_out[None],
        d_tokens[None],
        summed_grads[0],
        summed_grads[1],
        summed_grads[2],
        summed_grads[3],
    )


def solution(mesh):
    return jax.shard_map(
        per_device,
        mesh=mesh,
        in_specs=(
            P("dp", "seq", None),
            P("dp", None, "seq"),
            P("dp", None),
            P(),
            P(),
            P(),
            P(),
            P("dp", "seq", None),
        ),
        out_specs=(P("dp", "seq", None), P("dp", "seq", None), P(), P(), P(), P()),
        check_vma=False,
    )
```

profile of v0, /device:TPU:1, one launch (start us, length us, event | category | flops | bytes accessed | tf_op | source)
XLA Modules:
  0.0 733.5 jit_solution(9653681708044742473)
XLA Ops:
  14.1 2.9 reshape.756
  17.1 2.9 reshape.755
  20.0 3.3 select_reduce_fusion.2
  63.6 2.9 reshape.761
  66.5 2.9 reshape.760
  108.2 2.9 select_reduce_fusion.1
  115.0 30.2 %all_gather.3 = bf16[2,256,768]{2,0,1:T(2,128)(2,1)S(1)} all-gather(bf16[2,16,768]{2,0,1:T(2,128)(2,1)S(1)} %copy.404), channel_id=1, replica_groups=mesh['dp'=8,'seq'=16] {'seq'}, dimensions={1}, use_global_device_ids=true | all-gather | bytes 835584 | tf_op jit(solution)/shard_map/all_gather | solution.py:137
  159.7 3.5 fusion.125
  196.1 3.5 fusion.127
  207.4 2.7 fusion.124
  214.5 2.7 fusion.126
  254.6 3.6 multiply_reduce_fusion.5
  317.2 3.6 multiply_reduce_fusion.4
  343.0 2.9 fusion.44
  348.0 3.4 multiply_convert_fusion.1
  355.5 2.5 convolution_multiply_fusion.7
  365.9 2.9 fusion.42
  379.2 3.4 multiply_convert_fusion
  396.0 2.9 collective-permute-start.2
  420.7 2.5 copy.490
  427.5 3.0 squeeze.23
  430.5 3.0 squeeze.25
  433.5 97.6 %all-reduce.6.cloned.1.call-done = bf16[2,256,768]{2,0,1:T(2,128)(2,1)} async-done(((bf16[2,256,768]{2,0,1:T(2,128)(2,1)}), bf16[2,256,768]{2,0,1:T(2,128)(2,1)}) %all-reduce.6.cloned.1.call-update) | async-done | bytes 786448
  538.3 3.0 squeeze.24
  541.3 3.0 squeeze.26
  548.6 4.2 fusion.77
  552.9 3.1 fusion.13
  556.0 2.7 multiply_reduce_fusion
  558.7 67.7 %all-reduce.1 = (f32[768]{0:T(1024)}, f32[768]{0:T(1024)}) all-reduce(f32[768]{0:T(1024)S(1)} %get-tuple-element.6, f32[768]{0:T(1024)} %get-tuple-element.9), channel_id=1, replica_groups=mesh['dp'=8,'seq'=16] {'dp','seq'}, use_global_device_ids=true, to_apply=%region_57.58 | all-reduce | flops 1536 | bytes 12288 | tf_op jit(solution)/shard_map/psum | solution.py:302
  627.7 2.5 fusion.63
  630.3 88.0 %all-reduce.8.cloned.1.call-done = (f32[768,2304]{1,0:T(8,128)}, f32[768,768]{1,0:T(8,128)}) async-done(((f32[768,2304]{1,0:T(8,128)}, f32[768,768]{1,0:T(8,128)}), (f32[768,2304]{1,0:T(8,128)}, f32[768,768]{1,0:T(8,128)})) %all-reduce.8.cloned.1.call-update) | async-done | bytes 9437200 | tf_op jit(solution)/shard_map/psum | solution.py:302
  718.2 6.6 copy.553
  (373 shorter events, 344.8 us)
Async XLA Ops:
  7.2 4.5 copy-start
  7.2 524.0 %all-reduce.6.cloned.1.call-start = ((), (), s32[]{:S(2)}) async-start(), calls=%async_computation | async-start | bytes 1572864
  12.9 7.1 copy-start.60
  30.1 136.3 %collective-permute-start = (bf16[2,64,768]{2,1,0:T(8,128)(2,1)}, bf16[2,64,768]{2,1,0:T(8,128)(2,1)}, u32[]{:S(2)}, u32[]{:S(2)}) collective-permute-start(bf16[2,64,768]{2,1,0:T(8,128)(2,1)} %constant_dynamic-update-slice_fusion), channel_id=1, source_target_pairs={{0,1},{1,0},{2,3},{3,2},{4,5},{5,4},{6,7},{7,6},{8,9},{9,8},{10,11... | collective-permute-start | bytes 589832 | tf_op jit(solution)/shard_map/ppermute | solution.py:21
  59.2 10.2 %copy-start.62 = (s32[1,4]{1,0:T(1,128)S(1)}, s32[1,4]{1,0:T(1,128)}, u32[]{:S(2)}) copy-start(s32[1,4]{1,0:T(1,128)} %param.58) | copy-start | bytes 52
  157.3 5.9 copy-start.16
  157.4 5.9 copy-start.55
  157.4 6.7 copy-start.12
  157.4 6.7 copy-start.13
  157.4 6.7 copy-start.14
  157.4 6.7 copy-start.15
  157.4 6.7 copy-start.51
  163.2 5.3 copy-start.58
  163.2 5.3 copy-start.59
  168.4 31.3 %collective-permute-start.1 = (bf16[2,128,768]{2,1,0:T(8,128)(2,1)}, bf16[2,128,768]{2,1,0:T(8,128)(2,1)}, u32[]{:S(2)}, u32[]{:S(2)}) collective-permute-start(bf16[2,128,768]{2,1,0:T(8,128)(2,1)} %maximum_select_fusion.1), channel_id=1, source_target_pairs={{0,2},{2,0},{1,3},{3,1},{4,6},{6,4},{5,7},{7,5},{8,10},{10,8},{9,1... | collective-permute-start | bytes 1179656 | tf_op jit(solution)/shard_map/ppermute | solution.py:21
  277.1 4.6 copy-start.29
  326.9 4.6 copy-start.28
  326.9 5.6 copy-start.26
  326.9 5.6 copy-start.27
  329.1 13.9 %copy-start.41 = (f32[256,8]{0,1:T(8,128)S(1)}, f32[256,8]{0,1:T(8,128)}, u32[]{:S(2)}) copy-start(f32[256,8]{0,1:T(8,128)} %get-tuple-element.43) | copy-start | bytes 24580
  358.0 7.8 %copy-start.42 = (f32[256,8]{0,1:T(8,128)S(1)}, f32[256,8]{0,1:T(8,128)}, u32[]{:S(2)}) copy-start(f32[256,8]{0,1:T(8,128)} %get-tuple-element.41) | copy-start | bytes 24580
  392.4 325.9 %all-reduce.8.cloned.1.call-start = ((), (), s32[]{:S(2)}) async-start(), calls=%async_computation.1 | async-start | bytes 18874368 | tf_op jit(solution)/shard_map/psum | solution.py:302
  393.6 6.6 copy-start.5
  393.6 5.4 copy-start.4
  393.6 5.4 copy-start.30
  395.1 5.1 copy-start.6
  396.0 18.7 %collective-permute-start.2 = (bf16[2,128,768]{1,2,0:T(8,128)(2,1)}, bf16[2,128,768]{1,2,0:T(8,128)(2,1)}, u32[]{:S(2)}, u32[]{:S(2)}) collective-permute-start(bf16[2,128,768]{1,2,0:T(8,128)(2,1)} %select_convert_fusion.1), channel_id=1, source_target_pairs={{0,2},{2,0},{1,3},{3,1},{4,6},{6,4},{5,7},{7,5},{8,10},{10,8},{9,1... | collective-permute-start | bytes 1179656 | tf_op jit(solution)/shard_map/ppermute | solution.py:21
  404.1 6.5 copy-start.43
  404.1 6.5 copy-start.54
  416.6 2.9 collective-permute-start.3
  430.5 103.9 %copy-start.57 = (pred[16,16]{1,0:T(8,128)(4,1)S(1)}, pred[16,16]{1,0:T(8,128)(4,1)}, u32[]{:S(2)}) copy-start(pred[16,16]{1,0:T(8,128)(4,1)} %constant.114) | copy-start | bytes 772
  718.2 6.6 copy-start.11
  (37 other events, 100.4 us)
Sparse Core Ops, SparseCore 0:
  392.5 138.6 all-reduce.5
  553.0 165.2 all-reduce.7
where the time goes:
time: 746 us; the launch traced here: 734 us
  local copies, waits for them, and re-layouts  253 us (34%)
  waiting for transfers between devices  186 us (25%)
  blocking collectives  97.9 us (13%)
  matrix products  88.9 us (12%)
  other arithmetic  86.6 us (12%)
  between operations  15.8 us (2%)
    unnamed x3, waiting for transfers between devices  97.7 us
    psum x1, waiting for transfers between devices, per_device(): summed_grads = lax.psum((d_w_qkv, d_w_out, d_gain, d_bias), ('dp', 'seq'))  88 us
    psum x1, blocking collectives, per_device(): summed_grads = lax.psum((d_w_qkv, d_w_out, d_gain, d_bias), ('dp', 'seq'))  67.7 us
    broadcast_in_dim x22, local copies, waits for them, and re-layouts, spread_group(): jnp.where(group_marker(dilation, offset, count)[None, :, :, None], picked...  41.9 us
    slice x21, local copies, waits for them, and re-layouts, view_group(): piece = block_rows[:, offset * head_dim:offset * head_dim + group_width]  33.5 us
    all_gather x1, blocking collectives, per_device(): far_all = lax.all_gather(far_keys, 'seq', axis=1, tiled=True)  30.2 us
    reduce_sum x10, other arithmetic, pick_group(): return jnp.sum(chosen, axis=1, dtype=block.dtype)  17.4 us
    another operation x8, local copies, waits for them, and re-layouts, pick_group(): shaped = block.reshape(row_count // dilation, dilation, count, tail)  17.3 us
  transfers between devices with their start and end apart: 6, of which 2 were waited for; matrix products, arithmetic and copies ran while one was open for 25% of the time, Pallas kernels for 0%

commit v1 on v0

v1 whole, which is shorter than its diff:
```python
import jax
import jax.numpy as jnp
import numpy as np
from jax import lax
from jax.experimental import pallas as pl
from jax.experimental.pallas import tpu as pltpu
from jax.sharding import PartitionSpec as P

HEADS = 16
HD = 48
D = 768
T = 256
SCALE = HD ** (-0.5)
NEG = -1e30
BF = jnp.bfloat16
F32 = jnp.float32
AXES = ("dp", "seq")
VMEM_LIMIT = 56 << 20


def iota(shape, dim):
    return lax.broadcasted_iota(jnp.int32, shape, dim)


def tile_of(i):
    return (i >> 6) + ((i >> 4) & 3) * 4 + (i & 15) * 16


def nt(a, b):
    return lax.dot_general(a, b, (((1,), (1,)), ((), ())), preferred_element_type=F32)


def nn(a, b):
    return lax.dot_general(a, b, (((1,), (0,)), ((), ())), preferred_element_type=F32)


def tn(a, b):
    return lax.dot_general(a, b, (((0,), (0,)), ((), ())), preferred_element_type=F32)


def exact(a, b):
    hi = a.astype(BF)
    rest = a - hi.astype(F32)
    mid = rest.astype(BF)
    low = (rest - mid.astype(F32)).astype(BF)
    return nn(hi, b) + nn(mid, b) + nn(low, b)


def sort_matrix():
    return jnp.where(tile_of(iota((T, T), 0)) == iota((T, T), 1), 1.0, 0.0).astype(BF)


def unsort_matrix():
    return jnp.where(iota((T, T), 0) == tile_of(iota((T, T), 1)), 1.0, 0.0).astype(BF)


def span_mask(lo, shape):
    lane = iota(shape, 1)
    return jnp.where((lane >= lo) & (lane < lo + HD), 1.0, 0.0)


def head_window(h):
    start = HD * h // 128 * 128
    width = 128 if HD * h - start + HD <= 128 else 256
    return start, width


def head_mask(h):
    start, width = head_window(h)
    return span_mask(HD * h - start, (1, width)).astype(BF)


def group_window(g):
    return 192 * g // 128 * 128


def group_mask(g):
    lo = 192 * g - group_window(g) + HD * (iota((T, 256), 0) >> 6)
    return span_mask(lo, (T, 256)).astype(BF)


def far_mask():
    row = iota((T, D), 0)
    lo = HD * ((row >> 6) + 4 * ((row >> 4) & 3))
    return span_mask(lo, (T, D)).astype(BF)


def slide_of(meta, pos):
    end = meta[1]
    out = jnp.where(pos >= end, 1, 0)
    for n in range(2, 5):
        end = end + meta[n]
        out = out + jnp.where(pos >= end, 1, 0)
    return out


def row_ids(meta):
    return slide_of(meta, meta[0] * T + tile_of(iota((T, 1), 0)))


def bias_of(meta, pos):
    return jnp.where(row_ids(meta) == slide_of(meta, pos), 0.0, NEG)


def local_bias(meta):
    return bias_of(meta, meta[0] * T + tile_of(iota((1, T), 1)))


def mid_bias(meta):
    t = iota((T, T), 1)
    slot = t >> 6
    dev = meta[0] ^ (((slot & 1) << 1) | (slot >> 1))
    pos = dev * T + ((t >> 4) & 3) * 4 + (t & 15) * 16 + (iota((T, T), 0) >> 6)
    return bias_of(meta, pos)


def far_bias(meta):
    t = iota((T, T), 1)
    s = t >> 4
    code = ((s & 1) << 1) ^ (((s >> 1) & 1) << 2) ^ (((s >> 2) & 1) * 12) ^ (s >> 3)
    row = iota((T, T), 0)
    pos = (meta[0] ^ code) * T + (t & 15) * 16 + (row >> 6) + 4 * ((row >> 4) & 3)
    return bias_of(meta, pos)


def far_head(b):
    return b // 4 + 4 * (b % 4)


def fold_mid(x, masks):
    out = x[0:64] * masks[0]
    for c in range(1, 4):
        out = out + x[64 * c : 64 * c + 64] * masks[c]
    return out


def fold_far(x, masks):
    out = x[0:16] * masks[0]
    for b in range(1, 16):
        out = out + x[16 * b : 16 * b + 16] * masks[far_head(b)]
    return out


def pack_rows(x, head_masks):
    mids = [
        head_masks[c] + head_masks[4 + c] + head_masks[8 + c] + head_masks[12 + c]
        for c in range(4)
    ]
    return jnp.concatenate([fold_mid(x, mids), fold_far(x, head_masks)], axis=0)


def norm_parts(inputs):
    mean = jnp.mean(inputs, axis=1, keepdims=True)
    centred = inputs - mean
    var = jnp.mean(centred * centred, axis=1, keepdims=True)
    inv_std = lax.rsqrt(var + 1e-05)
    return centred * inv_std, inv_std


def pre_kernel(tok, coords, table, gain, bias, w_qkv, w_out, cot,
               inp_o, norm_o, qkv_o, da_o, cot_o, kv_o, qd_o):
    sort = sort_matrix()
    tok_s = nn(sort, tok[...])
    cot_s = nn(sort, cot[...]).astype(BF)
    grid = iota((T, T), 0)
    parts = []
    for axis in range(2):
        hot = jnp.where(grid == coords[axis : axis + 1, :], 1.0, 0.0).astype(BF)
        hot = nt(sort, hot).astype(BF)
        found = nn(hot, table[...])
        parts.append(found[:, :384] + found[:, 384:768] + found[:, 768:])
    inputs = tok_s + jnp.concatenate(parts, axis=1)
    inp_o[...] = inputs
    unit, _ = norm_parts(inputs)
    normed = (unit * gain[...] + bias[...]).astype(BF)
    norm_o[...] = normed
    qkv = nn(normed, w_qkv[...]).astype(BF)
    qkv_o[...] = qkv
    cot_o[...] = cot_s
    d_att = nt(cot_s, w_out[...]).astype(BF)
    da_o[...] = d_att
    masks = [span_mask(HD * h, (1, D)).astype(BF) for h in range(HEADS)]
    kv_o[:, :D] = pack_rows(qkv[:, D : 2 * D], masks)
    kv_o[:, D:] = pack_rows(qkv[:, 2 * D :], masks)
    qd_o[:, :D] = pack_rows(qkv[:, :D], masks)
    qd_o[:, D:] = pack_rows(d_att, masks)


def soft(scores):
    top = jnp.max(scores, axis=1, keepdims=True)
    shares = jnp.exp(scores - top)
    return top, jnp.sum(shares, axis=1, keepdims=True), shares.astype(BF)


def local_forward_kernel(meta, qkv, o_o, top_o, sum_o):
    bias = local_bias(meta)
    o_o[...] = jnp.zeros_like(o_o)
    lane = iota((T, 128), 1)
    tops = jnp.full((T, 128), NEG, F32)
    sums = jnp.zeros((T, 128), F32)
    for h in range(HEADS):
        s, w = head_window(h)
        mask = head_mask(h)
        q = qkv[:, s : s + w] * mask
        scores = nt(q, qkv[:, D + s : D + s + w]) * SCALE + bias
        top, total, shares = soft(scores)
        tops = jnp.where(lane == h, top, tops)
        sums = jnp.where(lane == h, total, sums)
        o_o[:, s : s + w] += nn(shares, qkv[:, 2 * D + s : 2 * D + s + w] * mask)
    top_o[...] = tops
    sum_o[...] = sums


def pick_all(mine, other, base, lo, width):
    return jnp.concatenate(
        [mine[base : base + 128, lo : lo + width], other[base : base + 128, lo : lo + width]],
        axis=0,
    )


def expand_matrix():
    head = iota((128, D), 0)
    lane = iota((128, D), 1)
    return jnp.where((lane >= head * HD) & (lane < head * HD + HD), 1.0, 0.0).astype(BF)


def gather_matrix():
    lane = iota((D, 128), 0)
    head = iota((D, 128), 1)
    return jnp.where((lane >= head * HD) & (lane < head * HD + HD), 1.0, 0.0).astype(BF)


def remote_forward_kernel(meta, qkv, kv_a, kv_b, o_l, top_l, sum_l, inp, d_att, w_out, cot,
                          att_o, out_o, stat_o, send_o, dw_o):
    lane = iota((T, 128), 1)
    row = iota((T, 128), 0)
    tops_m = jnp.full((T, 128), NEG, F32)
    sums_m = jnp.zeros((T, 128), F32)
    mid = mid_bias(meta)
    mid_parts = []
    for g in range(4):
        s = group_window(g)
        mask = group_mask(g)
        q = qkv[:, s : s + 256] * mask
        scores = nt(q, pick_all(kv_a, kv_b, 0, s, 256)) * SCALE + mid
        top, total, shares = soft(scores)
        here = lane == 4 * g + (row >> 6)
        tops_m = jnp.where(here, top, tops_m)
        sums_m = jnp.where(here, total, sums_m)
        mid_parts.append(nn(shares, pick_all(kv_a, kv_b, 0, D + s, 256)))
    mask = far_mask()
    scores = nt(qkv[:, :D] * mask, pick_all(kv_a, kv_b, 128, 0, D)) * SCALE + far_bias(meta)
    top, total, shares = soft(scores)
    far_part = nn(shares, pick_all(kv_a, kv_b, 128, D, D))
    here = lane == (row >> 6) + 4 * ((row >> 4) & 3)
    tops_f = jnp.where(here, top, NEG)
    sums_f = jnp.where(here, total, 0.0)
    highest = jnp.maximum(jnp.maximum(top_l[...], tops_m), tops_f)
    f_l = jnp.exp(top_l[...] - highest)
    f_m = jnp.exp(tops_m - highest)
    f_f = jnp.exp(tops_f - highest)
    totals = f_l * sum_l[...] + f_m * sums_m + f_f * sums_f
    totals = jnp.where(lane < HEADS, totals, 1.0)
    inverse = 1.0 / totals
    lse = highest + jnp.log(totals)
    w_m = f_m * inverse
    att = o_l[...] * exact(f_l * inverse, expand_matrix())
    w_f = jnp.sum(jnp.where(here, f_f * inverse, 0.0), axis=1, keepdims=True)
    att = att + far_part * w_f * mask.astype(F32)
    att_o[...] = jnp.zeros_like(att_o)
    acc = [att[:, 128 * n : 128 * n + 128] for n in range(6)]
    for g in range(4):
        n = group_window(g) // 128
        w_g = jnp.sum(jnp.where(lane == 4 * g + (row >> 6), w_m, 0.0), axis=1, keepdims=True)
        add = mid_parts[g] * w_g * group_mask(g).astype(F32)
        acc[n] = acc[n] + add[:, :128]
        acc[n + 1] = acc[n + 1] + add[:, 128:]
    att = jnp.concatenate(acc, axis=1).astype(BF)
    att_o[...] = att
    prod = d_att[...].astype(F32) * att.astype(F32)
    delta = exact(prod, gather_matrix())
    stat = jnp.where(lane < HEADS, lse, pltpu.roll(delta, HEADS, 1))
    stat = jnp.where(lane < 2 * HEADS, stat, 0.0)
    stat_o[...] = stat
    one = iota((1, 128), 1)
    send_o[0:64] = fold_mid(stat, [jnp.where((one & 3) == c, 1.0, 0.0) for c in range(4)])
    send_o[64:80] = fold_far(stat, [jnp.where((one & 15) == h, 1.0, 0.0) for h in range(HEADS)])
    layer = (inp[...] + nn(att, w_out[...])).astype(BF)
    out_o[...] = nn(unsort_matrix(), layer).astype(BF)
    dw_o[...] = tn(att, cot[...]).astype(BF)


def pick_mid_column(stat, col):
    return jnp.concatenate(
        [stat[64 * c : 64 * c + 64, col + c : col + c + 1] for c in range(4)], axis=0
    )


def pick_far_column(stat, col):
    return jnp.concatenate(
        [
            stat[16 * b : 16 * b + 16, col + far_head(b) : col + far_head(b) + 1]
            for b in range(16)
        ],
        axis=0,
    )


def query_backward_kernel(meta, qkv, d_att, stat, kv_a, kv_b, dq_o, dk_o, dv_o):
    bias = local_bias(meta)
    dq_o[...] = jnp.zeros_like(dq_o)
    dk_o[...] = jnp.zeros_like(dk_o)
    dv_o[...] = jnp.zeros_like(dv_o)
    for h in range(HEADS):
        s, w = head_window(h)
        mask = head_mask(h)
        q = qkv[:, s : s + w] * mask
        k = qkv[:, D + s : D + s + w] * mask
        da = d_att[:, s : s + w] * mask
        scores = nt(q, k) * SCALE + bias
        shares = jnp.exp(scores - stat[:, h : h + 1])
        d_shares = nt(da, qkv[:, 2 * D + s : 2 * D + s + w])
        ds = (shares * (d_shares - stat[:, HEADS + h : HEADS + h + 1])).astype(BF)
        dq_o[:, s : s + w] += nn(ds, k)
        dk_o[:, s : s + w] += tn(ds, q)
        dv_o[:, s : s + w] += tn(shares.astype(BF), da)
    mid = mid_bias(meta)
    for g in range(4):
        s = group_window(g)
        mask = group_mask(g)
        k = pick_all(kv_a, kv_b, 0, s, 256)
        scores = nt(qkv[:, s : s + 256] * mask, k) * SCALE + mid
        shares = jnp.exp(scores - pick_mid_column(stat, 4 * g))
        d_shares = nt(d_att[:, s : s + 256] * mask, pick_all(kv_a, kv_b, 0, D + s, 256))
        ds = (shares * (d_shares - pick_mid_column(stat, HEADS + 4 * g))).astype(BF)
        dq_o[:, s : s + 256] += nn(ds, k) * mask.astype(F32)
    mask = far_mask()
    k = pick_all(kv_a, kv_b, 128, 0, D)
    scores = nt(qkv[:, :D] * mask, k) * SCALE + far_bias(meta)
    shares = jnp.exp(scores - pick_far_column(stat, 0))
    d_shares = nt(d_att[...] * mask, pick_all(kv_a, kv_b, 128, D, D))
    ds = (shares * (d_shares - pick_far_column(stat, HEADS))).astype(BF)
    dq_o[...] += nn(ds, k) * mask.astype(F32)


def spread_mid(stat_t, row):
    return jnp.concatenate(
        [jnp.broadcast_to(stat_t[row + c : row + c + 1, :], (64, T)) for c in range(4)], axis=0
    )


def spread_far(stat_t, row):
    return jnp.concatenate(
        [
            jnp.broadcast_to(stat_t[row + far_head(b) : row + far_head(b) + 1, :], (16, T))
            for b in range(16)
        ],
        axis=0,
    )


def key_backward_kernel(meta, qkv, qd_a, qd_b, st_a, st_b, dq, dk, dv, inp, normed, gain,
                        w_qkv, cot, tok_o, dw_o, vec_o, dk_s, dv_s):
    dk_s[...] = dk[...]
    dv_s[...] = dv[...]
    stat_t = pick_all(st_a, st_b, 0, 0, 128).T
    mid = mid_bias(meta)
    for g in range(4):
        s = group_window(g)
        mask = group_mask(g)
        mask_f = mask.astype(F32)
        q = pick_all(qd_a, qd_b, 0, s, 256)
        da = pick_all(qd_a, qd_b, 0, D + s, 256)
        scores = nt(qkv[:, D + s : D + s + 256] * mask, q) * SCALE + mid
        shares = jnp.exp(scores - spread_mid(stat_t, 4 * g))
        d_shares = nt(qkv[:, 2 * D + s : 2 * D + s + 256] * mask, da)
        ds = (shares * (d_shares - spread_mid(stat_t, HEADS + 4 * g))).astype(BF)
        dk_s[:, s : s + 256] += nn(ds, q) * mask_f
        dv_s[:, s : s + 256] += nn(shares.astype(BF), da) * mask_f
    stat_t = pick_all(st_a, st_b, 128, 0, 128).T
    mask = far_mask()
    mask_f = mask.astype(F32)
    q = pick_all(qd_a, qd_b, 128, 0, D)
    da = pick_all(qd_a, qd_b, 128, D, D)
    scores = nt(qkv[:, D : 2 * D] * mask, q) * SCALE + far_bias(meta)
    shares = jnp.exp(scores - spread_far(stat_t, 0))
    d_shares = nt(qkv[:, 2 * D :] * mask, da)
    ds = (shares * (d_shares - spread_far(stat_t, HEADS))).astype(BF)
    dk_s[...] += nn(ds, q) * mask_f
    dv_s[...] += nn(shares.astype(BF), da) * mask_f
    d_qkv = jnp.concatenate(
        [
            (dq[...] * SCALE).astype(BF),
            (dk_s[...] * SCALE).astype(BF),
            dv_s[...].astype(BF),
        ],
        axis=1,
    )
    dw_o[...] = tn(normed[...], d_qkv).astype(BF)
    d_normed = nt(d_qkv, w_qkv[...])
    unit, inv_std = norm_parts(inp[...])
    d_gain = jnp.sum(d_normed * unit, axis=0, keepdims=True)
    d_bias = jnp.sum(d_normed, axis=0, keepdims=True)
    vec_o[...] = jnp.concatenate([d_gain, d_bias, jnp.zeros((6, D), F32)], axis=0)
    d_unit = d_normed * gain[...]
    mean_a = jnp.mean(d_unit, axis=1, keepdims=True)
    mean_b = jnp.mean(d_unit * unit, axis=1, keepdims=True)
    d_tok = cot[...].astype(F32) + inv_std * (d_unit - mean_a - unit * mean_b)
    tok_o[...] = nn(unsort_matrix(), d_tok.astype(BF)).astype(BF)


def call(kernel, outs, *args, smem=0, scratch=(), name=None, flops=0):
    specs = [pl.BlockSpec(memory_space=pltpu.SMEM)] * smem
    specs += [pl.BlockSpec(memory_space=pltpu.VMEM)] * (len(args) - smem)
    return pl.pallas_call(
        kernel,
        out_shape=[jax.ShapeDtypeStruct(shape, dtype) for shape, dtype in outs],
        in_specs=specs,
        out_specs=[pl.BlockSpec(memory_space=pltpu.VMEM)] * len(outs),
        scratch_shapes=scratch,
        compiler_params=pltpu.CompilerParams(vmem_limit_bytes=VMEM_LIMIT),
        cost_estimate=pl.CostEstimate(flops=flops, bytes_accessed=4 << 20, transcendentals=0),
        name=name,
    )(*args)


def swap_seq(block, code):
    return lax.ppermute(block, "seq", [(i, i ^ code) for i in range(16)])


def gather_rows(pack):
    from_y = swap_seq(pack, 2)
    far = jnp.concatenate([pack[64:], from_y[64:]], axis=0)
    far = jnp.concatenate([far, swap_seq(far, 4)], axis=0)
    far = jnp.concatenate([far, swap_seq(far, 12)], axis=0)
    mine = jnp.concatenate([pack[:64], from_y[:64], far], axis=0)
    return mine, swap_seq(mine, 1)


def decode(i):
    dp, seq = i // 16, i % 16
    return [dp // 2, (seq // 2) % 2 * 2 + dp % 2, seq // 4, seq % 2]


def encode(x, y, z, core):
    return (x * 2 + y % 2) * 16 + z * 4 + y // 2 * 2 + core


STEPS = [(n // 2, 3 if n % 2 else 1) for n in range(6)]


def step_route(number):
    turn, code = STEPS[number]
    route = []
    for i in range(128):
        place = decode(i)
        axis = (turn + place[3]) % 3
        place[axis] ^= code
        route.append((i, encode(*place)))
    return route


def step_bit(number, coords, core):
    turn, code = STEPS[number]
    v = jnp.where(core == 0, coords[turn % 3], coords[(turn + 1) % 3])
    return (v >> 1) if code == 3 else ((v + 1) >> 1) & 1


SPLITS = [0, 0, 0, 1, 1, 1]


def sum_everywhere(grads, extra):
    dp = lax.axis_index("dp")
    seq = lax.axis_index("seq")
    core = seq & 1
    coords = [dp >> 1, ((seq >> 1) & 1) * 2 + (dp & 1), seq >> 2]
    core_route = [(i, i ^ 1) for i in range(128)]

    def reduce_step(acc, extra, axis, bit, route):
        half = acc.shape[axis] // 2
        keep = lax.dynamic_slice_in_dim(acc, bit * half, half, axis)
        send = lax.dynamic_slice_in_dim(acc, (1 - bit) * half, half, axis).astype(BF)
        rows = jnp.pad(extra.astype(BF), ((0, 0), (0, send.shape[1] - extra.shape[1])))
        got = lax.ppermute(jnp.concatenate([send, rows], axis=0), AXES, route)
        n = send.shape[0]
        return (
            keep.astype(F32) + got[:n].astype(F32),
            extra + got[n:, : extra.shape[1]].astype(F32),
        )

    acc, extra = reduce_step(grads, extra, 0, core, core_route)
    bits = [step_bit(n, coords, core) for n in range(6)]
    for n in range(6):
        acc, extra = reduce_step(acc, extra, SPLITS[n], bits[n], step_route(n))
    block = acc.astype(BF)
    for n in reversed(range(6)):
        got = lax.ppermute(block, AXES, step_route(n))
        axis = SPLITS[n]
        block = jnp.where(
            bits[n] == 1,
            jnp.concatenate([got, block], axis=axis),
            jnp.concatenate([block, got], axis=axis),
        )
    got = lax.ppermute(block, AXES, core_route)
    block = jnp.where(
        core == 1,
        jnp.concatenate([got, block], axis=0),
        jnp.concatenate([block, got], axis=0),
    ).astype(F32)
    return block, extra


def position_table():
    quarter = D // 4
    frequency = 1.0 / 10000.0 ** (np.arange(quarter) / quarter)
    angle = np.arange(256)[:, None] * frequency[None, :]
    exact_values = np.concatenate([np.sin(angle), np.cos(angle)], axis=1).astype(np.float32)
    parts = []
    rest = exact_values
    for _ in range(3):
        part = rest.astype(jnp.bfloat16)
        parts.append(part)
        rest = rest - part.astype(np.float32)
    return np.concatenate(parts, axis=1)


def per_device(tokens, tile_coords, slide_lengths, norm_gain, norm_bias, w_qkv, w_out, cotangent):
    seq = lax.axis_index("seq").astype(jnp.int32)
    meta = jnp.concatenate([seq[None], slide_lengths[0], jnp.zeros((3,), jnp.int32)])
    gain = norm_gain[None]
    table = jnp.asarray(position_table())
    inp, normed, qkv, d_att, cot, kv_pack, qd_pack = call(
        pre_kernel,
        [((T, D), F32), ((T, D), BF), ((T, 3 * D), BF), ((T, D), BF), ((T, D), BF),
         ((80, 2 * D), BF), ((80, 2 * D), BF)],
        tokens[0], tile_coords[0], table, gain, norm_bias[None], w_qkv, w_out, cotangent[0],
        name="pre",
    )
    kv_a, kv_b = gather_rows(kv_pack)
    o_l, top_l, sum_l = call(
        local_forward_kernel,
        [((T, D), F32), ((T, 128), F32), ((T, 128), F32)],
        meta, qkv, smem=1, name="local_forward",
    )
    qd_a, qd_b = gather_rows(qd_pack)
    att, layer_out, stat, stat_pack, dw_out = call(
        remote_forward_kernel,
        [((T, D), BF), ((T, D), BF), ((T, 128), F32), ((80, 128), F32), ((D, D), BF)],
        meta, qkv, kv_a, kv_b, o_l, top_l, sum_l, inp, d_att, w_out, cot,
        smem=1, name="remote_forward",
    )
    st_a, st_b = gather_rows(stat_pack)
    dq, dk, dv = call(
        query_backward_kernel,
        [((T, D), F32)] * 3,
        meta, qkv, d_att, stat, kv_a, kv_b, smem=1, name="query_backward",
    )
    d_tokens, dw_qkv, vecs = call(
        key_backward_kernel,
        [((T, D), BF), ((D, 3 * D), BF), ((8, D), F32)],
        meta, qkv, qd_a, qd_b, st_a, st_b, dq, dk, dv, inp, normed, gain, w_qkv, cot,
        smem=1, name="key_backward",
        scratch=[pltpu.VMEM((T, D), F32), pltpu.VMEM((T, D), F32)],
    )
    extra = jnp.pad(vecs[:2].reshape(4, 384), ((0, 12), (0, 0)))
    total, extra = sum_everywhere(jnp.concatenate([dw_qkv, dw_out], axis=1), extra)
    vec = extra[:4].reshape(2, D)
    return (
        layer_out[None],
        d_tokens[None],
        total[:, : 3 * D],
        total[:, 3 * D :],
        vec[0],
        vec[1],
    )


def solution(mesh):
    return jax.shard_map(
        per_device,
        mesh=mesh,
        in_specs=(
            P("dp", "seq", None),
            P("dp", None, "seq"),
            P("dp", None),
            P(),
            P(),
            P(),
            P(),
            P("dp", "seq", None),
        ),
        out_specs=(P("dp", "seq", None), P("dp", "seq", None), P(), P(), P(), P()),
        check_vma=False,
    )
```

time: 746 us -> 237 us (0.32); the launches traced: 734 us -> 236 us
  local copies, waits for them, and re-layouts: 253 us -> 22.9 us
  blocking collectives: 97.9 us -> 0 us
  matrix products: 88.9 us -> 0 us
  waiting for transfers between devices: 186 us -> 102 us
  other arithmetic: 86.6 us -> 17 us
  starting transfers between devices: 6.08 us -> 56.1 us
  Pallas kernels: 0 us -> 37.3 us
  between operations: 15.8 us -> 1.12 us
    ppermute x4 -> x26, waiting for transfers between devices: 0.01 us -> 102 us  [the longest x7 43.2 us: reduce_step(): got = lax.ppermute(jnp.concatenate([send, rows], axis=0), AXES, route)]
    unnamed x3 -> x0, waiting for transfers between devices: 97.7 us -> none
    dot_general x42 -> x0, matrix products: 88.9 us -> none  [the longest x6 14.9 us: masked_scores(): jnp.einsum('qgd,kgd->gqk', q_lv, k_lv, preferred_element_type=jnp.float32)]
    psum x1 -> x0, waiting for transfers between devices: 88 us -> none  [per_device(): summed_grads = lax.psum((d_w_qkv, d_w_out, d_gain, d_bias), ('dp', 'seq'))]
    psum x1 -> x0, blocking collectives: 67.7 us -> none  [per_device(): summed_grads = lax.psum((d_w_qkv, d_w_out, d_gain, d_bias), ('dp', 'seq'))]
    ppermute x4 -> x26, starting transfers between devices: 6.01 us -> 56.1 us  [the longest x12 24.9 us: swap_seq(): return lax.ppermute(block, 'seq', [(i, i ^ code) for i in range(16)])]
    broadcast_in_dim x24 -> x2, local copies, waits for them, and re-layouts: 46.2 us -> 2.53 us  [the longest x1 1.27 us: per_device(): gain = norm_gain[None]]
    reshape x21 -> x1, local copies, waits for them, and re-layouts: 38 us -> 0.02 us  [per_device(): extra = jnp.pad(vecs[:2].reshape(4, 384), ((0, 12), (0, 0)))]
  transfers between devices with their start and end apart: 6 -> 26, of which waited for: 2 -> 21; matrix products, arithmetic and copies ran while one was open for 25% -> 3% of each run, Pallas kernels for 0% -> 9%
where the time goes in v1:
time: 237 us; the launch traced here: 236 us
  waiting for transfers between devices  102 us (43%)
  starting transfers between devices  56.1 us (24%)
  Pallas kernels  37.3 us (16%)
  local copies, waits for them, and re-layouts  22.9 us (10%)
  other arithmetic  17 us (7%)
    ppermute x7, waiting for transfers between devices, reduce_step(): got = lax.ppermute(jnp.concatenate([send, rows], axis=0), AXES, route)  43.2 us
    pallas_call x5, Pallas kernels, call(): pl.pallas_call(kernel, out_shape=[jax.ShapeDtypeStruct(shape, dtype) for...  37.3 us
    ppermute x6, waiting for transfers between devices, sum_everywhere(): got = lax.ppermute(block, AXES, step_route(n))  35.9 us
    ppermute x12, starting transfers between devices, swap_seq(): return lax.ppermute(block, 'seq', [(i, i ^ code) for i in range(16)])  24.9 us
    ppermute x12, waiting for transfers between devices, swap_seq(): return lax.ppermute(block, 'seq', [(i, i ^ code) for i in range(16)])  20.2 us
    ppermute x1, starting transfers between devices, sum_everywhere(): got = lax.ppermute(block, AXES, core_route)  12.8 us
    ppermute x7, starting transfers between devices, reduce_step(): got = lax.ppermute(jnp.concatenate([send, rows], axis=0), AXES, route)  10.5 us
    unnamed x40, local copies, waits for them, and re-layouts  10.2 us
  transfers between devices with their start and end apart: 26, of which 21 were waited for; matrix products, arithmetic and copies ran while one was open for 3% of the time, Pallas kernels for 9%

profile of v1, /device:TPU:1, one launch (start us, length us, event | category | flops | bytes accessed | tf_op | source)
XLA Modules:
  0.0 236.0 jit_solution(11016510093314418037)
XLA Ops:
  3.2 6.5 %pre.1 = (f32[256,768]{1,0:T(8,128)}, bf16[256,768]{1,0:T(8,128)(2,1)}, bf16[256,2304]{1,0:T(8,128)(2,1)}, bf16[256,768]{1,0:T(8,128)(2,1)}, bf16[256,768]{1,0:T...) custom-call(bf16[256,768]{1,0:T(8,128)(2,1)} %bitcast.7, s32[2,256]{1,0:T(2,128)} %bitcast.9, ...), custom_call_target="tpu_custom_call" | custom-call | bytes 4194304 | tf_op jit(solution)/shard_map/pre/pallas_call | solution.py:415
  9.6 3.7 %collective-permute-start = (bf16[80,1536]{1,0:T(8,128)(2,1)}, bf16[80,1536]{1,0:T(8,128)(2,1)S(1)}, u32[]{:S(2)}, u32[]{:S(2)}) collective-permute-start(bf16[80,1536]{1,0:T(8,128)(2,1)} %get-tuple-element.27), channel_id=1, source_target_pairs={{0,2},{1,3},{2,0},{3,1},{4,6},{5,7},{6,4},{7,5},{8,10},{9,11},{10,... | collective-permute-start | bytes 737288 | tf_op jit(solution)/shard_map/ppermute | solution.py:428
  15.4 3.6 %collective-permute-done = bf16[80,1536]{1,0:T(8,128)(2,1)S(1)} collective-permute-done((bf16[80,1536]{1,0:T(8,128)(2,1)}, bf16[80,1536]{1,0:T(8,128)(2,1)S(1)}, u32[]{:S(2)}, u32[]{:S(2)}) %collective-permute-start) | collective-permute-done | bytes 245792 | tf_op jit(solution)/shard_map/ppermute | solution.py:428
  21.6 2.7 %collective-permute-done.4 = bf16[80,1536]{1,0:T(8,128)(2,1)S(1)} collective-permute-done((bf16[80,1536]{1,0:T(8,128)(2,1)}, bf16[80,1536]{1,0:T(8,128)(2,1)S(1)}, u32[]{:S(2)}, u32[]{:S(2)}) %collective-permute-start.4) | collective-permute-done | bytes 245792 | tf_op jit(solution)/shard_map/ppermute | solution.py:428
  29.2 3.5 %collective-permute-done.2 = bf16[64,1536]{1,0:T(8,128)(2,1)S(1)} collective-permute-done((bf16[64,1536]{1,0:T(8,128)(2,1)S(1)}, bf16[64,1536]{1,0:T(8,128)(2,1)S(1)}, u32[]{:S(2)}, u32[]{:S(2)}) %collective-permute-start.2) | collective-permute-done | bytes 196640 | tf_op jit(solution)/shard_map/ppermute | solution.py:428
  32.7 3.1 %collective-permute-start.3 = (bf16[256,1536]{1,0:T(8,128)(2,1)S(1)}, bf16[256,1536]{1,0:T(8,128)(2,1)S(1)}, u32[]{:S(2)}, u32[]{:S(2)}) collective-permute-start(bf16[256,1536]{1,0:T(8,128)(2,1)S(1)} %constant_dynamic-update-slice_fusion.kv_a), channel_id=1, source_target_pairs={{0,1},{1,0},{2,3},{3,2},{4,5},{5,4},{6,7},{7,6},{8,9},{9,8},{10,11... | collective-permute-start | bytes 2359304 | tf_op jit(solution)/shard_map/ppermute | solution.py:428
  36.4 4.4 %local_forward.1 = (f32[256,768]{1,0:T(8,128)}, f32[256,128]{1,0:T(8,128)}, f32[256,128]{1,0:T(8,128)}) custom-call(s32[8]{0:T(128)} %pad_add_fusion.1.meta, bf16[256,2304]{1,0:T(8,128)(2,1)} %get-tuple-element.26.qkv), custom_call_target="tpu_custom_call" | custom-call | bytes 4194304 | tf_op jit(solution)/shard_map/local_forward/pallas_call | solution.py:415
  43.3 5.3 %collective-permute-done.6 = bf16[64,1536]{1,0:T(8,128)(2,1)S(1)} collective-permute-done((bf16[64,1536]{1,0:T(8,128)(2,1)S(1)}, bf16[64,1536]{1,0:T(8,128)(2,1)S(1)}, u32[]{:S(2)}, u32[]{:S(2)}) %collective-permute-start.6) | collective-permute-done | bytes 196640 | tf_op jit(solution)/shard_map/ppermute | solution.py:428
  50.5 7.3 %remote_forward.1 = (bf16[256,768]{1,0:T(8,128)(2,1)}, bf16[256,768]{1,0:T(8,128)(2,1)}, f32[256,128]{1,0:T(8,128)}, f32[80,128]{1,0:T(8,128)}, bf16[768,768]{1,0:T(8,128)(2,1)}) custom-call(s32[8]{0:T(128)} %pad_add_fusion.1.meta, bf16[256,2304]{1,0:T(8,128)(2,1)} %get-tuple-element.26.qkv, bf16[256,1536]{1,0:T(8,128)(2,1)} %copy-done.2, ...), custom_call_target="tpu_custom_call" | custom-call | bytes 4194304 | tf_op jit(solution)/shard_map/remote_forward/pallas_call | solution.py:415
  57.8 2.9 %collective-permute-start.8 = (f32[80,128]{1,0:T(8,128)}, f32[80,128]{1,0:T(8,128)S(1)}, u32[]{:S(2)}, u32[]{:S(2)}) collective-permute-start(f32[80,128]{1,0:T(8,128)} %get-tuple-element.36), channel_id=1, source_target_pairs={{0,2},{1,3},{2,0},{3,1},{4,6},{5,7},{6,4},{7,5},{8,10},{9,11},{10,... | collective-permute-start | bytes 122888 | tf_op jit(solution)/shard_map/ppermute | solution.py:428
  63.1 2.6 %collective-permute-done.9 = f32[32,128]{1,0:T(8,128)S(1)} collective-permute-done((f32[32,128]{1,0:T(8,128)S(1)}, f32[32,128]{1,0:T(8,128)S(1)}, u32[]{:S(2)}, u32[]{:S(2)}) %collective-permute-start.9) | collective-permute-done | bytes 16416 | tf_op jit(solution)/shard_map/ppermute | solution.py:428
  69.6 3.6 %collective-permute-start.11 = (f32[256,128]{1,0:T(8,128)S(1)}, f32[256,128]{1,0:T(8,128)S(1)}, u32[]{:S(2)}, u32[]{:S(2)}) collective-permute-start(f32[256,128]{1,0:T(8,128)S(1)} %constant_dynamic-update-slice_fusion.8.st_a), channel_id=1, source_target_pairs={{0,1},{1,0},{2,3},{3,2},{4,5},{5,4},{6,7},{7,6},{8,9},{9,8},{10,11... | collective-permute-start | bytes 393224 | tf_op jit(solution)/shard_map/ppermute | solution.py:428
  73.2 9.8 %query_backward.1 = (f32[256,768]{1,0:T(8,128)}, f32[256,768]{1,0:T(8,128)}, f32[256,768]{1,0:T(8,128)}) custom-call(s32[8]{0:T(128)} %pad_add_fusion.1.meta, bf16[256,2304]{1,0:T(8,128)(2,1)} %get-tuple-element.26.qkv, bf16[256,768]{1,0:T(8,128)(2,1)} %get-tuple-element.32.d_att, f32[256,128]{1,0:T(8,128)} %get-tuple-element.37.stat, ...), custom_call_target="tpu_custom_call" | custom-call | bytes 4194304 | tf_op jit(solution)/shard_map/query_backward/pallas_call | solution.py:415
  84.0 9.4 %key_backward.1 = (bf16[256,768]{1,0:T(8,128)(2,1)}, bf16[768,2304]{1,0:T(8,128)(2,1)}, f32[8,768]{1,0:T(8,128)}) custom-call(s32[8]{0:T(128)} %pad_add_fusion.1.meta, bf16[256,2304]{1,0:T(8,128)(2,1)} %get-tuple-element.26.qkv, bf16[256,1536]{1,0:T(8,128)(2,1)} %copy-done.4, bf16[256,1536]{1,0:T(8,128)(2,1)} %copy-done.6, f32[256,128]{1,0:T(8,128)} %copy-done.9, ...), custom_call_target="tpu_custom_call" | custom-call | bytes 4194304 | tf_op jit(solution)/shard_map/key_backward/pallas_call | solution.py:415
  94.1 2.6 %constant_dynamic-update-slice_fusion.15 = bf16[768,3072]{1,0:T(8,128)(2,1)S(1)} fusion(bf16[768,2304]{1,0:T(8,128)(2,1)} %get-tuple-element.43), kind=kLoop, calls=%fused_computation.63 | loop fusion | bytes 7077888
  99.6 4.8 %collective-permute-done.12 = bf16[400,3072]{1,0:T(8,128)(2,1)} collective-permute-done((bf16[400,3072]{1,0:T(8,128)(2,1)S(1)}, bf16[400,3072]{1,0:T(8,128)(2,1)}, u32[]{:S(2)}, u32[]{:S(2)}) %collective-permute-start.12) | collective-permute-done | bytes 2457632 | tf_op jit(solution)/shard_map/ppermute | solution.py:484
  104.3 3.2 %convert_add_fusion = f32[384,3072]{1,0:T(8,128)S(1)} fusion(bf16[400,3072]{1,0:T(8,128)(2,1)} %collective-permute-done.12, bf16[768,3072]{1,0:T(8,128)(2,1)} %copy-done.1, s32[]{:T(128)S(6)} %select_n.121), kind=kLoop, calls=%fused_computation.4 | loop fusion | flops 3538944 | bytes 9437188 | tf_op jit(solution)/shard_map/add | solution.py:487
  111.1 15.2 %collective-permute-done.13 = bf16[208,3072]{1,0:T(8,128)(2,1)} collective-permute-done((bf16[208,3072]{1,0:T(8,128)(2,1)S(1)}, bf16[208,3072]{1,0:T(8,128)(2,1)}, u32[]{:S(2)}, u32[]{:S(2)}) %collective-permute-start.13) | collective-permute-done | bytes 1277984 | tf_op jit(solution)/shard_map/ppermute | solution.py:484
  129.4 2.8 %collective-permute-start.14 = (bf16[112,3072]{1,0:T(8,128)(2,1)S(1)}, bf16[112,3072]{1,0:T(8,128)(2,1)}, u32[]{:S(2)}, u32[]{:S(2)}) collective-permute-start(bf16[112,3072]{1,0:T(8,128)(2,1)S(1)} %fusion.7), channel_id=1, source_target_pairs={{0,96},{1,19},{2,98},{3,17},{4,100},{5,23},{6,102},{7,21},{8,104},... | collective-permute-start | bytes 2064392 | tf_op jit(solution)/shard_map/ppermute | solution.py:484
  132.2 8.7 %collective-permute-done.14 = bf16[112,3072]{1,0:T(8,128)(2,1)} collective-permute-done((bf16[112,3072]{1,0:T(8,128)(2,1)S(1)}, bf16[112,3072]{1,0:T(8,128)(2,1)}, u32[]{:S(2)}, u32[]{:S(2)}) %collective-permute-start.14) | collective-permute-done | bytes 688160 | tf_op jit(solution)/shard_map/ppermute | solution.py:484
  143.0 6.9 %collective-permute-done.15 = bf16[64,3072]{1,0:T(8,128)(2,1)S(1)} collective-permute-done((bf16[64,3072]{1,0:T(8,128)(2,1)S(1)}, bf16[64,3072]{1,0:T(8,128)(2,1)S(1)}, u32[]{:S(2)}, u32[]{:S(2)}) %collective-permute-start.15) | collective-permute-done | bytes 393248 | tf_op jit(solution)/shard_map/ppermute | solution.py:484
  152.5 3.4 %collective-permute-done.16 = bf16[64,1536]{1,0:T(8,128)(2,1)S(1)} collective-permute-done((bf16[64,1536]{1,0:T(8,128)(2,1)S(1)}, bf16[64,1536]{1,0:T(8,128)(2,1)S(1)}, u32[]{:S(2)}, u32[]{:S(2)}) %collective-permute-start.16) | collective-permute-done | bytes 196640 | tf_op jit(solution)/shard_map/ppermute | solution.py:484
  157.0 2.6 %collective-permute-done.17 = bf16[64,768]{1,0:T(8,128)(2,1)S(1)} collective-permute-done((bf16[64,768]{1,0:T(8,128)(2,1)S(1)}, bf16[64,768]{1,0:T(8,128)(2,1)S(1)}, u32[]{:S(2)}, u32[]{:S(2)}) %collective-permute-start.17) | collective-permute-done | bytes 98336 | tf_op jit(solution)/shard_map/ppermute | solution.py:484
  168.1 3.2 %collective-permute-done.20 = bf16[48,768]{1,0:T(8,128)(2,1)S(1)} collective-permute-done((bf16[48,768]{1,0:T(8,128)(2,1)S(1)}, bf16[48,768]{1,0:T(8,128)(2,1)S(1)}, u32[]{:S(2)}, u32[]{:S(2)}) %collective-permute-start.20) | collective-permute-done | bytes 73760 | tf_op jit(solution)/shard_map/ppermute | solution.py:497
  173.7 2.9 %collective-permute-done.21 = bf16[48,1536]{1,0:T(8,128)(2,1)S(1)} collective-permute-done((bf16[48,1536]{1,0:T(8,128)(2,1)S(1)}, bf16[48,1536]{1,0:T(8,128)(2,1)S(1)}, u32[]{:S(2)}, u32[]{:S(2)}) %collective-permute-start.21) | collective-permute-done | bytes 147488 | tf_op jit(solution)/shard_map/ppermute | solution.py:497
  176.8 5.5 %collective-permute-done.22 = bf16[48,3072]{1,0:T(8,128)(2,1)S(1)} collective-permute-done((bf16[48,3072]{1,0:T(8,128)(2,1)S(1)}, bf16[48,3072]{1,0:T(8,128)(2,1)S(1)}, u32[]{:S(2)}, u32[]{:S(2)}) %collective-permute-start.22) | collective-permute-done | bytes 294944 | tf_op jit(solution)/shard_map/ppermute | solution.py:497
  182.5 2.7 %collective-permute-start.23 = (bf16[96,3072]{1,0:T(8,128)(2,1)S(1)}, bf16[96,3072]{1,0:T(8,128)(2,1)S(1)}, u32[]{:S(2)}, u32[]{:S(2)}) collective-permute-start(bf16[96,3072]{1,0:T(8,128)(2,1)S(1)} %maximum_select_fusion.3), channel_id=1, source_target_pairs={{0,96},{1,19},{2,98},{3,17},{4,100},{5,23},{6,102},{7,21},{8,104},... | collective-permute-start | bytes 1769480 | tf_op jit(solution)/shard_map/ppermute | solution.py:497
  185.2 7.3 %collective-permute-done.23 = bf16[96,3072]{1,0:T(8,128)(2,1)S(1)} collective-permute-done((bf16[96,3072]{1,0:T(8,128)(2,1)S(1)}, bf16[96,3072]{1,0:T(8,128)(2,1)S(1)}, u32[]{:S(2)}, u32[]{:S(2)}) %collective-permute-start.23) | collective-permute-done | bytes 589856 | tf_op jit(solution)/shard_map/ppermute | solution.py:497
  192.8 15.4 %collective-permute-done.24 = bf16[192,3072]{1,0:T(8,128)(2,1)} collective-permute-done((bf16[192,3072]{1,0:T(8,128)(2,1)S(1)}, bf16[192,3072]{1,0:T(8,128)(2,1)}, u32[]{:S(2)}, u32[]{:S(2)}) %collective-permute-start.24) | collective-permute-done | bytes 1179680 | tf_op jit(solution)/shard_map/ppermute | solution.py:497
  210.4 12.8 %collective-permute-start.25 = (bf16[384,3072]{1,0:T(8,128)(2,1)S(1)}, bf16[384,3072]{1,0:T(8,128)(2,1)}, u32[]{:S(2)}, u32[]{:S(2)}) collective-permute-start(bf16[384,3072]{1,0:T(8,128)(2,1)S(1)} %maximum_select_fusion.1), channel_id=1, source_target_pairs={{0,1},{1,0},{2,3},{3,2},{4,5},{5,4},{6,7},{7,6},{8,9},{9,8},{10,11... | collective-permute-start | bytes 7077896 | tf_op jit(solution)/shard_map/ppermute | solution.py:504
  227.4 3.5 %fusion.1 = f32[768,3072]{1,0:T(8,128)S(1)} fusion(bf16[384,3072]{1,0:T(8,128)(2,1)S(1)} %maximum_select_fusion.1, bf16[384,3072]{1,0:T(8,128)(2,1)} %collective-permute-done.25, pred[]{:T(512)S(6)} %eq.29), kind=kLoop, calls=%fused_computation.3 | loop fusion | flops 23592960 | bytes 14155777 | tf_op jit(solution)/shard_map/convert_element_type | solution.py:509
  232.5 3.5 %slice.148 = f32[768,2304]{1,0:T(8,128)} slice(f32[768,3072]{1,0:T(8,128)S(1)} %fusion.1), slice={[0:768], [0:2304]} | slice | bytes 14155776 | tf_op jit(solution)/shard_map/slice | solution.py:571
  (128 shorter events, 59.6 us)
Async XLA Ops:
  9.6 26.1 %copy-start.14 = (s32[1,4]{1,0:T(1,128)S(1)}, s32[1,4]{1,0:T(1,128)}, u32[]{:S(2)}) copy-start(s32[1,4]{1,0:T(1,128)} %param.11) | copy-start | bytes 52
  9.6 9.4 %collective-permute-start = (bf16[80,1536]{1,0:T(8,128)(2,1)}, bf16[80,1536]{1,0:T(8,128)(2,1)S(1)}, u32[]{:S(2)}, u32[]{:S(2)}) collective-permute-start(bf16[80,1536]{1,0:T(8,128)(2,1)} %get-tuple-element.27), channel_id=1, source_target_pairs={{0,2},{1,3},{2,0},{3,1},{4,6},{5,7},{6,4},{7,5},{8,10},{9,11},{10,... | collective-permute-start | bytes 737288 | tf_op jit(solution)/shard_map/ppermute | solution.py:428
  13.4 10.9 %collective-permute-start.4 = (bf16[80,1536]{1,0:T(8,128)(2,1)}, bf16[80,1536]{1,0:T(8,128)(2,1)S(1)}, u32[]{:S(2)}, u32[]{:S(2)}) collective-permute-start(bf16[80,1536]{1,0:T(8,128)(2,1)} %get-tuple-element.35), channel_id=1, source_target_pairs={{0,2},{1,3},{2,0},{3,1},{4,6},{5,7},{6,4},{7,5},{8,10},{9,11},{10,... | collective-permute-start | bytes 737288 | tf_op jit(solution)/shard_map/ppermute | solution.py:428
  19.9 7.0 %collective-permute-start.1 = (bf16[32,1536]{1,0:T(8,128)(2,1)S(1)}, bf16[32,1536]{1,0:T(8,128)(2,1)S(1)}, u32[]{:S(2)}, u32[]{:S(2)}) collective-permute-start(bf16[32,1536]{1,0:T(8,128)(2,1)S(1)} %pad_maximum_fusion.2), channel_id=1, source_target_pairs={{0,4},{1,5},{2,6},{3,7},{4,0},{5,1},{6,2},{7,3},{8,12},{9,13},{10,... | collective-permute-start | bytes 294920 | tf_op jit(solution)/shard_map/ppermute | solution.py:428
  25.1 15.7 %collective-permute-start.5 = (bf16[32,1536]{1,0:T(8,128)(2,1)S(1)}, bf16[32,1536]{1,0:T(8,128)(2,1)S(1)}, u32[]{:S(2)}, u32[]{:S(2)}) collective-permute-start(bf16[32,1536]{1,0:T(8,128)(2,1)S(1)} %pad_maximum_fusion.3), channel_id=1, source_target_pairs={{0,4},{1,5},{2,6},{3,7},{4,0},{5,1},{6,2},{7,3},{8,12},{9,13},{10,... | collective-permute-start | bytes 294920 | tf_op jit(solution)/shard_map/ppermute | solution.py:428
  26.9 5.8 %collective-permute-start.2 = (bf16[64,1536]{1,0:T(8,128)(2,1)S(1)}, bf16[64,1536]{1,0:T(8,128)(2,1)S(1)}, u32[]{:S(2)}, u32[]{:S(2)}) collective-permute-start(bf16[64,1536]{1,0:T(8,128)(2,1)S(1)} %pad_maximum_fusion), channel_id=1, source_target_pairs={{0,12},{1,13},{2,14},{3,15},{4,8},{5,9},{6,10},{7,11},{8,4},{9,5},... | collective-permute-start | bytes 589832 | tf_op jit(solution)/shard_map/ppermute | solution.py:428
  32.7 16.9 %copy-start.2 = (bf16[256,1536]{1,0:T(8,128)(2,1)}, bf16[256,1536]{1,0:T(8,128)(2,1)S(1)}, u32[]{:S(2)}) copy-start(bf16[256,1536]{1,0:T(8,128)(2,1)S(1)} %constant_dynamic-update-slice_fusion.kv_a) | copy-start | bytes 2359300
  32.7 16.9 %collective-permute-start.3 = (bf16[256,1536]{1,0:T(8,128)(2,1)S(1)}, bf16[256,1536]{1,0:T(8,128)(2,1)S(1)}, u32[]{:S(2)}, u32[]{:S(2)}) collective-permute-start(bf16[256,1536]{1,0:T(8,128)(2,1)S(1)} %constant_dynamic-update-slice_fusion.kv_a), channel_id=1, source_target_pairs={{0,1},{1,0},{2,3},{3,2},{4,5},{5,4},{6,7},{7,6},{8,9},{9,8},{10,11... | collective-permute-start | bytes 2359304 | tf_op jit(solution)/shard_map/ppermute | solution.py:428
  40.8 7.8 %collective-permute-start.6 = (bf16[64,1536]{1,0:T(8,128)(2,1)S(1)}, bf16[64,1536]{1,0:T(8,128)(2,1)S(1)}, u32[]{:S(2)}, u32[]{:S(2)}) collective-permute-start(bf16[64,1536]{1,0:T(8,128)(2,1)S(1)} %pad_maximum_fusion.1), channel_id=1, source_target_pairs={{0,12},{1,13},{2,14},{3,15},{4,8},{5,9},{6,10},{7,11},{8,4},{9,5},... | collective-permute-start | bytes 589832 | tf_op jit(solution)/shard_map/ppermute | solution.py:428
  48.6 34.4 %copy-start.4 = (bf16[256,1536]{1,0:T(8,128)(2,1)}, bf16[256,1536]{1,0:T(8,128)(2,1)S(1)}, u32[]{:S(2)}) copy-start(bf16[256,1536]{1,0:T(8,128)(2,1)S(1)} %constant_dynamic-update-slice_fusion.4.qd_a) | copy-start | bytes 2359300
  48.6 34.4 %collective-permute-start.7 = (bf16[256,1536]{1,0:T(8,128)(2,1)S(1)}, bf16[256,1536]{1,0:T(8,128)(2,1)S(1)}, u32[]{:S(2)}, u32[]{:S(2)}) collective-permute-start(bf16[256,1536]{1,0:T(8,128)(2,1)S(1)} %constant_dynamic-update-slice_fusion.4.qd_a), channel_id=1, source_target_pairs={{0,1},{1,0},{2,3},{3,2},{4,5},{5,4},{6,7},{7,6},{8,9},{9,8},{10,11... | collective-permute-start | bytes 2359304 | tf_op jit(solution)/shard_map/ppermute | solution.py:428
  57.8 4.6 %collective-permute-start.8 = (f32[80,128]{1,0:T(8,128)}, f32[80,128]{1,0:T(8,128)S(1)}, u32[]{:S(2)}, u32[]{:S(2)}) collective-permute-start(f32[80,128]{1,0:T(8,128)} %get-tuple-element.36), channel_id=1, source_target_pairs={{0,2},{1,3},{2,0},{3,1},{4,6},{5,7},{6,4},{7,5},{8,10},{9,11},{10,... | collective-permute-start | bytes 122888 | tf_op jit(solution)/shard_map/ppermute | solution.py:428
  63.0 2.6 %collective-permute-start.9 = (f32[32,128]{1,0:T(8,128)S(1)}, f32[32,128]{1,0:T(8,128)S(1)}, u32[]{:S(2)}, u32[]{:S(2)}) collective-permute-start(f32[32,128]{1,0:T(8,128)S(1)} %pad_maximum_fusion.6), channel_id=1, source_target_pairs={{0,4},{1,5},{2,6},{3,7},{4,0},{5,1},{6,2},{7,3},{8,12},{9,13},{10,... | collective-permute-start | bytes 49160 | tf_op jit(solution)/shard_map/ppermute | solution.py:428
  65.6 4.0 %collective-permute-start.10 = (f32[64,128]{1,0:T(8,128)S(1)}, f32[64,128]{1,0:T(8,128)S(1)}, u32[]{:S(2)}, u32[]{:S(2)}) collective-permute-start(f32[64,128]{1,0:T(8,128)S(1)} %pad_maximum_fusion.5), channel_id=1, source_target_pairs={{0,12},{1,13},{2,14},{3,15},{4,8},{5,9},{6,10},{7,11},{8,4},{9,5},... | collective-permute-start | bytes 98312 | tf_op jit(solution)/shard_map/ppermute | solution.py:428
  69.6 13.4 %collective-permute-start.11 = (f32[256,128]{1,0:T(8,128)S(1)}, f32[256,128]{1,0:T(8,128)S(1)}, u32[]{:S(2)}, u32[]{:S(2)}) collective-permute-start(f32[256,128]{1,0:T(8,128)S(1)} %constant_dynamic-update-slice_fusion.8.st_a), channel_id=1, source_target_pairs={{0,1},{1,0},{2,3},{3,2},{4,5},{5,4},{6,7},{7,6},{8,9},{9,8},{10,11... | collective-permute-start | bytes 393224 | tf_op jit(solution)/shard_map/ppermute | solution.py:428
  99.2 5.1 %collective-permute-start.12 = (bf16[400,3072]{1,0:T(8,128)(2,1)S(1)}, bf16[400,3072]{1,0:T(8,128)(2,1)}, u32[]{:S(2)}, u32[]{:S(2)}) collective-permute-start(bf16[400,3072]{1,0:T(8,128)(2,1)S(1)} %fusion.3), channel_id=1, source_target_pairs={{0,1},{1,0},{2,3},{3,2},{4,5},{5,4},{6,7},{7,6},{8,9},{9,8},{10,11... | collective-permute-start | bytes 7372808 | tf_op jit(solution)/shard_map/ppermute | solution.py:484
  109.8 16.5 %collective-permute-start.13 = (bf16[208,3072]{1,0:T(8,128)(2,1)S(1)}, bf16[208,3072]{1,0:T(8,128)(2,1)}, u32[]{:S(2)}, u32[]{:S(2)}) collective-permute-start(bf16[208,3072]{1,0:T(8,128)(2,1)S(1)} %fusion.5), channel_id=1, source_target_pairs={{0,32},{1,17},{2,34},{3,19},{4,36},{5,21},{6,38},{7,23},{8,40},{9,... | collective-permute-start | bytes 3833864 | tf_op jit(solution)/shard_map/ppermute | solution.py:484
  129.4 11.5 %collective-permute-start.14 = (bf16[112,3072]{1,0:T(8,128)(2,1)S(1)}, bf16[112,3072]{1,0:T(8,128)(2,1)}, u32[]{:S(2)}, u32[]{:S(2)}) collective-permute-start(bf16[112,3072]{1,0:T(8,128)(2,1)S(1)} %fusion.7), channel_id=1, source_target_pairs={{0,96},{1,19},{2,98},{3,17},{4,100},{5,23},{6,102},{7,21},{8,104},... | collective-permute-start | bytes 2064392 | tf_op jit(solution)/shard_map/ppermute | solution.py:484
  142.9 21.0 %copy-start.7 = (f32[16,384]{1,0:T(8,128)}, f32[16,384]{1,0:T(8,128)S(1)}, u32[]{:S(2)}) copy-start(f32[16,384]{1,0:T(8,128)S(1)} %get-tuple-element.47) | copy-start | bytes 73732
  142.9 7.0 %collective-permute-start.15 = (bf16[64,3072]{1,0:T(8,128)(2,1)S(1)}, bf16[64,3072]{1,0:T(8,128)(2,1)S(1)}, u32[]{:S(2)}, u32[]{:S(2)}) collective-permute-start(bf16[64,3072]{1,0:T(8,128)(2,1)S(1)} %fusion.8), channel_id=1, source_target_pairs={{0,16},{1,5},{2,18},{3,7},{4,20},{5,1},{6,22},{7,3},{8,24},{9,13},... | collective-permute-start | bytes 1179656 | tf_op jit(solution)/shard_map/ppermute | solution.py:484
  149.9 26.8 %copy-start.8 = (bf16[64,3072]{1,0:T(8,128)(2,1)}, bf16[64,3072]{1,0:T(8,128)(2,1)S(1)}, u32[]{:S(2)}) copy-start(bf16[64,3072]{1,0:T(8,128)(2,1)S(1)} %collective-permute-done.15) | copy-start | bytes 1179652
  150.1 5.8 %collective-permute-start.16 = (bf16[64,1536]{1,0:T(8,128)(2,1)S(1)}, bf16[64,1536]{1,0:T(8,128)(2,1)S(1)}, u32[]{:S(2)}, u32[]{:S(2)}) collective-permute-start(bf16[64,1536]{1,0:T(8,128)(2,1)S(1)} %fusion.10), channel_id=1, source_target_pairs={{0,18},{1,13},{2,16},{3,15},{4,22},{5,9},{6,20},{7,11},{8,26},{9,5... | collective-permute-start | bytes 589832 | tf_op jit(solution)/shard_map/ppermute | solution.py:484
  155.9 20.7 %copy-start.10 = (bf16[64,1536]{1,0:T(8,128)(2,1)}, bf16[64,1536]{1,0:T(8,128)(2,1)S(1)}, u32[]{:S(2)}) copy-start(bf16[64,1536]{1,0:T(8,128)(2,1)S(1)} %collective-permute-done.16) | copy-start | bytes 589828
  156.0 3.5 %collective-permute-start.17 = (bf16[64,768]{1,0:T(8,128)(2,1)S(1)}, bf16[64,768]{1,0:T(8,128)(2,1)S(1)}, u32[]{:S(2)}, u32[]{:S(2)}) collective-permute-start(bf16[64,768]{1,0:T(8,128)(2,1)S(1)} %fusion.12), channel_id=1, source_target_pairs={{0,4},{1,33},{2,6},{3,35},{4,0},{5,37},{6,2},{7,39},{8,12},{9,41},... | collective-permute-start | bytes 294920 | tf_op jit(solution)/shard_map/ppermute | solution.py:484
  159.6 4.2 %collective-permute-start.18 = (bf16[64,384]{1,0:T(8,128)(2,1)S(1)}, bf16[64,384]{1,0:T(8,128)(2,1)S(1)}, u32[]{:S(2)}, u32[]{:S(2)}) collective-permute-start(bf16[64,384]{1,0:T(8,128)(2,1)S(1)} %pad_maximum_fusion.4), channel_id=1, source_target_pairs={{0,12},{1,97},{2,14},{3,99},{4,8},{5,101},{6,10},{7,103},{8,4},{9,... | collective-permute-start | bytes 147464 | tf_op jit(solution)/shard_map/ppermute | solution.py:484
  163.9 4.1 %collective-permute-start.19 = (bf16[48,384]{1,0:T(8,128)(2,1)S(1)}, bf16[48,384]{1,0:T(8,128)(2,1)S(1)}, u32[]{:S(2)}, u32[]{:S(2)}) collective-permute-start(bf16[48,384]{1,0:T(8,128)(2,1)S(1)} %add_convert_fusion), channel_id=1, source_target_pairs={{0,12},{1,97},{2,14},{3,99},{4,8},{5,101},{6,10},{7,103},{8,4},{9,... | collective-permute-start | bytes 110600 | tf_op jit(solution)/shard_map/ppermute | solution.py:497
  168.0 3.3 %collective-permute-start.20 = (bf16[48,768]{1,0:T(8,128)(2,1)S(1)}, bf16[48,768]{1,0:T(8,128)(2,1)S(1)}, u32[]{:S(2)}, u32[]{:S(2)}) collective-permute-start(bf16[48,768]{1,0:T(8,128)(2,1)S(1)} %maximum_select_fusion.6), channel_id=1, source_target_pairs={{0,4},{1,33},{2,6},{3,35},{4,0},{5,37},{6,2},{7,39},{8,12},{9,41},... | collective-permute-start | bytes 221192 | tf_op jit(solution)/shard_map/ppermute | solution.py:497
  171.3 5.3 %collective-permute-start.21 = (bf16[48,1536]{1,0:T(8,128)(2,1)S(1)}, bf16[48,1536]{1,0:T(8,128)(2,1)S(1)}, u32[]{:S(2)}, u32[]{:S(2)}) collective-permute-start(bf16[48,1536]{1,0:T(8,128)(2,1)S(1)} %maximum_select_fusion.5), channel_id=1, source_target_pairs={{0,18},{1,13},{2,16},{3,15},{4,22},{5,9},{6,20},{7,11},{8,26},{9,5... | collective-permute-start | bytes 442376 | tf_op jit(solution)/shard_map/ppermute | solution.py:497
  176.7 5.7 %collective-permute-start.22 = (bf16[48,3072]{1,0:T(8,128)(2,1)S(1)}, bf16[48,3072]{1,0:T(8,128)(2,1)S(1)}, u32[]{:S(2)}, u32[]{:S(2)}) collective-permute-start(bf16[48,3072]{1,0:T(8,128)(2,1)S(1)} %maximum_select_fusion.4), channel_id=1, source_target_pairs={{0,16},{1,5},{2,18},{3,7},{4,20},{5,1},{6,22},{7,3},{8,24},{9,13},... | collective-permute-start | bytes 884744 | tf_op jit(solution)/shard_map/ppermute | solution.py:497
  182.5 10.0 %collective-permute-start.23 = (bf16[96,3072]{1,0:T(8,128)(2,1)S(1)}, bf16[96,3072]{1,0:T(8,128)(2,1)S(1)}, u32[]{:S(2)}, u32[]{:S(2)}) collective-permute-start(bf16[96,3072]{1,0:T(8,128)(2,1)S(1)} %maximum_select_fusion.3), channel_id=1, source_target_pairs={{0,96},{1,19},{2,98},{3,17},{4,100},{5,23},{6,102},{7,21},{8,104},... | collective-permute-start | bytes 1769480 | tf_op jit(solution)/shard_map/ppermute | solution.py:497
  192.7 15.5 %collective-permute-start.24 = (bf16[192,3072]{1,0:T(8,128)(2,1)S(1)}, bf16[192,3072]{1,0:T(8,128)(2,1)}, u32[]{:S(2)}, u32[]{:S(2)}) collective-permute-start(bf16[192,3072]{1,0:T(8,128)(2,1)S(1)} %maximum_select_fusion.2), channel_id=1, source_target_pairs={{0,32},{1,17},{2,34},{3,19},{4,36},{5,21},{6,38},{7,23},{8,40},{9,... | collective-permute-start | bytes 3538952 | tf_op jit(solution)/shard_map/ppermute | solution.py:497
  210.4 17.1 %collective-permute-start.25 = (bf16[384,3072]{1,0:T(8,128)(2,1)S(1)}, bf16[384,3072]{1,0:T(8,128)(2,1)}, u32[]{:S(2)}, u32[]{:S(2)}) collective-permute-start(bf16[384,3072]{1,0:T(8,128)(2,1)S(1)} %maximum_select_fusion.1), channel_id=1, source_target_pairs={{0,1},{1,0},{2,3},{3,2},{4,5},{5,4},{6,7},{7,6},{8,9},{9,8},{10,11... | collective-permute-start | bytes 7077896 | tf_op jit(solution)/shard_map/ppermute | solution.py:504
  (9 other events, 38.7 us)

commit v2 on v1

v2 whole, which is shorter than its diff:
```python
import functools

import jax
import jax.numpy as jnp
import numpy as np
from jax import lax
from jax.experimental import pallas as pl
from jax.experimental.pallas import tpu as pltpu
from jax.sharding import PartitionSpec as P

HEADS = 16
HD = 48
D = 768
T = 256
SCALE = HD ** (-0.5)
NEG = -1e30
BF = jnp.bfloat16
F32 = jnp.float32
AXES = ("dp", "seq")
WIDE = 384


def iota(shape, dim):
    return lax.broadcasted_iota(jnp.int32, shape, dim)


def tile_of(i):
    return (i >> 6) + ((i >> 4) & 3) * 4 + (i & 15) * 16


def nt(a, b):
    return lax.dot_general(a, b, (((1,), (1,)), ((), ())), preferred_element_type=F32)


def nn(a, b):
    return lax.dot_general(a, b, (((1,), (0,)), ((), ())), preferred_element_type=F32)


def tn(a, b):
    return lax.dot_general(a, b, (((0,), (0,)), ((), ())), preferred_element_type=F32)


def exact(a, b):
    hi = a.astype(BF)
    rest = a - hi.astype(F32)
    mid = rest.astype(BF)
    low = (rest - mid.astype(F32)).astype(BF)
    return nn(hi, b) + nn(mid, b) + nn(low, b)


def sort_matrix():
    return jnp.where(tile_of(iota((T, T), 0)) == iota((T, T), 1), 1.0, 0.0).astype(BF)


def unsort_matrix():
    return jnp.where(iota((T, T), 0) == tile_of(iota((T, T), 1)), 1.0, 0.0).astype(BF)


def span_mask(lo, shape):
    lane = iota(shape, 1)
    return jnp.where((lane >= lo) & (lane < lo + HD), 1.0, 0.0)


def head_window(h):
    start = HD * h // 128 * 128
    width = 128 if HD * h - start + HD <= 128 else 256
    return start, width


def head_mask(h):
    start, width = head_window(h)
    return span_mask(HD * h - start, (1, width)).astype(BF)


def group_window(g):
    return 192 * g // 128 * 128


def group_mask(g):
    lo = 192 * g - group_window(g) + HD * (iota((T, 256), 0) >> 6)
    return span_mask(lo, (T, 256)).astype(BF)


def far_mask():
    row = iota((T, D), 0)
    lo = HD * ((row >> 6) + 4 * ((row >> 4) & 3))
    return span_mask(lo, (T, D)).astype(BF)


def slide_of(meta, pos):
    end = meta[1]
    out = jnp.where(pos >= end, 1, 0)
    for n in range(2, 5):
        end = end + meta[n]
        out = out + jnp.where(pos >= end, 1, 0)
    return out


def row_ids(meta):
    return slide_of(meta, meta[0] * T + tile_of(iota((T, 1), 0)))


def bias_of(meta, pos):
    return jnp.where(row_ids(meta) == slide_of(meta, pos), 0.0, NEG)


def local_bias(meta):
    return bias_of(meta, meta[0] * T + tile_of(iota((1, T), 1)))


def mid_bias(meta):
    t = iota((T, T), 1)
    slot = t >> 6
    dev = meta[0] ^ (((slot & 1) << 1) | (slot >> 1))
    pos = dev * T + ((t >> 4) & 3) * 4 + (t & 15) * 16 + (iota((T, T), 0) >> 6)
    return bias_of(meta, pos)


def far_bias(meta):
    t = iota((T, T), 1)
    s = t >> 4
    code = ((s & 1) << 1) ^ (((s >> 1) & 1) << 2) ^ (((s >> 2) & 1) * 12) ^ (s >> 3)
    row = iota((T, T), 0)
    pos = (meta[0] ^ code) * T + (t & 15) * 16 + (row >> 6) + 4 * ((row >> 4) & 3)
    return bias_of(meta, pos)


def far_head(b):
    return b // 4 + 4 * (b % 4)


def fold_mid(x, masks):
    out = x[0:64] * masks[0]
    for c in range(1, 4):
        out = out + x[64 * c : 64 * c + 64] * masks[c]
    return out


def fold_far(x, masks):
    out = x[0:16] * masks[0]
    for b in range(1, 16):
        out = out + x[16 * b : 16 * b + 16] * masks[far_head(b)]
    return out


def pack_rows(x, head_masks):
    mids = [
        head_masks[c] + head_masks[4 + c] + head_masks[8 + c] + head_masks[12 + c]
        for c in range(4)
    ]
    return jnp.concatenate([fold_mid(x, mids), fold_far(x, head_masks)], axis=0)


def norm_parts(inputs):
    mean = jnp.mean(inputs, axis=1, keepdims=True)
    centred = inputs - mean
    var = jnp.mean(centred * centred, axis=1, keepdims=True)
    inv_std = lax.rsqrt(var + 1e-05)
    return centred * inv_std, inv_std


def pack_masks():
    return [span_mask(HD * h, (1, D)).astype(BF) for h in range(HEADS)]


def key_kernel(tok, coords, table, gain, bias, w_k, w_v, inp_o, norm_o, kv_o, pack_o):
    sort = sort_matrix()
    tok_s = nn(sort, tok[...])
    grid = iota((T, T), 0)
    parts = []
    for axis in range(2):
        hot = jnp.where(grid == coords[axis : axis + 1, :], 1.0, 0.0).astype(BF)
        hot = nt(sort, hot).astype(BF)
        found = nn(hot, table[...])
        parts.append(found[:, :384] + found[:, 384:768] + found[:, 768:])
    inputs = tok_s + jnp.concatenate(parts, axis=1)
    inp_o[...] = inputs
    unit, _ = norm_parts(inputs)
    normed = (unit * gain[...].reshape(1, D) + bias[...].reshape(1, D)).astype(BF)
    norm_o[...] = normed
    masks = pack_masks()
    for n, weight in enumerate((w_k, w_v)):
        part = nn(normed, weight[...]).astype(BF)
        kv_o[:, D * n : D * (n + 1)] = part
        pack_o[:, D * n : D * (n + 1)] = pack_rows(part, masks)


def query_kernel(normed, w_qkv, w_out, cot, q_o, da_o, cot_o, pack_o):
    cot_s = nn(sort_matrix(), cot[...]).astype(BF)
    cot_o[...] = cot_s
    q = nn(normed[...], w_qkv[...]).astype(BF)
    q_o[...] = q
    d_att = nt(cot_s, w_out[...]).astype(BF)
    da_o[...] = d_att
    masks = pack_masks()
    pack_o[:, :D] = pack_rows(q, masks)
    pack_o[:, D:] = pack_rows(d_att, masks)


def soft(scores):
    top = jnp.max(scores, axis=1, keepdims=True)
    shares = jnp.exp(scores - top)
    return top, jnp.sum(shares, axis=1, keepdims=True), shares.astype(BF)


def local_forward_kernel(meta, q_r, kv, o_o, top_o, sum_o, *, first):
    bias = local_bias(meta)
    o_o[...] = jnp.zeros_like(o_o)
    lane = iota((T, 128), 1)
    tops = jnp.full((T, 128), NEG, F32)
    sums = jnp.zeros((T, 128), F32)
    base = HD * first
    for h in range(first, first + 8):
        s, w = head_window(h)
        mask = head_mask(h)
        scores = nt(q_r[:, s : s + w] * mask, kv[:, s : s + w]) * SCALE + bias
        top, total, shares = soft(scores)
        tops = jnp.where(lane == h, top, tops)
        sums = jnp.where(lane == h, total, sums)
        o_o[:, s - base : s - base + w] += nn(shares, kv[:, D + s : D + s + w] * mask)
    top_o[...] = tops
    sum_o[...] = sums


def mid_rows(got, lo, width):
    return jnp.concatenate([got[0][:128, lo : lo + width], got[2][:128, lo : lo + width]], axis=0)


def far_rows(got, lo, width):
    at = slice(lo, lo + width)
    return jnp.concatenate([got[0][128:, at], got[1][:, at], got[2][128:, at], got[3][:, at]], axis=0)


def expand_matrix():
    head = iota((128, D), 0)
    lane = iota((128, D), 1)
    return jnp.where((lane >= head * HD) & (lane < head * HD + HD), 1.0, 0.0).astype(BF)


def gather_matrix():
    lane = iota((D, 128), 0)
    head = iota((D, 128), 1)
    return jnp.where((lane >= head * HD) & (lane < head * HD + HD), 1.0, 0.0).astype(BF)


def remote_forward_kernel(meta, q_r, kv_a1, kv_a2, kv_b1, kv_b2, o_1, top_1, sum_1, o_2, top_2, sum_2, d_att,
                          pack, att_o, stat_o, send_o):
    lane = iota((T, 128), 1)
    row = iota((T, 128), 0)
    got = (kv_a1, kv_a2, kv_b1, kv_b2)
    top_l = jnp.where(lane < 8, top_1[...], top_2[...])
    sum_l = jnp.where(lane < 8, sum_1[...], sum_2[...])
    tops_m = jnp.full((T, 128), NEG, F32)
    sums_m = jnp.zeros((T, 128), F32)
    mid = mid_bias(meta)
    mid_parts = []
    for g in range(4):
        s = group_window(g)
        mask = group_mask(g)
        q = q_r[:, s : s + 256] * mask
        scores = nt(q, mid_rows(got, s, 256)) * SCALE + mid
        top, total, shares = soft(scores)
        here = lane == 4 * g + (row >> 6)
        tops_m = jnp.where(here, top, tops_m)
        sums_m = jnp.where(here, total, sums_m)
        mid_parts.append(nn(shares, mid_rows(got, D + s, 256)))
    mask = far_mask()
    scores = nt(q_r[...] * mask, far_rows(got, 0, D)) * SCALE + far_bias(meta)
    top, total, shares = soft(scores)
    far_part = nn(shares, far_rows(got, D, D))
    here = lane == (row >> 6) + 4 * ((row >> 4) & 3)
    tops_f = jnp.where(here, top, NEG)
    sums_f = jnp.where(here, total, 0.0)
    highest = jnp.maximum(jnp.maximum(top_l, tops_m), tops_f)
    f_l = jnp.exp(top_l - highest)
    f_m = jnp.exp(tops_m - highest)
    f_f = jnp.exp(tops_f - highest)
    totals = f_l * sum_l + f_m * sums_m + f_f * sums_f
    totals = jnp.where(lane < HEADS, totals, 1.0)
    inverse = 1.0 / totals
    lse = highest + jnp.log(totals)
    w_m = f_m * inverse
    o_l = jnp.concatenate([o_1[...], o_2[...]], axis=1)
    att = o_l * exact(f_l * inverse, expand_matrix())
    w_f = jnp.sum(jnp.where(here, f_f * inverse, 0.0), axis=1, keepdims=True)
    att = att + far_part * w_f * mask.astype(F32)
    acc = [att[:, 128 * n : 128 * n + 128] for n in range(6)]
    for g in range(4):
        n = group_window(g) // 128
        w_g = jnp.sum(jnp.where(lane == 4 * g + (row >> 6), w_m, 0.0), axis=1, keepdims=True)
        add = mid_parts[g] * w_g * group_mask(g).astype(F32)
        acc[n] = acc[n] + add[:, :128]
        acc[n + 1] = acc[n + 1] + add[:, 128:]
    att = jnp.concatenate(acc, axis=1).astype(BF)
    att_o[...] = att
    prod = d_att[...].astype(F32) * att.astype(F32)
    delta = exact(prod, gather_matrix())
    stat = jnp.where(lane < HEADS, lse, pltpu.roll(delta, HEADS, 1))
    stat = jnp.where(lane < 2 * HEADS, stat, 0.0)
    stat_o[...] = stat
    one = iota((1, 128), 1)
    send_o[:, : 2 * D] = pack[...]
    mids = fold_mid(stat, [jnp.where((one & 3) == c, 1.0, 0.0) for c in range(4)])
    fars = fold_far(stat, [jnp.where((one & 15) == h, 1.0, 0.0) for h in range(HEADS)])
    send_o[:, 2 * D :] = three_parts(jnp.concatenate([mids, fars], axis=0))


def three_parts(x):
    lane = iota(x.shape, 1)
    hi = x.astype(BF).astype(F32)
    mid = (x - hi).astype(BF).astype(F32)
    low = x - hi - mid
    parts = jnp.where(lane < 64, pltpu.roll(mid, 32, 1), pltpu.roll(low, 64, 1))
    return jnp.where(lane < 32, hi, parts).astype(BF)


def out_kernel(att, inp, w_out, out_o):
    layer = (inp[...] + nn(att[...], w_out[...])).astype(BF)
    out_o[...] = nn(unsort_matrix(), layer).astype(BF)


def pick_mid_column(stat, col):
    return jnp.concatenate(
        [stat[64 * c : 64 * c + 64, col + c : col + c + 1] for c in range(4)], axis=0
    )


def pick_far_column(stat, col):
    return jnp.concatenate(
        [
            stat[16 * b : 16 * b + 16, col + far_head(b) : col + far_head(b) + 1]
            for b in range(16)
        ],
        axis=0,
    )


def local_backward_kernel(meta, q_r, kv, d_att, stat, dq_o, dk_o, dv_o, *, first):
    bias = local_bias(meta)
    dq_o[...] = jnp.zeros_like(dq_o)
    dk_o[...] = jnp.zeros_like(dk_o)
    dv_o[...] = jnp.zeros_like(dv_o)
    base = HD * first
    for h in range(first, first + 8):
        s, w = head_window(h)
        t = s - base
        mask = head_mask(h)
        q = q_r[:, s : s + w] * mask
        k = kv[:, s : s + w] * mask
        da = d_att[:, s : s + w] * mask
        scores = nt(q, k) * SCALE + bias
        shares = jnp.exp(scores - stat[:, h : h + 1])
        d_shares = nt(da, kv[:, D + s : D + s + w])
        ds = (shares * (d_shares - stat[:, HEADS + h : HEADS + h + 1])).astype(BF)
        dq_o[:, t : t + w] += nn(ds, k)
        dk_o[:, t : t + w] += tn(ds, q)
        dv_o[:, t : t + w] += tn(shares.astype(BF), da)


def query_backward_kernel(meta, q_r, d_att, stat, kv_a1, kv_a2, kv_b1, kv_b2, dq_o):
    got = (kv_a1, kv_a2, kv_b1, kv_b2)
    dq_o[...] = jnp.zeros_like(dq_o)
    mid = mid_bias(meta)
    for g in range(4):
        s = group_window(g)
        mask = group_mask(g)
        k = mid_rows(got, s, 256)
        scores = nt(q_r[:, s : s + 256] * mask, k) * SCALE + mid
        shares = jnp.exp(scores - pick_mid_column(stat, 4 * g))
        d_shares = nt(d_att[:, s : s + 256] * mask, mid_rows(got, D + s, 256))
        ds = (shares * (d_shares - pick_mid_column(stat, HEADS + 4 * g))).astype(BF)
        dq_o[:, s : s + 256] += nn(ds, k) * mask.astype(F32)
    mask = far_mask()
    k = far_rows(got, 0, D)
    scores = nt(q_r[...] * mask, k) * SCALE + far_bias(meta)
    shares = jnp.exp(scores - pick_far_column(stat, 0))
    d_shares = nt(d_att[...] * mask, far_rows(got, D, D))
    ds = (shares * (d_shares - pick_far_column(stat, HEADS))).astype(BF)
    dq_o[...] += nn(ds, k) * mask.astype(F32)


def spread_mid(stat_t, row):
    return jnp.concatenate(
        [jnp.broadcast_to(stat_t[row + c : row + c + 1, :], (64, T)) for c in range(4)], axis=0
    )


def spread_far(stat_t, row):
    return jnp.concatenate(
        [
            jnp.broadcast_to(stat_t[row + far_head(b) : row + far_head(b) + 1, :], (16, T))
            for b in range(16)
        ],
        axis=0,
    )


def joined_stats(rows):
    x = rows.astype(F32).T
    return x[:32] + (x[32:64] + x[64:96])


def key_backward_kernel(meta, kv, qd_a1, qd_a2, qd_b1, qd_b2, dq_r, dq_1, dk_1, dv_1, dq_2, dk_2, dv_2, cot,
                        all_o, kept_o, sent_o, dk_s, dv_s):
    got = (qd_a1, qd_a2, qd_b1, qd_b2)
    half = D // 2
    dk_s[:, :half] = dk_1[...]
    dk_s[:, half:] = dk_2[...]
    dv_s[:, :half] = dv_1[...]
    dv_s[:, half:] = dv_2[...]
    stat_t = joined_stats(mid_rows(got, 2 * D, 128))
    mid = mid_bias(meta)
    for g in range(4):
        s = group_window(g)
        mask = group_mask(g)
        mask_f = mask.astype(F32)
        q = mid_rows(got, s, 256)
        da = mid_rows(got, D + s, 256)
        scores = nt(kv[:, s : s + 256] * mask, q) * SCALE + mid
        shares = jnp.exp(scores - spread_mid(stat_t, 4 * g))
        d_shares = nt(kv[:, D + s : D + s + 256] * mask, da)
        ds = (shares * (d_shares - spread_mid(stat_t, HEADS + 4 * g))).astype(BF)
        dk_s[:, s : s + 256] += nn(ds, q) * mask_f
        dv_s[:, s : s + 256] += nn(shares.astype(BF), da) * mask_f
    stat_t = joined_stats(far_rows(got, 2 * D, 128))
    mask = far_mask()
    mask_f = mask.astype(F32)
    q = far_rows(got, 0, D)
    da = far_rows(got, D, D)
    scores = nt(kv[:, :D] * mask, q) * SCALE + far_bias(meta)
    shares = jnp.exp(scores - spread_far(stat_t, 0))
    d_shares = nt(kv[:, D:] * mask, da)
    ds = (shares * (d_shares - spread_far(stat_t, HEADS))).astype(BF)
    dk_s[...] += nn(ds, q) * mask_f
    dv_s[...] += nn(shares.astype(BF), da) * mask_f
    dq = jnp.concatenate([dq_1[...], dq_2[...]], axis=1) + dq_r[...]
    d_q = (dq * SCALE).astype(BF)
    d_k = (dk_s[...] * SCALE).astype(BF)
    d_v = dv_s[...].astype(BF)
    all_o[:, :D] = d_q
    all_o[:, D : 2 * D] = d_k
    all_o[:, 2 * D :] = d_v
    first = meta[5] == 0
    kept_o[:, :D] = jnp.where(first, d_q, d_v)
    kept_o[:, D:] = jnp.where(first, d_k, cot[...])
    sent_o[:, :D] = jnp.where(first, d_v, d_q)
    sent_o[:, D:] = jnp.where(first, cot[...], d_k)


def weight_grad_kernel(meta, own, other, norm_a, norm_b, att_a, att_b, keep_o, s1, s2, s3, left):
    left[0] = jnp.concatenate([norm_a[...], norm_b[...]], axis=0).T
    left[1] = left[0]

    @pl.when(meta[5] == 1)
    def _():
        left[1] = jnp.concatenate([att_a[...], att_b[...]], axis=0).T

    for d, out in ((2, s2), (1, s1), (3, s3), (0, keep_o)):
        j = (meta[6] + d) & 3
        cols = pl.ds(pl.multiple_of(j * WIDE, 128), WIDE)
        right = jnp.concatenate([own[:, cols], other[:, cols]], axis=0)
        out[...] = nn(left[j >> 1], right).astype(out.dtype)


def token_grad_kernel(d_qkv, w_qkv, inp, gain, cot, tok_o, ext_o):
    d_normed = nt(d_qkv[...], w_qkv[...])
    unit, inv_std = norm_parts(inp[...])
    d_gain = jnp.sum(d_normed * unit, axis=0, keepdims=True)
    d_bias = jnp.sum(d_normed, axis=0, keepdims=True)
    ext_o[...] = two_parts(jnp.concatenate(
        [d_gain[:, :WIDE], d_gain[:, WIDE:], d_bias[:, :WIDE], d_bias[:, WIDE:],
         jnp.zeros((4, WIDE), F32)], axis=0))
    d_unit = d_normed * gain[...].reshape(1, D)
    mean_a = jnp.mean(d_unit, axis=1, keepdims=True)
    mean_b = jnp.mean(d_unit * unit, axis=1, keepdims=True)
    d_tok = cot[...].astype(F32) + inv_std * (d_unit - mean_a - unit * mean_b)
    tok_o[...] = nn(unsort_matrix(), d_tok.astype(BF)).astype(BF)


def two_parts(ext):
    hi = ext.astype(BF)
    return jnp.concatenate([hi, (ext - hi.astype(F32)).astype(BF)], axis=0)


def whole_of(rows):
    return rows[:8].astype(F32) + rows[8:].astype(F32)


def ring_total(meta, slot, own, got, pad):
    pad[meta[slot]] = own
    for d, piece in enumerate(got, 1):
        pad[(meta[slot] - d) & 3] = piece
    return (pad[0] + pad[1]) + (pad[2] + pad[3])


def add_a_kernel(meta, keep, r1, r2, r3, ext, keep_o, s1, s2, s3):
    rows = D // 4
    for d, out in ((2, s2), (1, s1), (3, s3), (0, keep_o)):
        at = pl.ds(pl.multiple_of(((meta[7] + d) & 3) * rows, 16), rows)
        total = keep[at, :] + (r1[at, :].astype(F32) + r2[at, :].astype(F32) + r3[at, :].astype(F32))
        if d == 0:
            out[...] = total
        else:
            out[:rows] = total.astype(BF)
            out[rows:] = ext[...]


def add_b_kernel(meta, keep, r1, r2, r3, ext, out, pad):
    rows = D // 4
    got = (r1, r2, r3)
    total = keep[...]
    for r in got:
        total = total + r[:rows].astype(F32)
    out[:rows] = total.astype(BF)
    sums = ring_total(meta, 7, whole_of(ext[...]), [whole_of(r[rows:]) for r in got], pad)
    out[rows:] = two_parts(sums)


def add_c_kernel(meta, own, r1, r2, r3, out, ext_o, pad, ext_pad):
    rows = D // 4
    got = (r1, r2, r3)
    total = ring_total(meta, 8, own[:rows].astype(F32), [r[:rows].astype(F32) for r in got], pad)
    out[...] = total.astype(BF)
    sums = ring_total(meta, 8, whole_of(own[rows:]), [whole_of(r[rows:]) for r in got], ext_pad)
    ext_o[...] = two_parts(sums)


def merge_kernel(meta, own, r1, r2, r3, ext, out):
    rows = D // 4
    for d, piece in enumerate((own, r1, r2, r3)):
        at = pl.ds(pl.multiple_of(((meta[7] - d) & 3) * rows, 16), rows)
        out[at, :] = piece[...]
    out[D:] = ext[...]


def finish_kernel(meta, *refs, turns, first, last):
    count = 2 * len(turns)
    pieces, refs = refs[:count], refs[count:]
    if last:
        tails, refs = refs[:8], refs[8:]
    if not first:
        refs = refs[2:]
    qkv_o, out_o, *refs = refs
    if last:
        gain_o, bias_o, *refs = refs
    wide, sems, *refs = refs
    for n, piece in enumerate(pieces):
        half = n // len(turns)
        chunk = (meta[5] ^ half) * 4 + ((meta[6 if half == 0 else 9] - turns[n % len(turns)]) & 3)
        wide[n] = piece[...].astype(F32)

        @pl.when(chunk < 6)
        def _(n=n, chunk=chunk):
            at = pl.ds(pl.multiple_of(chunk * WIDE, 128), WIDE)
            pltpu.make_async_copy(wide.at[n], qkv_o.at[:, at], sems.at[n]).start()

        @pl.when(chunk >= 6)
        def _(n=n, chunk=chunk):
            at = pl.ds(pl.multiple_of((chunk - 6) * WIDE, 128), WIDE)
            pltpu.make_async_copy(wide.at[n], out_o.at[:, at], sems.at[n]).start()

    if last:
        pad = refs[0]
        for n, tail in enumerate(tails):
            half = n // 4
            place = (meta[6 if half == 0 else 9] - n % 4) & 3
            pad[(meta[5] ^ half) * 4 + place] = whole_of(tail[...])
        total = pad[0]
        for n in range(1, 8):
            total = total + pad[n]
        gain_o[...] = jnp.concatenate([total[0:1], total[1:2]], axis=1).reshape(D)
        bias_o[...] = jnp.concatenate([total[2:3], total[3:4]], axis=1).reshape(D)
    for n in range(count):
        pltpu.make_async_copy(wide.at[n], qkv_o.at[:, pl.ds(0, WIDE)], sems.at[n]).wait()


def finish(meta, pieces, turns, tails, outs):
    first, last = outs is None, tails is not None
    smem = pl.BlockSpec(memory_space=pltpu.SMEM)
    anywhere = pl.BlockSpec(memory_space=pl.ANY)
    head = pl.BlockSpec((D, WIDE), lambda i: (0, 0))
    tail = pl.BlockSpec((16, WIDE), lambda i: (D // 16, 0))
    args = [meta, *pieces] + (list(tails) if last else [])
    in_specs = [smem] + [head] * len(pieces) + ([tail] * 8 if last else [])
    aliases = {}
    if not first:
        aliases = {len(args): 0, len(args) + 1: 1}
        args += list(outs)
        in_specs += [anywhere] * 2
    out_shape = [jax.ShapeDtypeStruct((D, 3 * D), F32), jax.ShapeDtypeStruct((D, D), F32)]
    out_specs = [anywhere] * 2
    scratch = [pltpu.VMEM((len(pieces), D, WIDE), F32), pltpu.SemaphoreType.DMA((len(pieces),))]
    if last:
        out_shape += [jax.ShapeDtypeStruct((D,), F32)] * 2
        out_specs += [pl.BlockSpec((D,), lambda i: (0,))] * 2
        scratch += [pltpu.VMEM((8, 8, WIDE), F32)]
    return pl.pallas_call(
        functools.partial(finish_kernel, turns=turns, first=first, last=last),
        grid=(1,),
        in_specs=in_specs,
        out_specs=out_specs,
        out_shape=out_shape,
        scratch_shapes=scratch,
        input_output_aliases=aliases,
        compiler_params=pltpu.CompilerParams(vmem_limit_bytes=24 << 20),
        name="finish",
    )(*args)


def call(kernel, outs, *args, smem=0, scratch=(), name=None, limit=24, windows=None):
    specs = [pl.BlockSpec(memory_space=pltpu.SMEM)] * smem
    specs += [pl.BlockSpec(memory_space=pltpu.VMEM)] * (len(args) - smem)
    for n, (shape, index) in (windows or {}).items():
        specs[n] = pl.BlockSpec(shape, lambda i, index=index: index)
    return pl.pallas_call(
        kernel,
        grid=(1,) if windows else (),
        out_shape=[jax.ShapeDtypeStruct(shape, dtype) for shape, dtype in outs],
        in_specs=specs,
        out_specs=[pl.BlockSpec(memory_space=pltpu.VMEM)] * len(outs),
        scratch_shapes=scratch,
        compiler_params=pltpu.CompilerParams(vmem_limit_bytes=limit << 20),
        name=name,
    )(*args)


def swap_seq(block, code):
    return lax.ppermute(block, "seq", [(i, i ^ code) for i in range(16)])


def after(*values):
    return lax.optimization_barrier(values)


def join(*blocks):
    return jnp.concatenate(blocks, axis=0)


def decode(i):
    dp, seq = i // 16, i % 16
    return [dp // 2, (seq // 2) % 2 * 2 + dp % 2, seq // 4, seq % 2]


def encode(x, y, z, core):
    return (x * 2 + y % 2) * 16 + z * 4 + y // 2 * 2 + core


def ring_route(stage, d):
    route = []
    for i in range(128):
        place = decode(i)
        axis = (stage + place[3]) % 3
        place[axis] = (place[axis] + d) % 4
        route.append((i, encode(*place)))
    return route


def ring_send(blocks, stage):
    got = {d: lax.ppermute(blocks[d - 1], AXES, ring_route(stage, d)) for d in (2, 1, 3)}
    return got[1], got[2], got[3]


def place_meta(lengths):
    dp = lax.axis_index("dp").astype(jnp.int32)
    seq = lax.axis_index("seq").astype(jnp.int32)
    core = seq & 1
    coords = [dp >> 1, (seq & 2) + (dp & 1), seq >> 2]
    turns = [jnp.where(core == 0, coords[n], coords[(n + 1) % 3]) for n in range(3)]
    other = jnp.where(core == 0, coords[1], coords[0])
    values = jnp.stack([core] + turns + [other])
    return jnp.concatenate([seq[None], lengths, values, jnp.zeros((6,), jnp.int32)])


def sum_everywhere(meta, keep, sends, ext, beside):
    cut = D // 4
    pad = pltpu.VMEM((4, 8, WIDE), F32)
    got = ring_send(sends, 0)
    *got, _ = after(*got, beside)
    keep, *sends = call(
        add_a_kernel,
        [((cut, WIDE), F32)] + [((cut + 16, WIDE), BF)] * 3,
        meta, keep, *got, ext, smem=1, name="add_a",
    )
    got = ring_send(sends, 1)
    block = call(
        add_b_kernel, [((cut + 16, WIDE), BF)],
        meta, keep, *got, ext, smem=1, name="add_b", scratch=[pad],
    )[0]
    got = ring_send([block] * 3, 2)
    block, ext = call(
        add_c_kernel, [((cut, WIDE), BF), ((16, WIDE), BF)],
        meta, block, *got, smem=1, name="add_c",
        scratch=[pltpu.VMEM((4, cut, WIDE), F32), pad],
    )
    got = ring_send([block] * 3, 1)
    block = call(
        merge_kernel, [((D + 16, WIDE), BF)],
        meta, block, *got, ext, smem=1, name="merge_b",
    )[0]
    ring = {d: lax.ppermute(block, AXES, ring_route(0, d)) for d in (1, 3, 2)}
    ring[0] = block
    twin = {0: swap_seq(block, 1)}
    outs = finish(meta, [ring[0], twin[0]], (0,), None, None)
    ring[1], ring[3], *outs = after(ring[1], ring[3], *outs)
    twin[1], twin[3] = swap_seq(ring[1], 1), swap_seq(ring[3], 1)
    outs = finish(meta, [ring[1], ring[3], twin[1], twin[3]], (1, 3), None, outs)
    ring[2], *outs = after(ring[2], *outs)
    twin[2] = swap_seq(ring[2], 1)
    tails = [half[d] for half in (ring, twin) for d in range(4)]
    return finish(meta, [ring[2], twin[2]], (2,), tails, outs)


def position_table():
    quarter = D // 4
    frequency = 1.0 / 10000.0 ** (np.arange(quarter) / quarter)
    angle = np.arange(256)[:, None] * frequency[None, :]
    exact_values = np.concatenate([np.sin(angle), np.cos(angle)], axis=1).astype(np.float32)
    parts = []
    rest = exact_values
    for _ in range(3):
        part = rest.astype(jnp.bfloat16)
        parts.append(part)
        rest = rest - part.astype(np.float32)
    return np.concatenate(parts, axis=1)


def per_device(tokens, tile_coords, slide_lengths, norm_gain, norm_bias, w_qkv, w_out, cotangent):
    meta = place_meta(slide_lengths[0])
    table = jnp.asarray(position_table())
    inp, normed, kv, kv_pack = call(
        key_kernel,
        [((T, D), F32), ((T, D), BF), ((T, 2 * D), BF), ((80, 2 * D), BF)],
        tokens[0], tile_coords[0], table, norm_gain, norm_bias, w_qkv, w_qkv, name="keys",
        windows={5: ((D, D), (0, 1)), 6: ((D, D), (0, 2))},
    )
    from_y = swap_seq(kv_pack, 2)
    norm_b = swap_seq(normed, 1)
    q, d_att, cot, qd_pack = call(
        query_kernel,
        [((T, D), BF), ((T, D), BF), ((T, D), BF), ((80, 2 * D), BF)],
        normed, w_qkv, w_out, cotangent[0], name="queries",
        windows={1: ((D, D), (0, 0))},
    )
    from_y, q, norm_b = after(from_y, q, norm_b)
    far = join(kv_pack[64:], from_y[64:])
    from_z = swap_seq(far, 4)
    o_1, top_1, sum_1 = call(
        functools.partial(local_forward_kernel, first=0),
        [((T, D // 2), F32), ((T, 128), F32), ((T, 128), F32)],
        meta, q, kv, smem=1, name="local_forward",
    )
    from_z, o_1 = after(from_z, o_1)
    part = join(kv_pack[:64], from_y[:64], far, from_z)
    from_z = swap_seq(part[128:], 12)
    part, q = after(part, q)
    o_2, top_2, sum_2 = call(
        functools.partial(local_forward_kernel, first=8),
        [((T, D // 2), F32), ((T, 128), F32), ((T, 128), F32)],
        meta, q, kv, smem=1, name="local_forward",
    )
    twin = swap_seq(part, 1)
    from_z, twin, o_2 = after(from_z, twin, o_2)
    got_kv = (part, from_z, twin, swap_seq(from_z, 1))
    att, stat, pack = call(
        remote_forward_kernel,
        [((T, D), BF), ((T, 128), F32), ((80, 2 * D + 128), BF)],
        meta, q, *got_kv, o_1, top_1, sum_1, o_2, top_2, sum_2, d_att, qd_pack,
        smem=1, name="remote_forward",
    )
    from_y = swap_seq(pack, 2)
    att_b = swap_seq(att, 1)
    grads_1 = call(
        functools.partial(local_backward_kernel, first=0),
        [((T, D // 2), F32)] * 3,
        meta, q, kv, d_att, stat, smem=1, name="local_backward",
    )
    from_y, att_b, *grads_1 = after(from_y, att_b, *grads_1)
    far = join(pack[64:], from_y[64:])
    from_z = swap_seq(far, 4)
    far, q = after(far, q)
    grads_2 = call(
        functools.partial(local_backward_kernel, first=8),
        [((T, D // 2), F32)] * 3,
        meta, q, kv, d_att, stat, smem=1, name="local_backward",
    )
    from_z, *grads_2 = after(from_z, *grads_2)
    part = join(pack[:64], from_y[:64], far, from_z)
    from_z = swap_seq(part[128:], 12)
    part, q = after(part, q)
    dq_r = call(
        query_backward_kernel, [((T, D), F32)],
        meta, q, d_att, stat, *got_kv, smem=1, name="query_backward",
    )[0]
    twin = swap_seq(part, 1)
    from_z, twin, dq_r = after(from_z, twin, dq_r)
    d_qkv, own, sent = call(
        key_backward_kernel,
        [((T, 3 * D), BF), ((T, 2 * D), BF), ((T, 2 * D), BF)],
        meta, kv, part, from_z, twin, swap_seq(from_z, 1), dq_r, *grads_1, *grads_2, cot,
        smem=1, name="key_backward",
        scratch=[pltpu.VMEM((T, D), F32), pltpu.VMEM((T, D), F32)],
    )
    keep, *sends = call(
        weight_grad_kernel,
        [((D, WIDE), F32)] + [((D, WIDE), BF)] * 3,
        meta, own, swap_seq(sent, 1), normed, norm_b, att, att_b,
        smem=1, name="weight_grad",
        scratch=[pltpu.VMEM((2, D, 2 * T), BF)],
    )
    d_tokens, ext = call(
        token_grad_kernel,
        [((T, D), BF), ((16, WIDE), BF)],
        d_qkv, w_qkv, inp, norm_gain, cot, name="token_grad",
    )
    att, _ = after(att, keep)
    layer_out = call(out_kernel, [((T, D), BF)], att, inp, w_out, name="layer_out")[0]
    dw_qkv, dw_out, d_gain, d_bias = sum_everywhere(meta, keep, sends, ext, layer_out)
    return (
        layer_out[None],
        d_tokens[None],
        dw_qkv,
        dw_out,
        d_gain,
        d_bias,
    )


def solution(mesh):
    return jax.shard_map(
        per_device,
        mesh=mesh,
        in_specs=(
            P("dp", "seq", None),
            P("dp", None, "seq"),
            P("dp", None),
            P(),
            P(),
            P(),
            P(),
            P("dp", "seq", None),
        ),
        out_specs=(P("dp", "seq", None), P("dp", "seq", None), P(), P(), P(), P()),
        check_vma=False,
    )
```

time: 237 us -> 165 us (0.70)
  waiting for transfers between devices: 102 us -> 55.7 us
  other arithmetic: 17 us -> 1.64 us
  starting transfers between devices: 56.1 us -> 48.3 us
  local copies, waits for them, and re-layouts: 22.9 us -> 17.4 us
  Pallas kernels: 37.3 us -> 40.6 us
    ppermute x14 -> x15, waiting for transfers between devices: 81.4 us -> 38.6 us  [the longest x12 26.3 us: ring_send(): lax.ppermute(blocks[d - 1], AXES, ring_route(stage, d))]
    ppermute x14 -> x15, starting transfers between devices: 31.2 us -> 16.7 us  [the longest x12 14.7 us: ring_send(): lax.ppermute(blocks[d - 1], AXES, ring_route(stage, d))]
    add x7 -> x0, other arithmetic: 7.49 us -> none  [the longest x6 6.71 us: reduce_step(): keep.astype(F32) + got[:n].astype(F32)]
    slice x10 -> x6, local copies, waits for them, and re-layouts: 8.21 us -> 1.32 us  [the longest x2 1.27 us: per_device(): far = join(kv_pack[64:], from_y[64:])]
    ppermute x12 -> x17, starting transfers between devices: 24.9 us -> 31.6 us  [swap_seq(): return lax.ppermute(block, 'seq', [(i, i ^ code) for i in range(16)])]
    convert_element_type x8 -> x0, other arithmetic: 5.77 us -> none  [the longest x1 3.49 us: sum_everywhere(): block = jnp.where(core == 1, jnp.concatenate([got, block], axis=0), jnp.c...]
    unnamed x40 -> x70, local copies, waits for them, and re-layouts: 10.2 us -> 14.4 us
    pallas_call x5 -> x19, Pallas kernels: 37.3 us -> 40.6 us  [the longest x16 33.1 us: call(): pl.pallas_call(kernel, grid=(1,) if windows else (), out_shape=[jax.Shape...]
  transfers between devices with their start and end apart: 26 -> 32, of which waited for: 21 -> 24; matrix products, arithmetic and copies ran while one was open for 3% -> 1% of each run, Pallas kernels for 9% -> 14%
where the time goes in v2:
time: 165 us
  waiting for transfers between devices  55.7 us (34%)
  starting transfers between devices  48.3 us (29%)
  Pallas kernels  40.6 us (25%)
  local copies, waits for them, and re-layouts  17.4 us (11%)
    pallas_call x16, Pallas kernels, call(): pl.pallas_call(kernel, grid=(1,) if windows else (), out_shape=[jax.Shape...  33.1 us
    ppermute x17, starting transfers between devices, swap_seq(): return lax.ppermute(block, 'seq', [(i, i ^ code) for i in range(16)])  31.6 us
    ppermute x12, waiting for transfers between devices, ring_send(): lax.ppermute(blocks[d - 1], AXES, ring_route(stage, d))  26.3 us
    ppermute x17, waiting for transfers between devices, swap_seq(): return lax.ppermute(block, 'seq', [(i, i ^ code) for i in range(16)])  17.1 us
    ppermute x12, starting transfers between devices, ring_send(): lax.ppermute(blocks[d - 1], AXES, ring_route(stage, d))  14.7 us
    unnamed x70, local copies, waits for them, and re-layouts  14.4 us
    ppermute x3, waiting for transfers between devices, sum_everywhere(): ring = {d: lax.ppermute(block, AXES, ring_route(0, d)) for d in (1, 3, 2)}  12.3 us
    pallas_call x3, Pallas kernels, finish(): pl.pallas_call(functools.partial(finish_kernel, turns=turns, first=first,...  7.48 us
  transfers between devices with their start and end apart: 32, of which 24 were waited for; matrix products, arithmetic and copies ran while one was open for 1% of the time, Pallas kernels for 14%

profile of v2, /device:TPU:1, one launch (start us, length us, event | category | flops | bytes accessed | tf_op | source)
XLA Modules:
  0.0 164.7 jit_solution(3170482611781403311)
XLA Ops:
  0.6 2.0 %copy-done = bf16[768,2304]{1,0:T(8,128)(2,1)S(1)} copy-done((bf16[768,2304]{1,0:T(8,128)(2,1)S(1)}, bf16[768,2304]{1,0:T(8,128)(2,1)}, u32[]{:S(2)}) %copy-start) | copy-done | bytes 3538968
  6.8 2.0 %keys.1 = (f32[256,768]{1,0:T(8,128)S(1)}, bf16[256,768]{1,0:T(8,128)(2,1)S(1)}, bf16[256,1536]{1,0:T(8,128)(2,1)S(1)}, bf16[80,1536]{1,0:T(8,128)(2,1)S(1)}) custom-call(bf16[256,768]{1,0:T(8,128)(2,1)S(1)} %bitcast.12, s32[2,256]{1,0:T(2,128)S(1)} %bitcast.14, bf16[256,1152]{1,0:T(8,128)(2,1)S(1)} %copy-done.18, f32[768]{0:T(1024)S(1)} %copy-done.25, ...), custom_call_target="tpu_custom_call" | custom-call | tf_op jit(solution)/shard_map/keys/pallas_call | solution.py:615
  10.5 3.7 %collective-permute-start = (bf16[80,1536]{1,0:T(8,128)(2,1)S(1)}, bf16[80,1536]{1,0:T(8,128)(2,1)S(1)}, u32[]{:S(2)}, u32[]{:S(2)}) collective-permute-start(bf16[80,1536]{1,0:T(8,128)(2,1)S(1)} %get-tuple-element.89), channel_id=1, source_target_pairs={{0,2},{1,3},{2,0},{3,1},{4,6},{5,7},{6,4},{7,5},{8,10},{9,11},{10,... | collective-permute-start | bytes 737288 | tf_op jit(solution)/shard_map/ppermute | solution.py:628
  33.0 2.8 %collective-permute-start.3 = (bf16[64,1536]{1,0:T(8,128)(2,1)S(1)}, bf16[64,1536]{1,0:T(8,128)(2,1)S(1)}, u32[]{:S(2)}, u32[]{:S(2)}) collective-permute-start(bf16[64,1536]{1,0:T(8,128)(2,1)S(1)} %pad_maximum_fusion.2), channel_id=1, source_target_pairs={{0,12},{1,13},{2,14},{3,15},{4,8},{5,9},{6,10},{7,11},{8,4},{9,5},... | collective-permute-start | bytes 589832 | tf_op jit(solution)/shard_map/ppermute | solution.py:628
  37.6 3.3 %collective-permute-done.3.kv_a2 = bf16[64,1536]{1,0:T(8,128)(2,1)S(1)} collective-permute-done((bf16[64,1536]{1,0:T(8,128)(2,1)S(1)}, bf16[64,1536]{1,0:T(8,128)(2,1)S(1)}, u32[]{:S(2)}, u32[]{:S(2)}) %collective-permute-start.3) | collective-permute-done | bytes 196640 | tf_op jit(solution)/shard_map/ppermute | solution.py:628
  42.7 4.0 %remote_forward.1 = (bf16[256,768]{1,0:T(8,128)(2,1)S(1)}, f32[256,128]{1,0:T(8,128)S(1)}, bf16[80,1664]{1,0:T(8,128)(2,1)S(1)}) custom-call(s32[16]{0:T(128)S(1)} %concatenate.22.meta, bf16[256,768]{1,0:T(8,128)(2,1)S(1)} %copy-done.7, bf16[192,1536]{1,0:T(8,128)(2,1)} %constant_dynamic-update-slice_fusion.kv_a1, ...), custom_call_target="tpu_custom_call" | custom-call | tf_op jit(solution)/shard_map/remote_forward/pallas_call | solution.py:615
  47.3 2.9 %collective-permute-start.6 = (bf16[80,1664]{1,0:T(8,128)(2,1)S(1)}, bf16[80,1664]{1,0:T(8,128)(2,1)S(1)}, u32[]{:S(2)}, u32[]{:S(2)}) collective-permute-start(bf16[80,1664]{1,0:T(8,128)(2,1)S(1)} %get-tuple-element.111), channel_id=1, source_target_pairs={{0,2},{1,3},{2,0},{3,1},{4,6},{5,7},{6,4},{7,5},{8,10},{9,11},{10,... | collective-permute-start | bytes 798728 | tf_op jit(solution)/shard_map/ppermute | solution.py:628
  50.2 3.4 %local_backward.2 = (f32[256,384]{1,0:T(8,128)S(1)}, f32[256,384]{1,0:T(8,128)S(1)}, f32[256,384]{1,0:T(8,128)S(1)}) custom-call(s32[16]{0:T(128)S(1)} %concatenate.22.meta, bf16[256,768]{1,0:T(8,128)(2,1)S(1)} %copy-done.7, bf16[256,1536]{1,0:T(8,128)(2,1)S(1)} %copy-done.4, bf16[256,768]{1,0:T(8,128)(2,1)S(1)} %copy-done.9, ...), custom_call_target="tpu_custom_call" | custom-call | tf_op jit(solution)/shard_map/local_backward/pallas_call | solution.py:615
  53.6 2.9 %collective-permute-done.6 = bf16[80,1664]{1,0:T(8,128)(2,1)S(1)} collective-permute-done((bf16[80,1664]{1,0:T(8,128)(2,1)S(1)}, bf16[80,1664]{1,0:T(8,128)(2,1)S(1)}, u32[]{:S(2)}, u32[]{:S(2)}) %collective-permute-start.6) | collective-permute-done | bytes 266272 | tf_op jit(solution)/shard_map/ppermute | solution.py:628
  56.9 3.4 %local_backward.3 = (f32[256,384]{1,0:T(8,128)S(1)}, f32[256,384]{1,0:T(8,128)S(1)}, f32[256,384]{1,0:T(8,128)S(1)}) custom-call(s32[16]{0:T(128)S(1)} %concatenate.22.meta, bf16[256,768]{1,0:T(8,128)(2,1)S(1)} %copy-done.7, bf16[256,1536]{1,0:T(8,128)(2,1)S(1)} %copy-done.4, bf16[256,768]{1,0:T(8,128)(2,1)S(1)} %copy-done.9, ...), custom_call_target="tpu_custom_call" | custom-call | tf_op jit(solution)/shard_map/local_backward/pallas_call | solution.py:615
  60.4 2.1 %collective-permute-start.10 = (bf16[192,1664]{1,0:T(8,128)(2,1)S(1)}, bf16[192,1664]{1,0:T(8,128)(2,1)S(1)}, u32[]{:S(2)}, u32[]{:S(2)}) collective-permute-start(bf16[192,1664]{1,0:T(8,128)(2,1)S(1)} %pad_maximum_fusion.qd_a1), channel_id=1, source_target_pairs={{0,1},{1,0},{2,3},{3,2},{4,5},{5,4},{6,7},{7,6},{8,9},{9,8},{10,11... | collective-permute-start | bytes 1916936 | tf_op jit(solution)/shard_map/ppermute | solution.py:628
  62.6 2.7 %collective-permute-start.9 = (bf16[64,1664]{1,0:T(8,128)(2,1)S(1)}, bf16[64,1664]{1,0:T(8,128)(2,1)S(1)}, u32[]{:S(2)}, u32[]{:S(2)}) collective-permute-start(bf16[64,1664]{1,0:T(8,128)(2,1)S(1)} %pad_maximum_fusion.1), channel_id=1, source_target_pairs={{0,12},{1,13},{2,14},{3,15},{4,8},{5,9},{6,10},{7,11},{8,4},{9,5},... | collective-permute-start | bytes 638984 | tf_op jit(solution)/shard_map/ppermute | solution.py:628
  65.3 2.9 %query_backward.1.dq_r = f32[256,768]{1,0:T(8,128)S(1)} custom-call(s32[16]{0:T(128)S(1)} %concatenate.22.meta, bf16[256,768]{1,0:T(8,128)(2,1)S(1)} %copy-done.7, bf16[256,768]{1,0:T(8,128)(2,1)S(1)} %copy-done.9, f32[256,128]{1,0:T(8,128)S(1)} %get-tuple-element.112.stat, bf16[192,1536]{1,0:T(8,128)(2,1)} %constant_dynamic-update-slice_fusion.kv_a1, ...), custom_call_target="tpu_custom_call" | custom-call | tf_op jit(solution)/shard_map/query_backward/pallas_call | solution.py:615
  68.2 2.5 %collective-permute-done.9.qd_a2 = bf16[64,1664]{1,0:T(8,128)(2,1)S(1)} collective-permute-done((bf16[64,1664]{1,0:T(8,128)(2,1)S(1)}, bf16[64,1664]{1,0:T(8,128)(2,1)S(1)}, u32[]{:S(2)}, u32[]{:S(2)}) %collective-permute-start.9) | collective-permute-done | bytes 213024 | tf_op jit(solution)/shard_map/ppermute | solution.py:628
  72.6 2.9 %key_backward.1 = (bf16[256,2304]{1,0:T(8,128)(2,1)S(1)}, bf16[256,1536]{1,0:T(8,128)(2,1)S(1)}, bf16[256,1536]{1,0:T(8,128)(2,1)S(1)}) custom-call(s32[16]{0:T(128)S(1)} %concatenate.22.meta, bf16[256,1536]{1,0:T(8,128)(2,1)S(1)} %copy-done.4, bf16[192,1664]{1,0:T(8,128)(2,1)S(1)} %pad_maximum_fusion.qd_a1, ...), custom_call_target="tpu_custom_call" | custom-call | tf_op jit(solution)/shard_map/key_backward/pallas_call | solution.py:615
  77.9 3.1 %weight_grad.1 = (f32[768,384]{1,0:T(8,128)S(1)}, bf16[768,384]{1,0:T(8,128)(2,1)S(1)}, bf16[768,384]{1,0:T(8,128)(2,1)S(1)}, bf16[768,384]{1,0:T(8,128)(2,1)S(1)}) custom-call(s32[16]{0:T(128)S(1)} %concatenate.22.meta, bf16[256,1536]{1,0:T(8,128)(2,1)S(1)} %get-tuple-element.135.own, bf16[256,1536]{1,0:T(8,128)(2,1)S(1)} %collective-permute-done.12.other, ...), custom_call_target="tpu_custom_call" | custom-call | tf_op jit(solution)/shard_map/weight_grad/pallas_call | solution.py:615
  82.4 2.6 %collective-permute-start.14 = (bf16[768,384]{1,0:T(8,128)(2,1)S(1)}, bf16[768,384]{1,0:T(8,128)(2,1)S(1)}, u32[]{:S(2)}, u32[]{:S(2)}) collective-permute-start(bf16[768,384]{1,0:T(8,128)(2,1)S(1)} %get-tuple-element.145), channel_id=1, source_target_pairs={{0,64},{1,3},{2,66},{3,1},{4,68},{5,7},{6,70},{7,5},{8,72},{9,11},... | collective-permute-start | bytes 1769480 | tf_op jit(solution)/shard_map/ppermute | solution.py:659
  86.1 2.5 %token_grad.1 = (bf16[256,768]{1,0:T(8,128)(2,1)}, bf16[16,384]{1,0:T(8,128)(2,1)S(1)}) custom-call(bf16[256,2304]{1,0:T(8,128)(2,1)S(1)} %get-tuple-element.142.d_qkv, bf16[768,2304]{1,0:T(8,128)(2,1)S(1)} %copy-done.1, f32[256,768]{1,0:T(8,128)S(1)} %copy-done.13, f32[768]{0:T(1024)S(1)} %copy-done.26, bf16[256,768]{1,0:T(8,128)(2,1)S(1)} %copy-done.15), custom_call_target="tpu_custom_call" | custom-call | tf_op jit(solution)/shard_map/token_grad/pallas_call | solution.py:615
  91.4 7.5 %collective-permute-done.14.r2 = bf16[768,384]{1,0:T(8,128)(2,1)S(1)} collective-permute-done((bf16[768,384]{1,0:T(8,128)(2,1)S(1)}, bf16[768,384]{1,0:T(8,128)(2,1)S(1)}, u32[]{:S(2)}, u32[]{:S(2)}) %collective-permute-start.14) | collective-permute-done | bytes 589856 | tf_op jit(solution)/shard_map/ppermute | solution.py:659
  99.8 3.8 %collective-permute-start.17 = (bf16[208,384]{1,0:T(8,128)(2,1)S(1)}, bf16[208,384]{1,0:T(8,128)(2,1)S(1)}, u32[]{:S(2)}, u32[]{:S(2)}) collective-permute-start(bf16[208,384]{1,0:T(8,128)(2,1)S(1)} %get-tuple-element.153), channel_id=1, source_target_pairs={{0,2},{1,9},{2,0},{3,11},{4,6},{5,13},{6,4},{7,15},{8,10},{9,1},{1... | collective-permute-start | bytes 479240 | tf_op jit(solution)/shard_map/ppermute | solution.py:659
  105.4 2.9 %collective-permute-done.17.r2 = bf16[208,384]{1,0:T(8,128)(2,1)S(1)} collective-permute-done((bf16[208,384]{1,0:T(8,128)(2,1)S(1)}, bf16[208,384]{1,0:T(8,128)(2,1)S(1)}, u32[]{:S(2)}, u32[]{:S(2)}) %collective-permute-start.17) | collective-permute-done | bytes 159776 | tf_op jit(solution)/shard_map/ppermute | solution.py:659
  109.0 2.2 %collective-permute-start.21 = (bf16[208,384]{1,0:T(8,128)(2,1)S(1)}, bf16[208,384]{1,0:T(8,128)(2,1)S(1)}, u32[]{:S(2)}, u32[]{:S(2)}) collective-permute-start(bf16[208,384]{1,0:T(8,128)(2,1)S(1)} %add_b.1.own), channel_id=1, source_target_pairs={{0,12},{1,97},{2,14},{3,99},{4,0},{5,101},{6,2},{7,103},{8,4},{9,1... | collective-permute-start | bytes 479240 | tf_op jit(solution)/shard_map/ppermute | solution.py:659
  112.3 2.8 %collective-permute-done.21.r3 = bf16[208,384]{1,0:T(8,128)(2,1)S(1)} collective-permute-done((bf16[208,384]{1,0:T(8,128)(2,1)S(1)}, bf16[208,384]{1,0:T(8,128)(2,1)S(1)}, u32[]{:S(2)}, u32[]{:S(2)}) %collective-permute-start.21) | collective-permute-done | bytes 159776 | tf_op jit(solution)/shard_map/ppermute | solution.py:659
  121.9 3.0 %collective-permute-done.24.r3 = bf16[192,384]{1,0:T(8,128)(2,1)S(1)} collective-permute-done((bf16[192,384]{1,0:T(8,128)(2,1)S(1)}, bf16[192,384]{1,0:T(8,128)(2,1)S(1)}, u32[]{:S(2)}, u32[]{:S(2)}) %collective-permute-start.24) | collective-permute-done | bytes 147488 | tf_op jit(solution)/shard_map/ppermute | solution.py:659
  124.9 1.9 %collective-permute-done.23.r2 = bf16[192,384]{1,0:T(8,128)(2,1)S(1)} collective-permute-done((bf16[192,384]{1,0:T(8,128)(2,1)S(1)}, bf16[192,384]{1,0:T(8,128)(2,1)S(1)}, u32[]{:S(2)}, u32[]{:S(2)}) %collective-permute-start.23) | collective-permute-done | bytes 147488 | tf_op jit(solution)/shard_map/ppermute | solution.py:659
  128.9 5.5 %collective-permute-start.28 = (bf16[784,384]{1,0:T(8,128)(2,1)S(1)}, bf16[784,384]{1,0:T(8,128)(2,1)S(1)}, u32[]{:S(2)}, u32[]{:S(2)}) collective-permute-start(bf16[784,384]{1,0:T(8,128)(2,1)S(1)} %merge_b.1.refs_0_.refs_2_), channel_id=1, source_target_pairs={{0,1},{1,0},{2,3},{3,2},{4,5},{5,4},{6,7},{7,6},{8,9},{9,8},{10,11... | collective-permute-start | bytes 1806344 | tf_op jit(solution)/shard_map/ppermute | solution.py:628
  136.0 2.0 %finish.3 = (f32[768,2304]{1,0:T(8,128)}, f32[768,768]{1,0:T(8,128)}) custom-call(s32[16]{0:T(128)S(1)} %concatenate.22.meta, bf16[784,384]{1,0:T(8,128)(2,1)S(1)} %merge_b.1.refs_0_.refs_2_, bf16[784,384]{1,0:T(8,128)(2,1)S(1)} %collective-permute-done.28.refs_1_.refs_6_), custom_call_target="tpu_custom_call" | custom-call | tf_op jit(solution)/shard_map/finish/pallas_call | solution.py:597
  138.1 5.5 %collective-permute-done.27.refs_1_.refs_5_ = bf16[784,384]{1,0:T(8,128)(2,1)S(1)} collective-permute-done((bf16[784,384]{1,0:T(8,128)(2,1)S(1)}, bf16[784,384]{1,0:T(8,128)(2,1)S(1)}, u32[]{:S(2)}, u32[]{:S(2)}) %collective-permute-start.27) | collective-permute-done | bytes 602144 | tf_op jit(solution)/shard_map/ppermute | solution.py:700
  145.1 3.2 %collective-permute-start.29 = (bf16[784,384]{1,0:T(8,128)(2,1)S(1)}, bf16[784,384]{1,0:T(8,128)(2,1)S(1)}, u32[]{:S(2)}, u32[]{:S(2)}) collective-permute-start(bf16[784,384]{1,0:T(8,128)(2,1)S(1)} %collective-permute-done.26.refs_0_.refs_3_), channel_id=1, source_target_pairs={{0,1},{1,0},{2,3},{3,2},{4,5},{5,4},{6,7},{7,6},{8,9},{9,8},{10,11... | collective-permute-start | bytes 1806344 | tf_op jit(solution)/shard_map/ppermute | solution.py:628
  150.7 2.8 %finish.4 = (f32[768,2304]{1,0:T(8,128)}, f32[768,768]{1,0:T(8,128)}) custom-call(s32[16]{0:T(128)S(1)} %concatenate.22.meta, bf16[784,384]{1,0:T(8,128)(2,1)S(1)} %collective-permute-done.26.refs_0_.refs_3_, bf16[784,384]{1,0:T(8,128)(2,1)S(1)} %collective-permute-done.27.refs_1_.refs_5_, ...), custom_call_target="tpu_custom_call", output_to_operand_aliasing={{0}: (5, {}), {1}: (6, {})} | custom-call | tf_op jit(solution)/shard_map/finish/pallas_call | solution.py:597
  153.6 5.3 %collective-permute-done.25.refs_0_.refs_4_ = bf16[784,384]{1,0:T(8,128)(2,1)S(1)} collective-permute-done((bf16[784,384]{1,0:T(8,128)(2,1)S(1)}, bf16[784,384]{1,0:T(8,128)(2,1)S(1)}, u32[]{:S(2)}, u32[]{:S(2)}) %collective-permute-start.25) | collective-permute-done | bytes 602144 | tf_op jit(solution)/shard_map/ppermute | solution.py:700
  161.9 2.6 %finish.5 = (f32[768,2304]{1,0:T(8,128)}, f32[768,768]{1,0:T(8,128)}, f32[768]{0:T(1024)}, f32[768]{0:T(1024)}) custom-call(s32[16]{0:T(128)S(1)} %concatenate.22.meta, bf16[784,384]{1,0:T(8,128)(2,1)S(1)} %collective-permute-done.25.refs_0_.refs_4_, ...), custom_call_target="tpu_custom_call", output_to_operand_aliasing={{0}: (11, {}), {1}: (12, {})} | custom-call | tf_op jit(solution)/shard_map/finish/pallas_call | solution.py:597
  (135 shorter events, 60.7 us)
Async XLA Ops:
  10.5 9.1 %collective-permute-start = (bf16[80,1536]{1,0:T(8,128)(2,1)S(1)}, bf16[80,1536]{1,0:T(8,128)(2,1)S(1)}, u32[]{:S(2)}, u32[]{:S(2)}) collective-permute-start(bf16[80,1536]{1,0:T(8,128)(2,1)S(1)} %get-tuple-element.89), channel_id=1, source_target_pairs={{0,2},{1,3},{2,0},{3,1},{4,6},{5,7},{6,4},{7,5},{8,10},{9,11},{10,... | collective-permute-start | bytes 737288 | tf_op jit(solution)/shard_map/ppermute | solution.py:628
  14.2 5.4 %collective-permute-start.1 = (bf16[256,768]{1,0:T(8,128)(2,1)S(1)}, bf16[256,768]{1,0:T(8,128)(2,1)S(1)}, u32[]{:S(2)}, u32[]{:S(2)}) collective-permute-start(bf16[256,768]{1,0:T(8,128)(2,1)S(1)} %get-tuple-element.90.normed.norm_a), channel_id=1, source_target_pairs={{0,1},{1,0},{2,3},{3,2},{4,5},{5,4},{6,7},{7,6},{8,9},{9,8},{10,11... | collective-permute-start | bytes 1179656 | tf_op jit(solution)/shard_map/ppermute | solution.py:628
  23.0 5.7 %collective-permute-start.2 = (bf16[32,1536]{1,0:T(8,128)(2,1)}, bf16[32,1536]{1,0:T(8,128)(2,1)}, u32[]{:S(2)}, u32[]{:S(2)}) collective-permute-start(bf16[32,1536]{1,0:T(8,128)(2,1)} %pad_maximum_fusion.4), channel_id=1, source_target_pairs={{0,4},{1,5},{2,6},{3,7},{4,0},{5,1},{6,2},{7,3},{8,12},{9,13},{10,... | collective-permute-start | bytes 294920 | tf_op jit(solution)/shard_map/ppermute | solution.py:628
  30.3 10.6 %collective-permute-start.4 = (bf16[192,1536]{1,0:T(8,128)(2,1)}, bf16[192,1536]{1,0:T(8,128)(2,1)S(1)}, u32[]{:S(2)}, u32[]{:S(2)}) collective-permute-start(bf16[192,1536]{1,0:T(8,128)(2,1)} %constant_dynamic-update-slice_fusion.kv_a1), channel_id=1, source_target_pairs={{0,1},{1,0},{2,3},{3,2},{4,5},{5,4},{6,7},{7,6},{8,9},{9,8},{10,11... | collective-permute-start | bytes 1769480 | tf_op jit(solution)/shard_map/ppermute | solution.py:628
  33.0 7.9 %collective-permute-start.3 = (bf16[64,1536]{1,0:T(8,128)(2,1)S(1)}, bf16[64,1536]{1,0:T(8,128)(2,1)S(1)}, u32[]{:S(2)}, u32[]{:S(2)}) collective-permute-start(bf16[64,1536]{1,0:T(8,128)(2,1)S(1)} %pad_maximum_fusion.2), channel_id=1, source_target_pairs={{0,12},{1,13},{2,14},{3,15},{4,8},{5,9},{6,10},{7,11},{8,4},{9,5},... | collective-permute-start | bytes 589832 | tf_op jit(solution)/shard_map/ppermute | solution.py:628
  40.9 1.8 %collective-permute-start.5 = (bf16[64,1536]{1,0:T(8,128)(2,1)S(1)}, bf16[64,1536]{1,0:T(8,128)(2,1)S(1)}, u32[]{:S(2)}, u32[]{:S(2)}) collective-permute-start(bf16[64,1536]{1,0:T(8,128)(2,1)S(1)} %collective-permute-done.3.kv_a2), channel_id=1, source_target_pairs={{0,1},{1,0},{2,3},{3,2},{4,5},{5,4},{6,7},{7,6},{8,9},{9,8},{10,11... | collective-permute-start | bytes 589832 | tf_op jit(solution)/shard_map/ppermute | solution.py:628
  46.8 9.7 %collective-permute-start.7 = (bf16[256,768]{1,0:T(8,128)(2,1)S(1)}, bf16[256,768]{1,0:T(8,128)(2,1)S(1)}, u32[]{:S(2)}, u32[]{:S(2)}) collective-permute-start(bf16[256,768]{1,0:T(8,128)(2,1)S(1)} %get-tuple-element.140.att_a.att), channel_id=1, source_target_pairs={{0,1},{1,0},{2,3},{3,2},{4,5},{5,4},{6,7},{7,6},{8,9},{9,8},{10,11... | collective-permute-start | bytes 1179656 | tf_op jit(solution)/shard_map/ppermute | solution.py:628
  47.3 9.2 %collective-permute-start.6 = (bf16[80,1664]{1,0:T(8,128)(2,1)S(1)}, bf16[80,1664]{1,0:T(8,128)(2,1)S(1)}, u32[]{:S(2)}, u32[]{:S(2)}) collective-permute-start(bf16[80,1664]{1,0:T(8,128)(2,1)S(1)} %get-tuple-element.111), channel_id=1, source_target_pairs={{0,2},{1,3},{2,0},{3,1},{4,6},{5,7},{6,4},{7,5},{8,10},{9,11},{10,... | collective-permute-start | bytes 798728 | tf_op jit(solution)/shard_map/ppermute | solution.py:628
  56.5 3.9 %collective-permute-start.8 = (bf16[32,1664]{1,0:T(8,128)(2,1)S(1)}, bf16[32,1664]{1,0:T(8,128)(2,1)S(1)}, u32[]{:S(2)}, u32[]{:S(2)}) collective-permute-start(bf16[32,1664]{1,0:T(8,128)(2,1)S(1)} %pad_maximum_fusion.3), channel_id=1, source_target_pairs={{0,4},{1,5},{2,6},{3,7},{4,0},{5,1},{6,2},{7,3},{8,12},{9,13},{10,... | collective-permute-start | bytes 319496 | tf_op jit(solution)/shard_map/ppermute | solution.py:628
  60.4 10.3 %collective-permute-start.10 = (bf16[192,1664]{1,0:T(8,128)(2,1)S(1)}, bf16[192,1664]{1,0:T(8,128)(2,1)S(1)}, u32[]{:S(2)}, u32[]{:S(2)}) collective-permute-start(bf16[192,1664]{1,0:T(8,128)(2,1)S(1)} %pad_maximum_fusion.qd_a1), channel_id=1, source_target_pairs={{0,1},{1,0},{2,3},{3,2},{4,5},{5,4},{6,7},{7,6},{8,9},{9,8},{10,11... | collective-permute-start | bytes 1916936 | tf_op jit(solution)/shard_map/ppermute | solution.py:628
  62.6 8.2 %collective-permute-start.9 = (bf16[64,1664]{1,0:T(8,128)(2,1)S(1)}, bf16[64,1664]{1,0:T(8,128)(2,1)S(1)}, u32[]{:S(2)}, u32[]{:S(2)}) collective-permute-start(bf16[64,1664]{1,0:T(8,128)(2,1)S(1)} %pad_maximum_fusion.1), channel_id=1, source_target_pairs={{0,12},{1,13},{2,14},{3,15},{4,8},{5,9},{6,10},{7,11},{8,4},{9,5},... | collective-permute-start | bytes 638984 | tf_op jit(solution)/shard_map/ppermute | solution.py:628
  70.7 1.9 %collective-permute-start.11 = (bf16[64,1664]{1,0:T(8,128)(2,1)S(1)}, bf16[64,1664]{1,0:T(8,128)(2,1)S(1)}, u32[]{:S(2)}, u32[]{:S(2)}) collective-permute-start(bf16[64,1664]{1,0:T(8,128)(2,1)S(1)} %collective-permute-done.9.qd_a2), channel_id=1, source_target_pairs={{0,1},{1,0},{2,3},{3,2},{4,5},{5,4},{6,7},{7,6},{8,9},{9,8},{10,11... | collective-permute-start | bytes 638984 | tf_op jit(solution)/shard_map/ppermute | solution.py:628
  75.5 2.4 %collective-permute-start.12 = (bf16[256,1536]{1,0:T(8,128)(2,1)S(1)}, bf16[256,1536]{1,0:T(8,128)(2,1)S(1)}, u32[]{:S(2)}, u32[]{:S(2)}) collective-permute-start(bf16[256,1536]{1,0:T(8,128)(2,1)S(1)} %get-tuple-element.136), channel_id=1, source_target_pairs={{0,1},{1,0},{2,3},{3,2},{4,5},{5,4},{6,7},{7,6},{8,9},{9,8},{10,11... | collective-permute-start | bytes 2359304 | tf_op jit(solution)/shard_map/ppermute | solution.py:628
  81.0 10.4 %collective-permute-start.13 = (bf16[768,384]{1,0:T(8,128)(2,1)S(1)}, bf16[768,384]{1,0:T(8,128)(2,1)S(1)}, u32[]{:S(2)}, u32[]{:S(2)}) collective-permute-start(bf16[768,384]{1,0:T(8,128)(2,1)S(1)} %get-tuple-element.144), channel_id=1, source_target_pairs={{0,32},{1,17},{2,34},{3,19},{4,36},{5,21},{6,38},{7,23},{8,40},{9,... | collective-permute-start | bytes 1769480 | tf_op jit(solution)/shard_map/ppermute | solution.py:659
  82.4 16.5 %collective-permute-start.14 = (bf16[768,384]{1,0:T(8,128)(2,1)S(1)}, bf16[768,384]{1,0:T(8,128)(2,1)S(1)}, u32[]{:S(2)}, u32[]{:S(2)}) collective-permute-start(bf16[768,384]{1,0:T(8,128)(2,1)S(1)} %get-tuple-element.145), channel_id=1, source_target_pairs={{0,64},{1,3},{2,66},{3,1},{4,68},{5,7},{6,70},{7,5},{8,72},{9,11},... | collective-permute-start | bytes 1769480 | tf_op jit(solution)/shard_map/ppermute | solution.py:659
  85.0 13.9 %collective-permute-start.15 = (bf16[768,384]{1,0:T(8,128)(2,1)S(1)}, bf16[768,384]{1,0:T(8,128)(2,1)S(1)}, u32[]{:S(2)}, u32[]{:S(2)}) collective-permute-start(bf16[768,384]{1,0:T(8,128)(2,1)S(1)} %get-tuple-element.146), channel_id=1, source_target_pairs={{0,96},{1,19},{2,98},{3,17},{4,100},{5,23},{6,102},{7,21},{8,104},... | collective-permute-start | bytes 1769480 | tf_op jit(solution)/shard_map/ppermute | solution.py:659
  99.7 5.7 %collective-permute-start.16 = (bf16[208,384]{1,0:T(8,128)(2,1)S(1)}, bf16[208,384]{1,0:T(8,128)(2,1)S(1)}, u32[]{:S(2)}, u32[]{:S(2)}) collective-permute-start(bf16[208,384]{1,0:T(8,128)(2,1)S(1)} %get-tuple-element.152), channel_id=1, source_target_pairs={{0,16},{1,5},{2,18},{3,7},{4,20},{5,9},{6,22},{7,11},{8,24},{9,13}... | collective-permute-start | bytes 479240 | tf_op jit(solution)/shard_map/ppermute | solution.py:659
  99.8 8.5 %collective-permute-start.17 = (bf16[208,384]{1,0:T(8,128)(2,1)S(1)}, bf16[208,384]{1,0:T(8,128)(2,1)S(1)}, u32[]{:S(2)}, u32[]{:S(2)}) collective-permute-start(bf16[208,384]{1,0:T(8,128)(2,1)S(1)} %get-tuple-element.153), channel_id=1, source_target_pairs={{0,2},{1,9},{2,0},{3,11},{4,6},{5,13},{6,4},{7,15},{8,10},{9,1},{1... | collective-permute-start | bytes 479240 | tf_op jit(solution)/shard_map/ppermute | solution.py:659
  103.6 4.7 %collective-permute-start.18 = (bf16[208,384]{1,0:T(8,128)(2,1)S(1)}, bf16[208,384]{1,0:T(8,128)(2,1)S(1)}, u32[]{:S(2)}, u32[]{:S(2)}) collective-permute-start(bf16[208,384]{1,0:T(8,128)(2,1)S(1)} %get-tuple-element.154), channel_id=1, source_target_pairs={{0,18},{1,13},{2,16},{3,15},{4,22},{5,1},{6,20},{7,3},{8,26},{9,5}... | collective-permute-start | bytes 479240 | tf_op jit(solution)/shard_map/ppermute | solution.py:659
  109.0 6.2 %collective-permute-start.21 = (bf16[208,384]{1,0:T(8,128)(2,1)S(1)}, bf16[208,384]{1,0:T(8,128)(2,1)S(1)}, u32[]{:S(2)}, u32[]{:S(2)}) collective-permute-start(bf16[208,384]{1,0:T(8,128)(2,1)S(1)} %add_b.1.own), channel_id=1, source_target_pairs={{0,12},{1,97},{2,14},{3,99},{4,0},{5,101},{6,2},{7,103},{8,4},{9,1... | collective-permute-start | bytes 479240 | tf_op jit(solution)/shard_map/ppermute | solution.py:659
  111.2 5.7 %collective-permute-start.20 = (bf16[208,384]{1,0:T(8,128)(2,1)S(1)}, bf16[208,384]{1,0:T(8,128)(2,1)S(1)}, u32[]{:S(2)}, u32[]{:S(2)}) collective-permute-start(bf16[208,384]{1,0:T(8,128)(2,1)S(1)} %add_b.1.own), channel_id=1, source_target_pairs={{0,8},{1,65},{2,10},{3,67},{4,12},{5,69},{6,14},{7,71},{8,0},{9,73... | collective-permute-start | bytes 479240 | tf_op jit(solution)/shard_map/ppermute | solution.py:659
  111.6 7.3 %collective-permute-start.19 = (bf16[208,384]{1,0:T(8,128)(2,1)S(1)}, bf16[208,384]{1,0:T(8,128)(2,1)S(1)}, u32[]{:S(2)}, u32[]{:S(2)}) collective-permute-start(bf16[208,384]{1,0:T(8,128)(2,1)S(1)} %add_b.1.own), channel_id=1, source_target_pairs={{0,4},{1,33},{2,6},{3,35},{4,8},{5,37},{6,10},{7,39},{8,12},{9,41}... | collective-permute-start | bytes 479240 | tf_op jit(solution)/shard_map/ppermute | solution.py:659
  119.6 5.3 %collective-permute-start.24 = (bf16[192,384]{1,0:T(8,128)(2,1)S(1)}, bf16[192,384]{1,0:T(8,128)(2,1)S(1)}, u32[]{:S(2)}, u32[]{:S(2)}) collective-permute-start(bf16[192,384]{1,0:T(8,128)(2,1)S(1)} %get-tuple-element.155.own), channel_id=1, source_target_pairs={{0,18},{1,13},{2,16},{3,15},{4,22},{5,1},{6,20},{7,3},{8,26},{9,5}... | collective-permute-start | bytes 442376 | tf_op jit(solution)/shard_map/ppermute | solution.py:659
  121.2 5.6 %collective-permute-start.23 = (bf16[192,384]{1,0:T(8,128)(2,1)S(1)}, bf16[192,384]{1,0:T(8,128)(2,1)S(1)}, u32[]{:S(2)}, u32[]{:S(2)}) collective-permute-start(bf16[192,384]{1,0:T(8,128)(2,1)S(1)} %get-tuple-element.155.own), channel_id=1, source_target_pairs={{0,2},{1,9},{2,0},{3,11},{4,6},{5,13},{6,4},{7,15},{8,10},{9,1},{1... | collective-permute-start | bytes 442376 | tf_op jit(solution)/shard_map/ppermute | solution.py:659
  121.7 6.6 %collective-permute-start.22 = (bf16[192,384]{1,0:T(8,128)(2,1)S(1)}, bf16[192,384]{1,0:T(8,128)(2,1)S(1)}, u32[]{:S(2)}, u32[]{:S(2)}) collective-permute-start(bf16[192,384]{1,0:T(8,128)(2,1)S(1)} %get-tuple-element.155.own), channel_id=1, source_target_pairs={{0,16},{1,5},{2,18},{3,7},{4,20},{5,9},{6,22},{7,11},{8,24},{9,13}... | collective-permute-start | bytes 442376 | tf_op jit(solution)/shard_map/ppermute | solution.py:659
  128.9 7.1 %collective-permute-start.28 = (bf16[784,384]{1,0:T(8,128)(2,1)S(1)}, bf16[784,384]{1,0:T(8,128)(2,1)S(1)}, u32[]{:S(2)}, u32[]{:S(2)}) collective-permute-start(bf16[784,384]{1,0:T(8,128)(2,1)S(1)} %merge_b.1.refs_0_.refs_2_), channel_id=1, source_target_pairs={{0,1},{1,0},{2,3},{3,2},{4,5},{5,4},{6,7},{7,6},{8,9},{9,8},{10,11... | collective-permute-start | bytes 1806344 | tf_op jit(solution)/shard_map/ppermute | solution.py:628
  134.4 9.2 %collective-permute-start.27 = (bf16[784,384]{1,0:T(8,128)(2,1)S(1)}, bf16[784,384]{1,0:T(8,128)(2,1)S(1)}, u32[]{:S(2)}, u32[]{:S(2)}) collective-permute-start(bf16[784,384]{1,0:T(8,128)(2,1)S(1)} %merge_b.1.refs_0_.refs_2_), channel_id=1, source_target_pairs={{0,96},{1,19},{2,98},{3,17},{4,100},{5,23},{6,102},{7,21},{8,104},... | collective-permute-start | bytes 1806344 | tf_op jit(solution)/shard_map/ppermute | solution.py:700
  134.7 10.4 %collective-permute-start.26 = (bf16[784,384]{1,0:T(8,128)(2,1)S(1)}, bf16[784,384]{1,0:T(8,128)(2,1)S(1)}, u32[]{:S(2)}, u32[]{:S(2)}) collective-permute-start(bf16[784,384]{1,0:T(8,128)(2,1)S(1)} %merge_b.1.refs_0_.refs_2_), channel_id=1, source_target_pairs={{0,32},{1,17},{2,34},{3,19},{4,36},{5,21},{6,38},{7,23},{8,40},{9,... | collective-permute-start | bytes 1806344 | tf_op jit(solution)/shard_map/ppermute | solution.py:700
  145.1 4.8 %collective-permute-start.29 = (bf16[784,384]{1,0:T(8,128)(2,1)S(1)}, bf16[784,384]{1,0:T(8,128)(2,1)S(1)}, u32[]{:S(2)}, u32[]{:S(2)}) collective-permute-start(bf16[784,384]{1,0:T(8,128)(2,1)S(1)} %collective-permute-done.26.refs_0_.refs_3_), channel_id=1, source_target_pairs={{0,1},{1,0},{2,3},{3,2},{4,5},{5,4},{6,7},{7,6},{8,9},{9,8},{10,11... | collective-permute-start | bytes 1806344 | tf_op jit(solution)/shard_map/ppermute | solution.py:628
  148.2 2.5 %collective-permute-start.30 = (bf16[784,384]{1,0:T(8,128)(2,1)S(1)}, bf16[784,384]{1,0:T(8,128)(2,1)S(1)}, u32[]{:S(2)}, u32[]{:S(2)}) collective-permute-start(bf16[784,384]{1,0:T(8,128)(2,1)S(1)} %collective-permute-done.27.refs_1_.refs_5_), channel_id=1, source_target_pairs={{0,1},{1,0},{2,3},{3,2},{4,5},{5,4},{6,7},{7,6},{8,9},{9,8},{10,11... | collective-permute-start | bytes 1806344 | tf_op jit(solution)/shard_map/ppermute | solution.py:628
  148.2 10.7 %collective-permute-start.25 = (bf16[784,384]{1,0:T(8,128)(2,1)S(1)}, bf16[784,384]{1,0:T(8,128)(2,1)S(1)}, u32[]{:S(2)}, u32[]{:S(2)}) collective-permute-start(bf16[784,384]{1,0:T(8,128)(2,1)S(1)} %merge_b.1.refs_0_.refs_2_), channel_id=1, source_target_pairs={{0,64},{1,3},{2,66},{3,1},{4,68},{5,7},{6,70},{7,5},{8,72},{9,11},... | collective-permute-start | bytes 1806344 | tf_op jit(solution)/shard_map/ppermute | solution.py:700
  158.9 3.0 %collective-permute-start.31 = (bf16[784,384]{1,0:T(8,128)(2,1)S(1)}, bf16[784,384]{1,0:T(8,128)(2,1)S(1)}, u32[]{:S(2)}, u32[]{:S(2)}) collective-permute-start(bf16[784,384]{1,0:T(8,128)(2,1)S(1)} %collective-permute-done.25.refs_0_.refs_4_), channel_id=1, source_target_pairs={{0,1},{1,0},{2,3},{3,2},{4,5},{5,4},{6,7},{7,6},{8,9},{9,8},{10,11... | collective-permute-start | bytes 1806344 | tf_op jit(solution)/shard_map/ppermute | solution.py:628
  (34 other events, 159.8 us)

commit v3 on v2

--- a/solution.py
+++ b/solution.py
@@ -119,9 +119,9 @@
 def far_bias(meta):
     t = iota((T, T), 1)
     s = t >> 4
-    code = ((s & 1) << 1) ^ (((s >> 1) & 1) << 2) ^ (((s >> 2) & 1) * 12) ^ (s >> 3)
+    place = (((meta[0] >> 2) - (s >> 1)) & 3) * 4 + ((meta[0] & 3) ^ ((s & 1) << 1) ^ (s >> 3))
     row = iota((T, T), 0)
-    pos = (meta[0] ^ code) * T + (t & 15) * 16 + (row >> 6) + 4 * ((row >> 4) & 3)
+    pos = place * T + (t & 15) * 16 + (row >> 6) + 4 * ((row >> 4) & 3)
     return bias_of(meta, pos)
 
 
@@ -163,14 +163,27 @@
     return [span_mask(HD * h, (1, D)).astype(BF) for h in range(HEADS)]
 
 
-def key_kernel(tok, coords, table, gain, bias, w_k, w_v, inp_o, norm_o, kv_o, pack_o):
+def key_kernel(tok_h, coords, table_h, gain, bias, w_h, inp_o, norm_o, kv_o, pack_o,
+               tok, table, weight, sems):
+    copies = [
+        pltpu.make_async_copy(tok_h, tok, sems.at[0]),
+        pltpu.make_async_copy(table_h, table, sems.at[1]),
+        pltpu.make_async_copy(w_h.at[:, pl.ds(D, D)], weight.at[0], sems.at[2]),
+        pltpu.make_async_copy(w_h.at[:, pl.ds(2 * D, D)], weight.at[1], sems.at[3]),
+    ]
+    for copy in copies:
+        copy.start()
     sort = sort_matrix()
-    tok_s = nn(sort, tok[...])
     grid = iota((T, T), 0)
-    parts = []
+    hots = []
     for axis in range(2):
         hot = jnp.where(grid == coords[axis : axis + 1, :], 1.0, 0.0).astype(BF)
-        hot = nt(sort, hot).astype(BF)
+        hots.append(nt(sort, hot).astype(BF))
+    copies[0].wait()
+    tok_s = nn(sort, tok[...])
+    copies[1].wait()
+    parts = []
+    for hot in hots:
         found = nn(hot, table[...])
         parts.append(found[:, :384] + found[:, 384:768] + found[:, 768:])
     inputs = tok_s + jnp.concatenate(parts, axis=1)
@@ -179,8 +192,9 @@
     normed = (unit * gain[...].reshape(1, D) + bias[...].reshape(1, D)).astype(BF)
     norm_o[...] = normed
     masks = pack_masks()
-    for n, weight in enumerate((w_k, w_v)):
-        part = nn(normed, weight[...]).astype(BF)
+    for n in range(2):
+        copies[2 + n].wait()
+        part = nn(normed, weight[n]).astype(BF)
         kv_o[:, D * n : D * (n + 1)] = part
         pack_o[:, D * n : D * (n + 1)] = pack_rows(part, masks)
 
@@ -223,12 +237,16 @@
 
 
 def mid_rows(got, lo, width):
-    return jnp.concatenate([got[0][:128, lo : lo + width], got[2][:128, lo : lo + width]], axis=0)
+    return jnp.concatenate([got[0][:128, lo : lo + width], got[4][:128, lo : lo + width]], axis=0)
 
 
 def far_rows(got, lo, width):
     at = slice(lo, lo + width)
-    return jnp.concatenate([got[0][128:, at], got[1][:, at], got[2][128:, at], got[3][:, at]], axis=0)
+    rows = []
+    for n in (0, 4):
+        rows.append(got[n][128:, at])
+        rows += [got[n + d][:, at] for d in (1, 2, 3)]
+    return jnp.concatenate(rows, axis=0)
 
 
 def expand_matrix():
@@ -243,11 +261,11 @@
     return jnp.where((lane >= head * HD) & (lane < head * HD + HD), 1.0, 0.0).astype(BF)
 
 
-def remote_forward_kernel(meta, q_r, kv_a1, kv_a2, kv_b1, kv_b2, o_1, top_1, sum_1, o_2, top_2, sum_2, d_att,
-                          pack, att_o, stat_o, send_o):
+def remote_forward_kernel(meta, q_r, *refs):
+    got = refs[:8]
+    o_1, top_1, sum_1, o_2, top_2, sum_2, d_att, pack, att_o, stat_o, send_o = refs[8:]
     lane = iota((T, 128), 1)
     row = iota((T, 128), 0)
-    got = (kv_a1, kv_a2, kv_b1, kv_b2)
     top_l = jnp.where(lane < 8, top_1[...], top_2[...])
     sum_l = jnp.where(lane < 8, sum_1[...], sum_2[...])
     tops_m = jnp.full((T, 128), NEG, F32)
@@ -357,8 +375,8 @@
         dv_o[:, t : t + w] += tn(shares.astype(BF), da)
 
 
-def query_backward_kernel(meta, q_r, d_att, stat, kv_a1, kv_a2, kv_b1, kv_b2, dq_o):
-    got = (kv_a1, kv_a2, kv_b1, kv_b2)
+def query_backward_kernel(meta, q_r, d_att, stat, *refs):
+    got, dq_o = refs[:8], refs[8]
     dq_o[...] = jnp.zeros_like(dq_o)
     mid = mid_bias(meta)
     for g in range(4):
@@ -400,9 +418,10 @@
     return x[:32] + (x[32:64] + x[64:96])
 
 
-def key_backward_kernel(meta, kv, qd_a1, qd_a2, qd_b1, qd_b2, dq_r, dq_1, dk_1, dv_1, dq_2, dk_2, dv_2, cot,
-                        all_o, kept_o, sent_o, dk_s, dv_s):
-    got = (qd_a1, qd_a2, qd_b1, qd_b2)
+def key_backward_kernel(meta, kv, *refs):
+    got = refs[:8]
+    dq_r, dq_1, dk_1, dv_1, dq_2, dk_2, dv_2, cot = refs[8:16]
+    all_o, kept_o, sent_o, dk_s, dv_s = refs[16:]
     half = D // 2
     dk_s[:, :half] = dk_1[...]
     dk_s[:, half:] = dk_2[...]
@@ -516,25 +535,26 @@
     out[rows:] = two_parts(sums)
 
 
-def add_c_kernel(meta, own, r1, r2, r3, out, ext_o, pad, ext_pad):
+def add_c_kernel(own, r1, r2, r3, out):
     rows = D // 4
-    got = (r1, r2, r3)
-    total = ring_total(meta, 8, own[:rows].astype(F32), [r[:rows].astype(F32) for r in got], pad)
-    out[...] = total.astype(BF)
-    sums = ring_total(meta, 8, whole_of(own[rows:]), [whole_of(r[rows:]) for r in got], ext_pad)
-    ext_o[...] = two_parts(sums)
-
-
-def merge_kernel(meta, own, r1, r2, r3, ext, out):
+
+    def total(a, b, c, d):
+        return (a + c) + (b + d)
+
+    out[:rows] = total(*[r[:rows].astype(F32) for r in (own, r1, r2, r3)]).astype(BF)
+    out[rows:] = two_parts(total(*[whole_of(r[rows:]) for r in (own, r1, r2, r3)]))
+
+
+def merge_kernel(meta, own, r1, r2, r3, out):
     rows = D // 4
+    out[D:] = own[rows:]
     for d, piece in enumerate((own, r1, r2, r3)):
         at = pl.ds(pl.multiple_of(((meta[7] - d) & 3) * rows, 16), rows)
-        out[at, :] = piece[...]
-    out[D:] = ext[...]
-
-
-def finish_kernel(meta, *refs, turns, first, last):
-    count = 2 * len(turns)
+        out[at, :] = piece[:rows]
+
+
+def finish_kernel(meta, *refs, marks, first, last):
+    count = len(marks)
     pieces, refs = refs[:count], refs[count:]
     if last:
         tails, refs = refs[:8], refs[8:]
@@ -543,45 +563,54 @@
     qkv_o, out_o, *refs = refs
     if last:
         gain_o, bias_o, *refs = refs
-    wide, sems, *refs = refs
-    for n, piece in enumerate(pieces):
-        half = n // len(turns)
-        chunk = (meta[5] ^ half) * 4 + ((meta[6 if half == 0 else 9] - turns[n % len(turns)]) & 3)
-        wide[n] = piece[...].astype(F32)
+    sems, wide = refs[0], refs[1 : 1 + count]
+    for n, (piece, (core, turn, row)) in enumerate(zip(pieces, marks)):
+        chunk = (meta[5] ^ core) * 4 + ((meta[9 if core else 6] - turn) & 3)
+        size = wide[n].shape[0]
+        wide[n][...] = piece[:size].astype(F32)
 
         @pl.when(chunk < 6)
-        def _(n=n, chunk=chunk):
+        def _(n=n, chunk=chunk, row=row, size=size):
             at = pl.ds(pl.multiple_of(chunk * WIDE, 128), WIDE)
-            pltpu.make_async_copy(wide.at[n], qkv_o.at[:, at], sems.at[n]).start()
+            to = qkv_o.at[pl.ds(row, size), at]
+            pltpu.make_async_copy(wide[n], to, sems.at[n]).start()
 
         @pl.when(chunk >= 6)
-        def _(n=n, chunk=chunk):
+        def _(n=n, chunk=chunk, row=row, size=size):
             at = pl.ds(pl.multiple_of((chunk - 6) * WIDE, 128), WIDE)
-            pltpu.make_async_copy(wide.at[n], out_o.at[:, at], sems.at[n]).start()
+            to = out_o.at[pl.ds(row, size), at]
+            pltpu.make_async_copy(wide[n], to, sems.at[n]).start()
 
     if last:
-        pad = refs[0]
+        pad = refs[1 + count]
         for n, tail in enumerate(tails):
-            half = n // 4
-            place = (meta[6 if half == 0 else 9] - n % 4) & 3
-            pad[(meta[5] ^ half) * 4 + place] = whole_of(tail[...])
+            core = n // 4
+            place = (meta[9 if core else 6] - n % 4) & 3
+            pad[(meta[5] ^ core) * 4 + place] = whole_of(tail[...])
         total = pad[0]
         for n in range(1, 8):
             total = total + pad[n]
         gain_o[...] = jnp.concatenate([total[0:1], total[1:2]], axis=1).reshape(D)
         bias_o[...] = jnp.concatenate([total[2:3], total[3:4]], axis=1).reshape(D)
     for n in range(count):
-        pltpu.make_async_copy(wide.at[n], qkv_o.at[:, pl.ds(0, WIDE)], sems.at[n]).wait()
-
-
-def finish(meta, pieces, turns, tails, outs):
+        to = qkv_o.at[pl.ds(0, wide[n].shape[0]), pl.ds(0, WIDE)]
+        pltpu.make_async_copy(wide[n], to, sems.at[n]).wait()
+
+
+def finish(meta, pieces, outs, tails=None):
     first, last = outs is None, tails is not None
+    marks = tuple(piece[1:] for piece in pieces)
+    arrays = [piece[0] for piece in pieces]
     smem = pl.BlockSpec(memory_space=pltpu.SMEM)
     anywhere = pl.BlockSpec(memory_space=pl.ANY)
-    head = pl.BlockSpec((D, WIDE), lambda i: (0, 0))
-    tail = pl.BlockSpec((16, WIDE), lambda i: (D // 16, 0))
-    args = [meta, *pieces] + (list(tails) if last else [])
-    in_specs = [smem] + [head] * len(pieces) + ([tail] * 8 if last else [])
+    whole = pl.BlockSpec(memory_space=pltpu.VMEM)
+    args = [meta, *arrays]
+    in_specs = [smem] + [whole] * len(arrays)
+    if last:
+        args += tails
+        for tail in tails:
+            index = (tail.shape[0] // 16 - 1, 0)
+            in_specs.append(pl.BlockSpec((16, WIDE), lambda i, index=index: index))
     aliases = {}
     if not first:
         aliases = {len(args): 0, len(args) + 1: 1}
@@ -589,13 +618,15 @@
         in_specs += [anywhere] * 2
     out_shape = [jax.ShapeDtypeStruct((D, 3 * D), F32), jax.ShapeDtypeStruct((D, D), F32)]
     out_specs = [anywhere] * 2
-    scratch = [pltpu.VMEM((len(pieces), D, WIDE), F32), pltpu.SemaphoreType.DMA((len(pieces),))]
+    scratch = [pltpu.SemaphoreType.DMA((len(pieces),))]
+    for array in arrays:
+        scratch.append(pltpu.VMEM((array.shape[0] // WIDE * WIDE, WIDE), F32))
     if last:
         out_shape += [jax.ShapeDtypeStruct((D,), F32)] * 2
         out_specs += [pl.BlockSpec((D,), lambda i: (0,))] * 2
         scratch += [pltpu.VMEM((8, 8, WIDE), F32)]
     return pl.pallas_call(
-        functools.partial(finish_kernel, turns=turns, first=first, last=last),
+        functools.partial(finish_kernel, marks=marks, first=first, last=last),
         grid=(1,),
         in_specs=in_specs,
         out_specs=out_specs,
@@ -607,9 +638,12 @@
     )(*args)
 
 
-def call(kernel, outs, *args, smem=0, scratch=(), name=None, limit=24, windows=None):
+def call(kernel, outs, *args, smem=0, scratch=(), name=None, limit=24, windows=None,
+         anywhere=()):
     specs = [pl.BlockSpec(memory_space=pltpu.SMEM)] * smem
     specs += [pl.BlockSpec(memory_space=pltpu.VMEM)] * (len(args) - smem)
+    for n in anywhere:
+        specs[n] = pl.BlockSpec(memory_space=pl.ANY)
     for n, (shape, index) in (windows or {}).items():
         specs[n] = pl.BlockSpec(shape, lambda i, index=index: index)
     return pl.pallas_call(
@@ -628,6 +662,14 @@
     return lax.ppermute(block, "seq", [(i, i ^ code) for i in range(16)])
 
 
+def z_send(block):
+    def shift(d):
+        return lax.ppermute(block, "seq", [(i, (i + 4 * d) % 16) for i in range(16)])
+
+    got = {d: shift(d) for d in (2, 1, 3)}
+    return [got[1], got[2], got[3]]
+
+
 def after(*values):
     return lax.optimization_barrier(values)
 
@@ -655,8 +697,12 @@
     return route
 
 
+def hop(block, stage, d):
+    return lax.ppermute(block, AXES, ring_route(stage, d))
+
+
 def ring_send(blocks, stage):
-    got = {d: lax.ppermute(blocks[d - 1], AXES, ring_route(stage, d)) for d in (2, 1, 3)}
+    got = {d: hop(blocks[d - 1], stage, d) for d in (2, 1, 3)}
     return got[1], got[2], got[3]
 
 
@@ -673,7 +719,6 @@
 
 def sum_everywhere(meta, keep, sends, ext, beside):
     cut = D // 4
-    pad = pltpu.VMEM((4, 8, WIDE), F32)
     got = ring_send(sends, 0)
     *got, _ = after(*got, beside)
     keep, *sends = call(
@@ -684,30 +729,21 @@
     got = ring_send(sends, 1)
     block = call(
         add_b_kernel, [((cut + 16, WIDE), BF)],
-        meta, keep, *got, ext, smem=1, name="add_b", scratch=[pad],
+        meta, keep, *got, ext, smem=1, name="add_b", scratch=[pltpu.VMEM((4, 8, WIDE), F32)],
     )[0]
     got = ring_send([block] * 3, 2)
-    block, ext = call(
-        add_c_kernel, [((cut, WIDE), BF), ((16, WIDE), BF)],
-        meta, block, *got, smem=1, name="add_c",
-        scratch=[pltpu.VMEM((4, cut, WIDE), F32), pad],
-    )
+    block = call(add_c_kernel, [((cut + 16, WIDE), BF)], block, *got, name="add_c")[0]
     got = ring_send([block] * 3, 1)
     block = call(
-        merge_kernel, [((D + 16, WIDE), BF)],
-        meta, block, *got, ext, smem=1, name="merge_b",
+        merge_kernel, [((D + 16, WIDE), BF)], meta, block, *got, smem=1, name="merge_b",
     )[0]
-    ring = {d: lax.ppermute(block, AXES, ring_route(0, d)) for d in (1, 3, 2)}
-    ring[0] = block
-    twin = {0: swap_seq(block, 1)}
-    outs = finish(meta, [ring[0], twin[0]], (0,), None, None)
-    ring[1], ring[3], *outs = after(ring[1], ring[3], *outs)
-    twin[1], twin[3] = swap_seq(ring[1], 1), swap_seq(ring[3], 1)
-    outs = finish(meta, [ring[1], ring[3], twin[1], twin[3]], (1, 3), None, outs)
-    ring[2], *outs = after(ring[2], *outs)
-    twin[2] = swap_seq(ring[2], 1)
-    tails = [half[d] for half in (ring, twin) for d in range(4)]
-    return finish(meta, [ring[2], twin[2]], (2,), tails, outs)
+    ring = [block, *ring_send([block] * 3, 0)]
+    twin = [swap_seq(block, 1)]
+    outs = finish(meta, [(block, 0, 0, 0), (twin[0], 1, 0, 0)], None)
+    *ring, first = after(*ring, outs[0])
+    twin += [swap_seq(piece, 1) for piece in ring[1:]]
+    outs = finish(meta, [(ring[d], 0, d, 0) for d in (1, 2, 3)], (first, outs[1]))
+    return finish(meta, [(twin[d], 1, d, 0) for d in (1, 2, 3)], outs, ring + twin)
 
 
 def position_table():
@@ -730,41 +766,41 @@
     inp, normed, kv, kv_pack = call(
         key_kernel,
         [((T, D), F32), ((T, D), BF), ((T, 2 * D), BF), ((80, 2 * D), BF)],
-        tokens[0], tile_coords[0], table, norm_gain, norm_bias, w_qkv, w_qkv, name="keys",
-        windows={5: ((D, D), (0, 1)), 6: ((D, D), (0, 2))},
+        tokens[0], tile_coords[0], table, norm_gain, norm_bias, w_qkv, name="keys", limit=60,
+        anywhere=(0, 2, 5),
+        scratch=[
+            pltpu.VMEM((T, D), BF), pltpu.VMEM((T, 3 * D // 2), BF), pltpu.VMEM((2, D, D), BF),
+            pltpu.SemaphoreType.DMA((4,)),
+        ],
     )
     from_y = swap_seq(kv_pack, 2)
     norm_b = swap_seq(normed, 1)
     q, d_att, cot, qd_pack = call(
         query_kernel,
         [((T, D), BF), ((T, D), BF), ((T, D), BF), ((80, 2 * D), BF)],
-        normed, w_qkv, w_out, cotangent[0], name="queries",
+        normed, w_qkv, w_out, cotangent[0], name="queries", limit=60,
         windows={1: ((D, D), (0, 0))},
     )
     from_y, q, norm_b = after(from_y, q, norm_b)
     far = join(kv_pack[64:], from_y[64:])
-    from_z = swap_seq(far, 4)
-    o_1, top_1, sum_1 = call(
-        functools.partial(local_forward_kernel, first=0),
-        [((T, D // 2), F32), ((T, 128), F32), ((T, 128), F32)],
-        meta, q, kv, smem=1, name="local_forward",
-    )
-    from_z, o_1 = after(from_z, o_1)
-    part = join(kv_pack[:64], from_y[:64], far, from_z)
-    from_z = swap_seq(part[128:], 12)
-    part, q = after(part, q)
-    o_2, top_2, sum_2 = call(
-        functools.partial(local_forward_kernel, first=8),
-        [((T, D // 2), F32), ((T, 128), F32), ((T, 128), F32)],
-        meta, q, kv, smem=1, name="local_forward",
-    )
+    from_z = z_send(far)
+    far, q = after(far, q)
+    part = join(kv_pack[:64], from_y[:64], far)
     twin = swap_seq(part, 1)
-    from_z, twin, o_2 = after(from_z, twin, o_2)
-    got_kv = (part, from_z, twin, swap_seq(from_z, 1))
+    tops = [
+        call(
+            functools.partial(local_forward_kernel, first=first),
+            [((T, D // 2), F32), ((T, 128), F32), ((T, 128), F32)],
+            meta, q, kv, smem=1, name="local_forward",
+        )
+        for first in (0, 8)
+    ]
+    *from_z, twin, _, _ = after(*from_z, twin, tops[0][0], tops[1][0])
+    got_kv = (part, *from_z, twin, *[swap_seq(rows, 1) for rows in from_z])
     att, stat, pack = call(
         remote_forward_kernel,
         [((T, D), BF), ((T, 128), F32), ((80, 2 * D + 128), BF)],
-        meta, q, *got_kv, o_1, top_1, sum_1, o_2, top_2, sum_2, d_att, qd_pack,
+        meta, q, *got_kv, *tops[0], *tops[1], d_att, qd_pack,
         smem=1, name="remote_forward",
     )
     from_y = swap_seq(pack, 2)
@@ -774,29 +810,27 @@
         [((T, D // 2), F32)] * 3,
         meta, q, kv, d_att, stat, smem=1, name="local_backward",
     )
-    from_y, att_b, *grads_1 = after(from_y, att_b, *grads_1)
+    dq_r = call(
+        query_backward_kernel, [((T, D), F32)],
+        meta, q, d_att, stat, *got_kv, smem=1, name="query_backward",
+    )[0]
+    from_y, att_b, dq_r, *grads_1 = after(from_y, att_b, dq_r, *grads_1)
     far = join(pack[64:], from_y[64:])
-    from_z = swap_seq(far, 4)
+    from_z = z_send(far)
     far, q = after(far, q)
+    part = join(pack[:64], from_y[:64], far)
+    twin = swap_seq(part, 1)
     grads_2 = call(
         functools.partial(local_backward_kernel, first=8),
         [((T, D // 2), F32)] * 3,
         meta, q, kv, d_att, stat, smem=1, name="local_backward",
     )
-    from_z, *grads_2 = after(from_z, *grads_2)
-    part = join(pack[:64], from_y[:64], far, from_z)
-    from_z = swap_seq(part[128:], 12)
-    part, q = after(part, q)
-    dq_r = call(
-        query_backward_kernel, [((T, D), F32)],
-        meta, q, d_att, stat, *got_kv, smem=1, name="query_backward",
-    )[0]
-    twin = swap_seq(part, 1)
-    from_z, twin, dq_r = after(from_z, twin, dq_r)
+    *from_z, twin, _ = after(*from_z, twin, grads_2[0])
+    got_qd = (part, *from_z, twin, *[swap_seq(rows, 1) for rows in from_z])
     d_qkv, own, sent = call(
         key_backward_kernel,
         [((T, 3 * D), BF), ((T, 2 * D), BF), ((T, 2 * D), BF)],
-        meta, kv, part, from_z, twin, swap_seq(from_z, 1), dq_r, *grads_1, *grads_2, cot,
+        meta, kv, *got_qd, dq_r, *grads_1, *grads_2, cot,
         smem=1, name="key_backward",
         scratch=[pltpu.VMEM((T, D), F32), pltpu.VMEM((T, D), F32)],
     )

time: 165 us -> 144 us (0.87)
  local copies, waits for them, and re-layouts: 17.4 us -> 1.96 us
  starting transfers between devices: 48.3 us -> 41.6 us
  Pallas kernels: 40.6 us -> 44.6 us
    unnamed x70 -> x22, local copies, waits for them, and re-layouts: 14.4 us -> 0.04 us
    ppermute x17, starting transfers between devices: 31.6 us -> 20.1 us  [swap_seq(): return lax.ppermute(block, 'seq', [(i, i ^ code) for i in range(16)])]
    ppermute x17, waiting for transfers between devices: 17.1 us -> 5.77 us  [swap_seq(): return lax.ppermute(block, 'seq', [(i, i ^ code) for i in range(16)])]
    ppermute x15 -> x21, waiting for transfers between devices: 38.6 us -> 48.3 us  [the longest x15 40.6 us: hop(): return lax.ppermute(block, AXES, ring_route(stage, d))]
    ppermute x15 -> x21, starting transfers between devices: 16.7 us -> 21.5 us  [the longest x15 15.4 us: hop(): return lax.ppermute(block, AXES, ring_route(stage, d))]
    pallas_call x16, Pallas kernels: 33.1 us -> 37.1 us  [call(): pl.pallas_call(kernel, grid=(1,) if windows else (), out_shape=[jax.Shape...]
  transfers between devices with their start and end apart: 32 -> 38, of which waited for: 24 -> 28; matrix products, arithmetic and copies ran while one was open for 1% -> 1% of each run, Pallas kernels for 14% -> 17%
where the time goes in v3:
time: 144 us; the launch traced here: 143 us
  waiting for transfers between devices  54.1 us (38%)
  Pallas kernels  44.6 us (31%)
  starting transfers between devices  41.6 us (29%)
  local copies, waits for them, and re-layouts  1.96 us (1%)
    ppermute x15, waiting for transfers between devices, hop(): return lax.ppermute(block, AXES, ring_route(stage, d))  40.6 us
    pallas_call x16, Pallas kernels, call(): pl.pallas_call(kernel, grid=(1,) if windows else (), out_shape=[jax.Shape...  37.1 us
    ppermute x17, starting transfers between devices, swap_seq(): return lax.ppermute(block, 'seq', [(i, i ^ code) for i in range(16)])  20.1 us
    ppermute x15, starting transfers between devices, hop(): return lax.ppermute(block, AXES, ring_route(stage, d))  15.4 us
    ppermute x6, waiting for transfers between devices, shift(): lax.ppermute(block, 'seq', [(i, (i + 4 * d) % 16) for i in range(16)])  7.72 us
    pallas_call x3, Pallas kernels, finish(): pl.pallas_call(functools.partial(finish_kernel, marks=marks, first=first,...  7.48 us
    ppermute x6, starting transfers between devices, shift(): lax.ppermute(block, 'seq', [(i, (i + 4 * d) % 16) for i in range(16)])  6.02 us
    ppermute x17, waiting for transfers between devices, swap_seq(): return lax.ppermute(block, 'seq', [(i, i ^ code) for i in range(16)])  5.77 us
  transfers between devices with their start and end apart: 38, of which 28 were waited for; matrix products, arithmetic and copies ran while one was open for 1% of the time, Pallas kernels for 17%

profile of v3, /device:TPU:1, one launch (start us, length us, event | category | flops | bytes accessed | tf_op | source)
XLA Modules:
  0.0 143.3 jit_solution(11262763640905992299)
XLA Ops:
  0.6 4.9 %keys.1 = (f32[256,768]{1,0:T(8,128)}, bf16[256,768]{1,0:T(8,128)(2,1)}, bf16[256,1536]{1,0:T(8,128)(2,1)}, bf16[80,1536]{1,0:T(8,128)(2,1)}) custom-call(bf16[256,768]{1,0:T(8,128)(2,1)} %bitcast.13, s32[2,256]{1,0:T(2,128)} %bitcast.15, bf16[256,1152]{1,0:T(8,128)(2,1)} %constant.18.clone.table_h, f32[768]{0:T(1024)} %gain.3, f32[768]{0:T(1024)} %bias.1, ...), custom_call_target="tpu_custom_call" | custom-call | tf_op jit(solution)/shard_map/keys/pallas_call | solution.py:649
  7.1 3.0 %collective-permute-start = (bf16[80,1536]{1,0:T(8,128)(2,1)}, bf16[80,1536]{1,0:T(8,128)(2,1)S(1)}, u32[]{:S(2)}, u32[]{:S(2)}) collective-permute-start(bf16[80,1536]{1,0:T(8,128)(2,1)} %get-tuple-element.80), channel_id=1, source_target_pairs={{0,2},{1,3},{2,0},{3,1},{4,6},{5,7},{6,4},{7,5},{8,10},{9,11},{10,... | collective-permute-start | bytes 737288 | tf_op jit(solution)/shard_map/ppermute | solution.py:662
  11.9 3.7 %queries.1 = (bf16[256,768]{1,0:T(8,128)(2,1)}, bf16[256,768]{1,0:T(8,128)(2,1)}, bf16[256,768]{1,0:T(8,128)(2,1)}, bf16[80,1536]{1,0:T(8,128)(2,1)}) custom-call(bf16[256,768]{1,0:T(8,128)(2,1)} %get-tuple-element.81.normed.norm_a, bf16[768,2304]{1,0:T(8,128)(2,1)} %w_qkv.3, bf16[768,768]{1,0:T(8,128)(2,1)} %w_out.3, bf16[256,768]{1,0:T(8,128)(2,1)} %bitcast.14), custom_call_target="tpu_custom_call" | custom-call | tf_op jit(solution)/shard_map/queries/pallas_call | solution.py:649
  17.4 3.8 %collective-permute-start.4 = (bf16[32,1536]{1,0:T(8,128)(2,1)S(1)}, bf16[32,1536]{1,0:T(8,128)(2,1)S(1)}, u32[]{:S(2)}, u32[]{:S(2)}) collective-permute-start(bf16[32,1536]{1,0:T(8,128)(2,1)S(1)} %pad_maximum_fusion.3), channel_id=1, source_target_pairs={{0,12},{1,13},{2,14},{3,15},{4,0},{5,1},{6,2},{7,3},{8,4},{9,5},{1... | collective-permute-start | bytes 294920 | tf_op jit(solution)/shard_map/ppermute | solution.py:667
  22.0 1.8 %local_forward.3 = (f32[256,384]{1,0:T(8,128)S(1)}, f32[256,128]{1,0:T(8,128)S(1)}, f32[256,128]{1,0:T(8,128)S(1)}) custom-call(s32[16]{0:T(128)S(1)} %concatenate.15.meta, bf16[256,768]{1,0:T(8,128)(2,1)S(1)} %copy-done.2, bf16[256,1536]{1,0:T(8,128)(2,1)S(1)} %copy-done.1), custom_call_target="tpu_custom_call" | custom-call | tf_op jit(solution)/shard_map/local_forward/pallas_call | solution.py:649
  26.8 2.2 %collective-permute-done.2.refs_1_ = bf16[32,1536]{1,0:T(8,128)(2,1)S(1)} collective-permute-done((bf16[32,1536]{1,0:T(8,128)(2,1)S(1)}, bf16[32,1536]{1,0:T(8,128)(2,1)S(1)}, u32[]{:S(2)}, u32[]{:S(2)}) %collective-permute-start.2) | collective-permute-done | bytes 98336 | tf_op jit(solution)/shard_map/ppermute | solution.py:667
  31.2 3.4 %remote_forward.1 = (bf16[256,768]{1,0:T(8,128)(2,1)S(1)}, f32[256,128]{1,0:T(8,128)S(1)}, bf16[80,1664]{1,0:T(8,128)(2,1)S(1)}) custom-call(s32[16]{0:T(128)S(1)} %concatenate.15.meta, bf16[256,768]{1,0:T(8,128)(2,1)S(1)} %copy-done.2, bf16[160,1536]{1,0:T(8,128)(2,1)S(1)} %pad_maximum_fusion.1.refs_0_, ...), custom_call_target="tpu_custom_call" | custom-call | tf_op jit(solution)/shard_map/remote_forward/pallas_call | solution.py:649
  35.1 2.9 %collective-permute-start.9 = (bf16[80,1664]{1,0:T(8,128)(2,1)S(1)}, bf16[80,1664]{1,0:T(8,128)(2,1)S(1)}, u32[]{:S(2)}, u32[]{:S(2)}) collective-permute-start(bf16[80,1664]{1,0:T(8,128)(2,1)S(1)} %get-tuple-element.101), channel_id=1, source_target_pairs={{0,2},{1,3},{2,0},{3,1},{4,6},{5,7},{6,4},{7,5},{8,10},{9,11},{10,... | collective-permute-start | bytes 798728 | tf_op jit(solution)/shard_map/ppermute | solution.py:662
  38.0 3.4 %local_backward.2 = (f32[256,384]{1,0:T(8,128)S(1)}, f32[256,384]{1,0:T(8,128)S(1)}, f32[256,384]{1,0:T(8,128)S(1)}) custom-call(s32[16]{0:T(128)S(1)} %concatenate.15.meta, bf16[256,768]{1,0:T(8,128)(2,1)S(1)} %copy-done.2, bf16[256,1536]{1,0:T(8,128)(2,1)S(1)} %copy-done.1, bf16[256,768]{1,0:T(8,128)(2,1)S(1)} %copy-done.3, ...), custom_call_target="tpu_custom_call" | custom-call | tf_op jit(solution)/shard_map/local_backward/pallas_call | solution.py:649
  41.4 2.3 %query_backward.1.refs_8_ = f32[256,768]{1,0:T(8,128)S(1)} custom-call(s32[16]{0:T(128)S(1)} %concatenate.15.meta, bf16[256,768]{1,0:T(8,128)(2,1)S(1)} %copy-done.2, bf16[256,768]{1,0:T(8,128)(2,1)S(1)} %copy-done.3, f32[256,128]{1,0:T(8,128)S(1)} %get-tuple-element.102.stat, bf16[160,1536]{1,0:T(8,128)(2,1)S(1)} %pad_maximum_fusion.1.refs_0_, ...), custom_call_target="tpu_custom_call" | custom-call | tf_op jit(solution)/shard_map/query_backward/pallas_call | solution.py:649
  47.0 3.4 %local_backward.3 = (f32[256,384]{1,0:T(8,128)S(1)}, f32[256,384]{1,0:T(8,128)S(1)}, f32[256,384]{1,0:T(8,128)S(1)}) custom-call(s32[16]{0:T(128)S(1)} %concatenate.15.meta, bf16[256,768]{1,0:T(8,128)(2,1)S(1)} %copy-done.2, bf16[256,1536]{1,0:T(8,128)(2,1)S(1)} %copy-done.1, bf16[256,768]{1,0:T(8,128)(2,1)S(1)} %copy-done.3, ...), custom_call_target="tpu_custom_call" | custom-call | tf_op jit(solution)/shard_map/local_backward/pallas_call | solution.py:649
  51.9 3.0 %collective-permute-done.11.refs_1_ = bf16[32,1664]{1,0:T(8,128)(2,1)S(1)} collective-permute-done((bf16[32,1664]{1,0:T(8,128)(2,1)S(1)}, bf16[32,1664]{1,0:T(8,128)(2,1)S(1)}, u32[]{:S(2)}, u32[]{:S(2)}) %collective-permute-start.11) | collective-permute-done | bytes 106528 | tf_op jit(solution)/shard_map/ppermute | solution.py:667
  56.8 3.0 %key_backward.1 = (bf16[256,2304]{1,0:T(8,128)(2,1)S(1)}, bf16[256,1536]{1,0:T(8,128)(2,1)S(1)}, bf16[256,1536]{1,0:T(8,128)(2,1)S(1)}) custom-call(s32[16]{0:T(128)S(1)} %concatenate.15.meta, bf16[256,1536]{1,0:T(8,128)(2,1)S(1)} %copy-done.1, bf16[160,1664]{1,0:T(8,128)(2,1)S(1)} %pad_maximum_fusion.refs_0_, ...), custom_call_target="tpu_custom_call" | custom-call | tf_op jit(solution)/shard_map/key_backward/pallas_call | solution.py:649
  60.2 1.9 %collective-permute-done.18.other = bf16[256,1536]{1,0:T(8,128)(2,1)S(1)} collective-permute-done((bf16[256,1536]{1,0:T(8,128)(2,1)S(1)}, bf16[256,1536]{1,0:T(8,128)(2,1)S(1)}, u32[]{:S(2)}, u32[]{:S(2)}) %collective-permute-start.18) | collective-permute-done | bytes 786464 | tf_op jit(solution)/shard_map/ppermute | solution.py:662
  62.2 3.1 %weight_grad.1 = (f32[768,384]{1,0:T(8,128)S(1)}, bf16[768,384]{1,0:T(8,128)(2,1)S(1)}, bf16[768,384]{1,0:T(8,128)(2,1)S(1)}, bf16[768,384]{1,0:T(8,128)(2,1)S(1)}) custom-call(s32[16]{0:T(128)S(1)} %concatenate.15.meta, bf16[256,1536]{1,0:T(8,128)(2,1)S(1)} %get-tuple-element.121.own, bf16[256,1536]{1,0:T(8,128)(2,1)S(1)} %collective-permute-done.18.other, ...), custom_call_target="tpu_custom_call" | custom-call | tf_op jit(solution)/shard_map/weight_grad/pallas_call | solution.py:649
  66.6 2.6 %collective-permute-start.20 = (bf16[768,384]{1,0:T(8,128)(2,1)S(1)}, bf16[768,384]{1,0:T(8,128)(2,1)S(1)}, u32[]{:S(2)}, u32[]{:S(2)}) collective-permute-start(bf16[768,384]{1,0:T(8,128)(2,1)S(1)} %get-tuple-element.131), channel_id=1, source_target_pairs={{0,64},{1,3},{2,66},{3,1},{4,68},{5,7},{6,70},{7,5},{8,72},{9,11},... | collective-permute-start | bytes 1769480 | tf_op jit(solution)/shard_map/ppermute | solution.py:701
  70.3 2.5 %token_grad.1 = (bf16[256,768]{1,0:T(8,128)(2,1)}, bf16[16,384]{1,0:T(8,128)(2,1)S(1)}) custom-call(bf16[256,2304]{1,0:T(8,128)(2,1)S(1)} %get-tuple-element.128.d_qkv, bf16[768,2304]{1,0:T(8,128)(2,1)S(1)} %copy-done, f32[256,768]{1,0:T(8,128)S(1)} %copy-done.5, f32[768]{0:T(1024)S(1)} %copy-done.9, bf16[256,768]{1,0:T(8,128)(2,1)S(1)} %copy-done.6), custom_call_target="tpu_custom_call" | custom-call | tf_op jit(solution)/shard_map/token_grad/pallas_call | solution.py:649
  75.6 7.5 %collective-permute-done.20.r2 = bf16[768,384]{1,0:T(8,128)(2,1)S(1)} collective-permute-done((bf16[768,384]{1,0:T(8,128)(2,1)S(1)}, bf16[768,384]{1,0:T(8,128)(2,1)S(1)}, u32[]{:S(2)}, u32[]{:S(2)}) %collective-permute-start.20) | collective-permute-done | bytes 589856 | tf_op jit(solution)/shard_map/ppermute | solution.py:701
  86.7 4.4 %collective-permute-done.22.r1 = bf16[208,384]{1,0:T(8,128)(2,1)S(1)} collective-permute-done((bf16[208,384]{1,0:T(8,128)(2,1)S(1)}, bf16[208,384]{1,0:T(8,128)(2,1)S(1)}, u32[]{:S(2)}, u32[]{:S(2)}) %collective-permute-start.22) | collective-permute-done | bytes 159776 | tf_op jit(solution)/shard_map/ppermute | solution.py:701
  92.4 2.2 %collective-permute-start.27 = (bf16[208,384]{1,0:T(8,128)(2,1)S(1)}, bf16[208,384]{1,0:T(8,128)(2,1)S(1)}, u32[]{:S(2)}, u32[]{:S(2)}) collective-permute-start(bf16[208,384]{1,0:T(8,128)(2,1)S(1)} %add_b.1.own), channel_id=1, source_target_pairs={{0,12},{1,97},{2,14},{3,99},{4,0},{5,101},{6,2},{7,103},{8,4},{9,1... | collective-permute-start | bytes 479240 | tf_op jit(solution)/shard_map/ppermute | solution.py:701
  95.7 2.8 %collective-permute-done.27.r3 = bf16[208,384]{1,0:T(8,128)(2,1)S(1)} collective-permute-done((bf16[208,384]{1,0:T(8,128)(2,1)S(1)}, bf16[208,384]{1,0:T(8,128)(2,1)S(1)}, u32[]{:S(2)}, u32[]{:S(2)}) %collective-permute-start.27) | collective-permute-done | bytes 159776 | tf_op jit(solution)/shard_map/ppermute | solution.py:701
  98.5 2.0 %collective-permute-done.26.r2 = bf16[208,384]{1,0:T(8,128)(2,1)S(1)} collective-permute-done((bf16[208,384]{1,0:T(8,128)(2,1)S(1)}, bf16[208,384]{1,0:T(8,128)(2,1)S(1)}, u32[]{:S(2)}, u32[]{:S(2)}) %collective-permute-start.26) | collective-permute-done | bytes 159776 | tf_op jit(solution)/shard_map/ppermute | solution.py:701
  102.4 2.1 %collective-permute-start.30 = (bf16[208,384]{1,0:T(8,128)(2,1)S(1)}, bf16[208,384]{1,0:T(8,128)(2,1)S(1)}, u32[]{:S(2)}, u32[]{:S(2)}) collective-permute-start(bf16[208,384]{1,0:T(8,128)(2,1)S(1)} %add_c.1.own), channel_id=1, source_target_pairs={{0,18},{1,13},{2,16},{3,15},{4,22},{5,1},{6,20},{7,3},{8,26},{9,5}... | collective-permute-start | bytes 479240 | tf_op jit(solution)/shard_map/ppermute | solution.py:701
  105.1 3.3 %collective-permute-done.30.r3 = bf16[208,384]{1,0:T(8,128)(2,1)S(1)} collective-permute-done((bf16[208,384]{1,0:T(8,128)(2,1)S(1)}, bf16[208,384]{1,0:T(8,128)(2,1)S(1)}, u32[]{:S(2)}, u32[]{:S(2)}) %collective-permute-start.30) | collective-permute-done | bytes 159776 | tf_op jit(solution)/shard_map/ppermute | solution.py:701
  112.4 3.7 %collective-permute-start.34 = (bf16[784,384]{1,0:T(8,128)(2,1)S(1)}, bf16[784,384]{1,0:T(8,128)(2,1)S(1)}, u32[]{:S(2)}, u32[]{:S(2)}) collective-permute-start(bf16[784,384]{1,0:T(8,128)(2,1)S(1)} %merge_b.1.refs_0_.refs_3_), channel_id=1, source_target_pairs={{0,1},{1,0},{2,3},{3,2},{4,5},{5,4},{6,7},{7,6},{8,9},{9,8},{10,11... | collective-permute-start | bytes 1806344 | tf_op jit(solution)/shard_map/ppermute | solution.py:662
  117.8 2.0 %finish.3 = (f32[768,2304]{1,0:T(8,128)}, f32[768,768]{1,0:T(8,128)}) custom-call(s32[16]{0:T(128)S(1)} %concatenate.15.meta, bf16[784,384]{1,0:T(8,128)(2,1)S(1)} %merge_b.1.refs_0_.refs_3_, bf16[784,384]{1,0:T(8,128)(2,1)S(1)} %collective-permute-done.34.refs_1_.refs_7_), custom_call_target="tpu_custom_call" | custom-call | tf_op jit(solution)/shard_map/finish/pallas_call | solution.py:628
  119.9 5.5 %collective-permute-done.33.refs_2_.refs_6_ = bf16[784,384]{1,0:T(8,128)(2,1)S(1)} collective-permute-done((bf16[784,384]{1,0:T(8,128)(2,1)S(1)}, bf16[784,384]{1,0:T(8,128)(2,1)S(1)}, u32[]{:S(2)}, u32[]{:S(2)}) %collective-permute-start.33) | collective-permute-done | bytes 602144 | tf_op jit(solution)/shard_map/ppermute | solution.py:701
  125.3 1.8 %collective-permute-done.32.refs_1_.refs_5_ = bf16[784,384]{1,0:T(8,128)(2,1)S(1)} collective-permute-done((bf16[784,384]{1,0:T(8,128)(2,1)S(1)}, bf16[784,384]{1,0:T(8,128)(2,1)S(1)}, u32[]{:S(2)}, u32[]{:S(2)}) %collective-permute-start.32) | collective-permute-done | bytes 602144 | tf_op jit(solution)/shard_map/ppermute | solution.py:701
  127.2 6.4 %collective-permute-done.31.refs_0_.refs_4_ = bf16[784,384]{1,0:T(8,128)(2,1)S(1)} collective-permute-done((bf16[784,384]{1,0:T(8,128)(2,1)S(1)}, bf16[784,384]{1,0:T(8,128)(2,1)S(1)}, u32[]{:S(2)}, u32[]{:S(2)}) %collective-permute-start.31) | collective-permute-done | bytes 602144 | tf_op jit(solution)/shard_map/ppermute | solution.py:701
  133.6 3.2 %collective-permute-start.35 = (bf16[784,384]{1,0:T(8,128)(2,1)S(1)}, bf16[784,384]{1,0:T(8,128)(2,1)S(1)}, u32[]{:S(2)}, u32[]{:S(2)}) collective-permute-start(bf16[784,384]{1,0:T(8,128)(2,1)S(1)} %collective-permute-done.31.refs_0_.refs_4_), channel_id=1, source_target_pairs={{0,1},{1,0},{2,3},{3,2},{4,5},{5,4},{6,7},{7,6},{8,9},{9,8},{10,11... | collective-permute-start | bytes 1806344 | tf_op jit(solution)/shard_map/ppermute | solution.py:662
  137.3 2.4 %finish.4 = (f32[768,2304]{1,0:T(8,128)}, f32[768,768]{1,0:T(8,128)}) custom-call(s32[16]{0:T(128)S(1)} %concatenate.15.meta, bf16[784,384]{1,0:T(8,128)(2,1)S(1)} %collective-permute-done.31.refs_0_.refs_4_, bf16[784,384]{1,0:T(8,128)(2,1)S(1)} %collective-permute-done.32.refs_1_.refs_5_, ...), custom_call_target="tpu_custom_call", output_to_operand_aliasing={{0}: (4, {}), {1}: (5, {})} | custom-call | tf_op jit(solution)/shard_map/finish/pallas_call | solution.py:628
  140.1 3.0 %finish.5 = (f32[768,2304]{1,0:T(8,128)}, f32[768,768]{1,0:T(8,128)}, f32[768]{0:T(1024)}, f32[768]{0:T(1024)}) custom-call(s32[16]{0:T(128)S(1)} %concatenate.15.meta, bf16[784,384]{1,0:T(8,128)(2,1)S(1)} %collective-permute-done.35.refs_0_.refs_8_, ...), custom_call_target="tpu_custom_call", output_to_operand_aliasing={{0}: (12, {}), {1}: (13, {})} | custom-call | tf_op jit(solution)/shard_map/finish/pallas_call | solution.py:628
  (99 shorter events, 38.8 us)
Async XLA Ops:
  5.6 10.8 %collective-permute-start.1 = (bf16[256,768]{1,0:T(8,128)(2,1)}, bf16[256,768]{1,0:T(8,128)(2,1)S(1)}, u32[]{:S(2)}, u32[]{:S(2)}) collective-permute-start(bf16[256,768]{1,0:T(8,128)(2,1)} %get-tuple-element.81.normed.norm_a), channel_id=1, source_target_pairs={{0,1},{1,0},{2,3},{3,2},{4,5},{5,4},{6,7},{7,6},{8,9},{9,8},{10,11... | collective-permute-start | bytes 1179656 | tf_op jit(solution)/shard_map/ppermute | solution.py:662
  7.1 9.3 %collective-permute-start = (bf16[80,1536]{1,0:T(8,128)(2,1)}, bf16[80,1536]{1,0:T(8,128)(2,1)S(1)}, u32[]{:S(2)}, u32[]{:S(2)}) collective-permute-start(bf16[80,1536]{1,0:T(8,128)(2,1)} %get-tuple-element.80), channel_id=1, source_target_pairs={{0,2},{1,3},{2,0},{3,1},{4,6},{5,7},{6,4},{7,5},{8,10},{9,11},{10,... | collective-permute-start | bytes 737288 | tf_op jit(solution)/shard_map/ppermute | solution.py:662
  16.5 12.5 %collective-permute-start.5 = (bf16[160,1536]{1,0:T(8,128)(2,1)S(1)}, bf16[160,1536]{1,0:T(8,128)(2,1)S(1)}, u32[]{:S(2)}, u32[]{:S(2)}) collective-permute-start(bf16[160,1536]{1,0:T(8,128)(2,1)S(1)} %pad_maximum_fusion.1.refs_0_), channel_id=1, source_target_pairs={{0,1},{1,0},{2,3},{3,2},{4,5},{5,4},{6,7},{7,6},{8,9},{9,8},{10,11... | collective-permute-start | bytes 1474568 | tf_op jit(solution)/shard_map/ppermute | solution.py:662
  17.4 8.3 %collective-permute-start.4 = (bf16[32,1536]{1,0:T(8,128)(2,1)S(1)}, bf16[32,1536]{1,0:T(8,128)(2,1)S(1)}, u32[]{:S(2)}, u32[]{:S(2)}) collective-permute-start(bf16[32,1536]{1,0:T(8,128)(2,1)S(1)} %pad_maximum_fusion.3), channel_id=1, source_target_pairs={{0,12},{1,13},{2,14},{3,15},{4,0},{5,1},{6,2},{7,3},{8,4},{9,5},{1... | collective-permute-start | bytes 294920 | tf_op jit(solution)/shard_map/ppermute | solution.py:667
  21.2 5.6 %collective-permute-start.3 = (bf16[32,1536]{1,0:T(8,128)(2,1)S(1)}, bf16[32,1536]{1,0:T(8,128)(2,1)S(1)}, u32[]{:S(2)}, u32[]{:S(2)}) collective-permute-start(bf16[32,1536]{1,0:T(8,128)(2,1)S(1)} %pad_maximum_fusion.3), channel_id=1, source_target_pairs={{0,8},{1,9},{2,10},{3,11},{4,12},{5,13},{6,14},{7,15},{8,0},{9,1},... | collective-permute-start | bytes 294920 | tf_op jit(solution)/shard_map/ppermute | solution.py:667
  21.2 7.8 %collective-permute-start.2 = (bf16[32,1536]{1,0:T(8,128)(2,1)S(1)}, bf16[32,1536]{1,0:T(8,128)(2,1)S(1)}, u32[]{:S(2)}, u32[]{:S(2)}) collective-permute-start(bf16[32,1536]{1,0:T(8,128)(2,1)S(1)} %pad_maximum_fusion.3), channel_id=1, source_target_pairs={{0,4},{1,5},{2,6},{3,7},{4,8},{5,9},{6,10},{7,11},{8,12},{9,13},{1... | collective-permute-start | bytes 294920 | tf_op jit(solution)/shard_map/ppermute | solution.py:667
  34.6 9.7 %collective-permute-start.10 = (bf16[256,768]{1,0:T(8,128)(2,1)S(1)}, bf16[256,768]{1,0:T(8,128)(2,1)S(1)}, u32[]{:S(2)}, u32[]{:S(2)}) collective-permute-start(bf16[256,768]{1,0:T(8,128)(2,1)S(1)} %get-tuple-element.126.att_a.att), channel_id=1, source_target_pairs={{0,1},{1,0},{2,3},{3,2},{4,5},{5,4},{6,7},{7,6},{8,9},{9,8},{10,11... | collective-permute-start | bytes 1179656 | tf_op jit(solution)/shard_map/ppermute | solution.py:662
  35.1 9.2 %collective-permute-start.9 = (bf16[80,1664]{1,0:T(8,128)(2,1)S(1)}, bf16[80,1664]{1,0:T(8,128)(2,1)S(1)}, u32[]{:S(2)}, u32[]{:S(2)}) collective-permute-start(bf16[80,1664]{1,0:T(8,128)(2,1)S(1)} %get-tuple-element.101), channel_id=1, source_target_pairs={{0,2},{1,3},{2,0},{3,1},{4,6},{5,7},{6,4},{7,5},{8,10},{9,11},{10,... | collective-permute-start | bytes 798728 | tf_op jit(solution)/shard_map/ppermute | solution.py:662
  44.4 10.5 %collective-permute-start.14 = (bf16[160,1664]{1,0:T(8,128)(2,1)S(1)}, bf16[160,1664]{1,0:T(8,128)(2,1)S(1)}, u32[]{:S(2)}, u32[]{:S(2)}) collective-permute-start(bf16[160,1664]{1,0:T(8,128)(2,1)S(1)} %pad_maximum_fusion.refs_0_), channel_id=1, source_target_pairs={{0,1},{1,0},{2,3},{3,2},{4,5},{5,4},{6,7},{7,6},{8,9},{9,8},{10,11... | collective-permute-start | bytes 1597448 | tf_op jit(solution)/shard_map/ppermute | solution.py:662
  45.6 4.9 %collective-permute-start.13 = (bf16[32,1664]{1,0:T(8,128)(2,1)S(1)}, bf16[32,1664]{1,0:T(8,128)(2,1)S(1)}, u32[]{:S(2)}, u32[]{:S(2)}) collective-permute-start(bf16[32,1664]{1,0:T(8,128)(2,1)S(1)} %pad_maximum_fusion.2), channel_id=1, source_target_pairs={{0,12},{1,13},{2,14},{3,15},{4,0},{5,1},{6,2},{7,3},{8,4},{9,5},{1... | collective-permute-start | bytes 319496 | tf_op jit(solution)/shard_map/ppermute | solution.py:667
  46.2 5.7 %collective-permute-start.12 = (bf16[32,1664]{1,0:T(8,128)(2,1)S(1)}, bf16[32,1664]{1,0:T(8,128)(2,1)S(1)}, u32[]{:S(2)}, u32[]{:S(2)}) collective-permute-start(bf16[32,1664]{1,0:T(8,128)(2,1)S(1)} %pad_maximum_fusion.2), channel_id=1, source_target_pairs={{0,8},{1,9},{2,10},{3,11},{4,12},{5,13},{6,14},{7,15},{8,0},{9,1},... | collective-permute-start | bytes 319496 | tf_op jit(solution)/shard_map/ppermute | solution.py:667
  46.3 8.6 %collective-permute-start.11 = (bf16[32,1664]{1,0:T(8,128)(2,1)S(1)}, bf16[32,1664]{1,0:T(8,128)(2,1)S(1)}, u32[]{:S(2)}, u32[]{:S(2)}) collective-permute-start(bf16[32,1664]{1,0:T(8,128)(2,1)S(1)} %pad_maximum_fusion.2), channel_id=1, source_target_pairs={{0,4},{1,5},{2,6},{3,7},{4,8},{5,9},{6,10},{7,11},{8,12},{9,13},{1... | collective-permute-start | bytes 319496 | tf_op jit(solution)/shard_map/ppermute | solution.py:667
  59.8 2.4 %collective-permute-start.18 = (bf16[256,1536]{1,0:T(8,128)(2,1)S(1)}, bf16[256,1536]{1,0:T(8,128)(2,1)S(1)}, u32[]{:S(2)}, u32[]{:S(2)}) collective-permute-start(bf16[256,1536]{1,0:T(8,128)(2,1)S(1)} %get-tuple-element.122), channel_id=1, source_target_pairs={{0,1},{1,0},{2,3},{3,2},{4,5},{5,4},{6,7},{7,6},{8,9},{9,8},{10,11... | collective-permute-start | bytes 2359304 | tf_op jit(solution)/shard_map/ppermute | solution.py:662
  65.3 10.4 %collective-permute-start.19 = (bf16[768,384]{1,0:T(8,128)(2,1)S(1)}, bf16[768,384]{1,0:T(8,128)(2,1)S(1)}, u32[]{:S(2)}, u32[]{:S(2)}) collective-permute-start(bf16[768,384]{1,0:T(8,128)(2,1)S(1)} %get-tuple-element.130), channel_id=1, source_target_pairs={{0,32},{1,17},{2,34},{3,19},{4,36},{5,21},{6,38},{7,23},{8,40},{9,... | collective-permute-start | bytes 1769480 | tf_op jit(solution)/shard_map/ppermute | solution.py:701
  66.6 16.5 %collective-permute-start.20 = (bf16[768,384]{1,0:T(8,128)(2,1)S(1)}, bf16[768,384]{1,0:T(8,128)(2,1)S(1)}, u32[]{:S(2)}, u32[]{:S(2)}) collective-permute-start(bf16[768,384]{1,0:T(8,128)(2,1)S(1)} %get-tuple-element.131), channel_id=1, source_target_pairs={{0,64},{1,3},{2,66},{3,1},{4,68},{5,7},{6,70},{7,5},{8,72},{9,11},... | collective-permute-start | bytes 1769480 | tf_op jit(solution)/shard_map/ppermute | solution.py:701
  69.2 13.9 %collective-permute-start.21 = (bf16[768,384]{1,0:T(8,128)(2,1)S(1)}, bf16[768,384]{1,0:T(8,128)(2,1)S(1)}, u32[]{:S(2)}, u32[]{:S(2)}) collective-permute-start(bf16[768,384]{1,0:T(8,128)(2,1)S(1)} %get-tuple-element.132), channel_id=1, source_target_pairs={{0,96},{1,19},{2,98},{3,17},{4,100},{5,23},{6,102},{7,21},{8,104},... | collective-permute-start | bytes 1769480 | tf_op jit(solution)/shard_map/ppermute | solution.py:701
  84.0 7.1 %collective-permute-start.22 = (bf16[208,384]{1,0:T(8,128)(2,1)S(1)}, bf16[208,384]{1,0:T(8,128)(2,1)S(1)}, u32[]{:S(2)}, u32[]{:S(2)}) collective-permute-start(bf16[208,384]{1,0:T(8,128)(2,1)S(1)} %get-tuple-element.138), channel_id=1, source_target_pairs={{0,16},{1,5},{2,18},{3,7},{4,20},{5,9},{6,22},{7,11},{8,24},{9,13}... | collective-permute-start | bytes 479240 | tf_op jit(solution)/shard_map/ppermute | solution.py:701
  84.0 7.0 %collective-permute-start.23 = (bf16[208,384]{1,0:T(8,128)(2,1)S(1)}, bf16[208,384]{1,0:T(8,128)(2,1)S(1)}, u32[]{:S(2)}, u32[]{:S(2)}) collective-permute-start(bf16[208,384]{1,0:T(8,128)(2,1)S(1)} %get-tuple-element.139), channel_id=1, source_target_pairs={{0,2},{1,9},{2,0},{3,11},{4,6},{5,13},{6,4},{7,15},{8,10},{9,1},{1... | collective-permute-start | bytes 479240 | tf_op jit(solution)/shard_map/ppermute | solution.py:701
  85.5 6.2 %collective-permute-start.24 = (bf16[208,384]{1,0:T(8,128)(2,1)S(1)}, bf16[208,384]{1,0:T(8,128)(2,1)S(1)}, u32[]{:S(2)}, u32[]{:S(2)}) collective-permute-start(bf16[208,384]{1,0:T(8,128)(2,1)S(1)} %get-tuple-element.140), channel_id=1, source_target_pairs={{0,18},{1,13},{2,16},{3,15},{4,22},{5,1},{6,20},{7,3},{8,26},{9,5}... | collective-permute-start | bytes 479240 | tf_op jit(solution)/shard_map/ppermute | solution.py:701
  92.4 6.2 %collective-permute-start.27 = (bf16[208,384]{1,0:T(8,128)(2,1)S(1)}, bf16[208,384]{1,0:T(8,128)(2,1)S(1)}, u32[]{:S(2)}, u32[]{:S(2)}) collective-permute-start(bf16[208,384]{1,0:T(8,128)(2,1)S(1)} %add_b.1.own), channel_id=1, source_target_pairs={{0,12},{1,97},{2,14},{3,99},{4,0},{5,101},{6,2},{7,103},{8,4},{9,1... | collective-permute-start | bytes 479240 | tf_op jit(solution)/shard_map/ppermute | solution.py:701
  94.6 5.9 %collective-permute-start.26 = (bf16[208,384]{1,0:T(8,128)(2,1)S(1)}, bf16[208,384]{1,0:T(8,128)(2,1)S(1)}, u32[]{:S(2)}, u32[]{:S(2)}) collective-permute-start(bf16[208,384]{1,0:T(8,128)(2,1)S(1)} %add_b.1.own), channel_id=1, source_target_pairs={{0,8},{1,65},{2,10},{3,67},{4,12},{5,69},{6,14},{7,71},{8,0},{9,73... | collective-permute-start | bytes 479240 | tf_op jit(solution)/shard_map/ppermute | solution.py:701
  95.1 7.1 %collective-permute-start.25 = (bf16[208,384]{1,0:T(8,128)(2,1)S(1)}, bf16[208,384]{1,0:T(8,128)(2,1)S(1)}, u32[]{:S(2)}, u32[]{:S(2)}) collective-permute-start(bf16[208,384]{1,0:T(8,128)(2,1)S(1)} %add_b.1.own), channel_id=1, source_target_pairs={{0,4},{1,33},{2,6},{3,35},{4,8},{5,37},{6,10},{7,39},{8,12},{9,41}... | collective-permute-start | bytes 479240 | tf_op jit(solution)/shard_map/ppermute | solution.py:701
  102.4 6.1 %collective-permute-start.30 = (bf16[208,384]{1,0:T(8,128)(2,1)S(1)}, bf16[208,384]{1,0:T(8,128)(2,1)S(1)}, u32[]{:S(2)}, u32[]{:S(2)}) collective-permute-start(bf16[208,384]{1,0:T(8,128)(2,1)S(1)} %add_c.1.own), channel_id=1, source_target_pairs={{0,18},{1,13},{2,16},{3,15},{4,22},{5,1},{6,20},{7,3},{8,26},{9,5}... | collective-permute-start | bytes 479240 | tf_op jit(solution)/shard_map/ppermute | solution.py:701
  104.5 5.7 %collective-permute-start.29 = (bf16[208,384]{1,0:T(8,128)(2,1)S(1)}, bf16[208,384]{1,0:T(8,128)(2,1)S(1)}, u32[]{:S(2)}, u32[]{:S(2)}) collective-permute-start(bf16[208,384]{1,0:T(8,128)(2,1)S(1)} %add_c.1.own), channel_id=1, source_target_pairs={{0,2},{1,9},{2,0},{3,11},{4,6},{5,13},{6,4},{7,15},{8,10},{9,1},{1... | collective-permute-start | bytes 479240 | tf_op jit(solution)/shard_map/ppermute | solution.py:701
  104.5 7.3 %collective-permute-start.28 = (bf16[208,384]{1,0:T(8,128)(2,1)S(1)}, bf16[208,384]{1,0:T(8,128)(2,1)S(1)}, u32[]{:S(2)}, u32[]{:S(2)}) collective-permute-start(bf16[208,384]{1,0:T(8,128)(2,1)S(1)} %add_c.1.own), channel_id=1, source_target_pairs={{0,16},{1,5},{2,18},{3,7},{4,20},{5,9},{6,22},{7,11},{8,24},{9,13}... | collective-permute-start | bytes 479240 | tf_op jit(solution)/shard_map/ppermute | solution.py:701
  112.4 5.4 %collective-permute-start.34 = (bf16[784,384]{1,0:T(8,128)(2,1)S(1)}, bf16[784,384]{1,0:T(8,128)(2,1)S(1)}, u32[]{:S(2)}, u32[]{:S(2)}) collective-permute-start(bf16[784,384]{1,0:T(8,128)(2,1)S(1)} %merge_b.1.refs_0_.refs_3_), channel_id=1, source_target_pairs={{0,1},{1,0},{2,3},{3,2},{4,5},{5,4},{6,7},{7,6},{8,9},{9,8},{10,11... | collective-permute-start | bytes 1806344 | tf_op jit(solution)/shard_map/ppermute | solution.py:662
  116.2 9.2 %collective-permute-start.33 = (bf16[784,384]{1,0:T(8,128)(2,1)S(1)}, bf16[784,384]{1,0:T(8,128)(2,1)S(1)}, u32[]{:S(2)}, u32[]{:S(2)}) collective-permute-start(bf16[784,384]{1,0:T(8,128)(2,1)S(1)} %merge_b.1.refs_0_.refs_3_), channel_id=1, source_target_pairs={{0,96},{1,19},{2,98},{3,17},{4,100},{5,23},{6,102},{7,21},{8,104},... | collective-permute-start | bytes 1806344 | tf_op jit(solution)/shard_map/ppermute | solution.py:701
  116.5 10.7 %collective-permute-start.32 = (bf16[784,384]{1,0:T(8,128)(2,1)S(1)}, bf16[784,384]{1,0:T(8,128)(2,1)S(1)}, u32[]{:S(2)}, u32[]{:S(2)}) collective-permute-start(bf16[784,384]{1,0:T(8,128)(2,1)S(1)} %merge_b.1.refs_0_.refs_3_), channel_id=1, source_target_pairs={{0,64},{1,3},{2,66},{3,1},{4,68},{5,7},{6,70},{7,5},{8,72},{9,11},... | collective-permute-start | bytes 1806344 | tf_op jit(solution)/shard_map/ppermute | solution.py:701
  117.0 16.6 %collective-permute-start.31 = (bf16[784,384]{1,0:T(8,128)(2,1)S(1)}, bf16[784,384]{1,0:T(8,128)(2,1)S(1)}, u32[]{:S(2)}, u32[]{:S(2)}) collective-permute-start(bf16[784,384]{1,0:T(8,128)(2,1)S(1)} %merge_b.1.refs_0_.refs_3_), channel_id=1, source_target_pairs={{0,32},{1,17},{2,34},{3,19},{4,36},{5,21},{6,38},{7,23},{8,40},{9,... | collective-permute-start | bytes 1806344 | tf_op jit(solution)/shard_map/ppermute | solution.py:701
  133.6 6.1 %collective-permute-start.35 = (bf16[784,384]{1,0:T(8,128)(2,1)S(1)}, bf16[784,384]{1,0:T(8,128)(2,1)S(1)}, u32[]{:S(2)}, u32[]{:S(2)}) collective-permute-start(bf16[784,384]{1,0:T(8,128)(2,1)S(1)} %collective-permute-done.31.refs_0_.refs_4_), channel_id=1, source_target_pairs={{0,1},{1,0},{2,3},{3,2},{4,5},{5,4},{6,7},{7,6},{8,9},{9,8},{10,11... | collective-permute-start | bytes 1806344 | tf_op jit(solution)/shard_map/ppermute | solution.py:662
  136.8 3.0 %collective-permute-start.36 = (bf16[784,384]{1,0:T(8,128)(2,1)S(1)}, bf16[784,384]{1,0:T(8,128)(2,1)S(1)}, u32[]{:S(2)}, u32[]{:S(2)}) collective-permute-start(bf16[784,384]{1,0:T(8,128)(2,1)S(1)} %collective-permute-done.32.refs_1_.refs_5_), channel_id=1, source_target_pairs={{0,1},{1,0},{2,3},{3,2},{4,5},{5,4},{6,7},{7,6},{8,9},{9,8},{10,11... | collective-permute-start | bytes 1806344 | tf_op jit(solution)/shard_map/ppermute | solution.py:662
  136.8 3.4 %collective-permute-start.37 = (bf16[784,384]{1,0:T(8,128)(2,1)S(1)}, bf16[784,384]{1,0:T(8,128)(2,1)S(1)}, u32[]{:S(2)}, u32[]{:S(2)}) collective-permute-start(bf16[784,384]{1,0:T(8,128)(2,1)S(1)} %collective-permute-done.33.refs_2_.refs_6_), channel_id=1, source_target_pairs={{0,1},{1,0},{2,3},{3,2},{4,5},{5,4},{6,7},{7,6},{8,9},{9,8},{10,11... | collective-permute-start | bytes 1806344 | tf_op jit(solution)/shard_map/ppermute | solution.py:662
  (17 other events, 96.4 us)

commit v4 on v3

--- a/solution.py
+++ b/solution.py
@@ -355,6 +355,7 @@
 
 def local_backward_kernel(meta, q_r, kv, d_att, stat, dq_o, dk_o, dv_o, *, first):
     bias = local_bias(meta)
+    stat_t = stat[...].T
     dq_o[...] = jnp.zeros_like(dq_o)
     dk_o[...] = jnp.zeros_like(dk_o)
     dv_o[...] = jnp.zeros_like(dv_o)
@@ -366,13 +367,13 @@
         q = q_r[:, s : s + w] * mask
         k = kv[:, s : s + w] * mask
         da = d_att[:, s : s + w] * mask
-        scores = nt(q, k) * SCALE + bias
-        shares = jnp.exp(scores - stat[:, h : h + 1])
-        d_shares = nt(da, kv[:, D + s : D + s + w])
-        ds = (shares * (d_shares - stat[:, HEADS + h : HEADS + h + 1])).astype(BF)
-        dq_o[:, t : t + w] += nn(ds, k)
-        dk_o[:, t : t + w] += tn(ds, q)
-        dv_o[:, t : t + w] += tn(shares.astype(BF), da)
+        scores = nt(k, q) * SCALE + bias
+        shares = jnp.exp(scores - stat_t[h : h + 1, :])
+        d_shares = nt(kv[:, D + s : D + s + w], da)
+        ds = (shares * (d_shares - stat_t[HEADS + h : HEADS + h + 1, :])).astype(BF)
+        dk_o[:, t : t + w] += nn(ds, q)
+        dv_o[:, t : t + w] += nn(shares.astype(BF), da)
+        dq_o[:, t : t + w] += tn(ds, k)
 
 
 def query_backward_kernel(meta, q_r, d_att, stat, *refs):
@@ -466,7 +467,7 @@
     sent_o[:, D:] = jnp.where(first, cot[...], d_k)
 
 
-def weight_grad_kernel(meta, own, other, norm_a, norm_b, att_a, att_b, keep_o, s1, s2, s3, left):
+def left_kernel(meta, norm_a, norm_b, att_a, att_b, left):
     left[0] = jnp.concatenate([norm_a[...], norm_b[...]], axis=0).T
     left[1] = left[0]
 
@@ -474,6 +475,8 @@
     def _():
         left[1] = jnp.concatenate([att_a[...], att_b[...]], axis=0).T
 
+
+def weight_grad_kernel(meta, own, other, left, keep_o, s1, s2, s3):
     for d, out in ((2, s2), (1, s1), (3, s3), (0, keep_o)):
         j = (meta[6] + d) & 3
         cols = pl.ds(pl.multiple_of(j * WIDE, 128), WIDE)
@@ -740,10 +743,13 @@
     ring = [block, *ring_send([block] * 3, 0)]
     twin = [swap_seq(block, 1)]
     outs = finish(meta, [(block, 0, 0, 0), (twin[0], 1, 0, 0)], None)
-    *ring, first = after(*ring, outs[0])
-    twin += [swap_seq(piece, 1) for piece in ring[1:]]
-    outs = finish(meta, [(ring[d], 0, d, 0) for d in (1, 2, 3)], (first, outs[1]))
-    return finish(meta, [(twin[d], 1, d, 0) for d in (1, 2, 3)], outs, ring + twin)
+    ring[2], first = after(ring[2], outs[0])
+    twin += [None, swap_seq(ring[2], 1), None]
+    outs = finish(meta, [(ring[2], 0, 2, 0)], (first, outs[1]))
+    ring[1], ring[3], *outs = after(ring[1], ring[3], *outs)
+    twin[1], twin[3] = swap_seq(ring[1], 1), swap_seq(ring[3], 1)
+    outs = finish(meta, [(ring[1], 0, 1, 0), (ring[3], 0, 3, 0), (twin[2], 1, 2, 0)], outs)
+    return finish(meta, [(twin[1], 1, 1, 0), (twin[3], 1, 3, 0)], outs, ring + twin)
 
 
 def position_table():
@@ -834,12 +840,15 @@
         smem=1, name="key_backward",
         scratch=[pltpu.VMEM((T, D), F32), pltpu.VMEM((T, D), F32)],
     )
+    left = call(
+        left_kernel, [((2, D, 2 * T), BF)],
+        meta, normed, norm_b, att, att_b, smem=1, name="left",
+    )[0]
+    other, left = after(swap_seq(sent, 1), left)
     keep, *sends = call(
         weight_grad_kernel,
         [((D, WIDE), F32)] + [((D, WIDE), BF)] * 3,
-        meta, own, swap_seq(sent, 1), normed, norm_b, att, att_b,
-        smem=1, name="weight_grad",
-        scratch=[pltpu.VMEM((2, D, 2 * T), BF)],
+        meta, own, other, left, smem=1, name="weight_grad",
     )
     d_tokens, ext = call(
         token_grad_kernel,

time: 144 us -> 139 us (0.965)
  waiting for transfers between devices: 54.1 us -> 47.6 us
    ppermute x15, waiting for transfers between devices: 40.6 us -> 36.8 us  [hop(): return lax.ppermute(block, AXES, ring_route(stage, d))]
    ppermute x17, waiting for transfers between devices: 5.77 us -> 4.05 us  [swap_seq(): return lax.ppermute(block, 'seq', [(i, i ^ code) for i in range(16)])]
    ppermute x17, starting transfers between devices: 20.1 us -> 18.4 us  [swap_seq(): return lax.ppermute(block, 'seq', [(i, i ^ code) for i in range(16)])]
    pallas_call x3 -> x4, Pallas kernels: 7.48 us -> 8.72 us  [finish(): pl.pallas_call(functools.partial(finish_kernel, marks=marks, first=first,...]
    pallas_call x16 -> x17, Pallas kernels: 37.1 us -> 37.2 us  [call(): pl.pallas_call(kernel, grid=(1,) if windows else (), out_shape=[jax.Shape...]
  transfers between devices with their start and end apart: 38 -> 38, of which waited for: 28 -> 27; matrix products, arithmetic and copies ran while one was open for 1% -> 1% of each run, Pallas kernels for 17% -> 20%
where the time goes in v4:
time: 139 us
  waiting for transfers between devices  47.6 us (34%)
  Pallas kernels  45.9 us (33%)
  starting transfers between devices  41.4 us (30%)
  local copies, waits for them, and re-layouts  2.97 us (2%)
    pallas_call x17, Pallas kernels, call(): pl.pallas_call(kernel, grid=(1,) if windows else (), out_shape=[jax.Shape...  37.2 us
    ppermute x15, waiting for transfers between devices, hop(): return lax.ppermute(block, AXES, ring_route(stage, d))  36.8 us
    ppermute x17, starting transfers between devices, swap_seq(): return lax.ppermute(block, 'seq', [(i, i ^ code) for i in range(16)])  18.4 us
    ppermute x15, starting transfers between devices, hop(): return lax.ppermute(block, AXES, ring_route(stage, d))  16.8 us
    pallas_call x4, Pallas kernels, finish(): pl.pallas_call(functools.partial(finish_kernel, marks=marks, first=first,...  8.72 us
    ppermute x6, waiting for transfers between devices, shift(): lax.ppermute(block, 'seq', [(i, (i + 4 * d) % 16) for i in range(16)])  6.67 us
    ppermute x6, starting transfers between devices, shift(): lax.ppermute(block, 'seq', [(i, (i + 4 * d) % 16) for i in range(16)])  6.23 us
    ppermute x17, waiting for transfers between devices, swap_seq(): return lax.ppermute(block, 'seq', [(i, i ^ code) for i in range(16)])  4.05 us
  transfers between devices with their start and end apart: 38, of which 27 were waited for; matrix products, arithmetic and copies ran while one was open for 1% of the time, Pallas kernels for 20%

profile of v4, /device:TPU:1, one launch (start us, length us, event | category | flops | bytes accessed | tf_op | source)
XLA Modules:
  0.0 139.0 jit_solution(16346971121367720065)
XLA Ops:
  0.6 4.9 %keys.1 = (f32[256,768]{1,0:T(8,128)}, bf16[256,768]{1,0:T(8,128)(2,1)}, bf16[256,1536]{1,0:T(8,128)(2,1)}, bf16[80,1536]{1,0:T(8,128)(2,1)}) custom-call(bf16[256,768]{1,0:T(8,128)(2,1)} %bitcast.13, s32[2,256]{1,0:T(2,128)} %bitcast.15, bf16[256,1152]{1,0:T(8,128)(2,1)} %constant.18.clone.table_h, f32[768]{0:T(1024)} %gain.3, f32[768]{0:T(1024)} %bias.1, ...), custom_call_target="tpu_custom_call" | custom-call | tf_op jit(solution)/shard_map/keys/pallas_call | solution.py:652
  7.1 3.0 %collective-permute-start = (bf16[80,1536]{1,0:T(8,128)(2,1)}, bf16[80,1536]{1,0:T(8,128)(2,1)S(1)}, u32[]{:S(2)}, u32[]{:S(2)}) collective-permute-start(bf16[80,1536]{1,0:T(8,128)(2,1)} %get-tuple-element.85), channel_id=1, source_target_pairs={{0,2},{1,3},{2,0},{3,1},{4,6},{5,7},{6,4},{7,5},{8,10},{9,11},{10,... | collective-permute-start | bytes 737288 | tf_op jit(solution)/shard_map/ppermute | solution.py:665
  11.9 3.8 %queries.1 = (bf16[256,768]{1,0:T(8,128)(2,1)}, bf16[256,768]{1,0:T(8,128)(2,1)}, bf16[256,768]{1,0:T(8,128)(2,1)}, bf16[80,1536]{1,0:T(8,128)(2,1)}) custom-call(bf16[256,768]{1,0:T(8,128)(2,1)} %get-tuple-element.86.normed.norm_a, bf16[768,2304]{1,0:T(8,128)(2,1)} %w_qkv.3, bf16[768,768]{1,0:T(8,128)(2,1)} %w_out.3, bf16[256,768]{1,0:T(8,128)(2,1)} %bitcast.14), custom_call_target="tpu_custom_call" | custom-call | tf_op jit(solution)/shard_map/queries/pallas_call | solution.py:652
  17.4 3.8 %collective-permute-start.4 = (bf16[32,1536]{1,0:T(8,128)(2,1)S(1)}, bf16[32,1536]{1,0:T(8,128)(2,1)S(1)}, u32[]{:S(2)}, u32[]{:S(2)}) collective-permute-start(bf16[32,1536]{1,0:T(8,128)(2,1)S(1)} %pad_maximum_fusion.3), channel_id=1, source_target_pairs={{0,12},{1,13},{2,14},{3,15},{4,0},{5,1},{6,2},{7,3},{8,4},{9,5},{1... | collective-permute-start | bytes 294920 | tf_op jit(solution)/shard_map/ppermute | solution.py:670
  23.0 1.8 %local_forward.3 = (f32[256,384]{1,0:T(8,128)S(1)}, f32[256,128]{1,0:T(8,128)S(1)}, f32[256,128]{1,0:T(8,128)S(1)}) custom-call(s32[16]{0:T(128)S(1)} %concatenate.15.meta, bf16[256,768]{1,0:T(8,128)(2,1)S(1)} %copy-done.2, bf16[256,1536]{1,0:T(8,128)(2,1)S(1)} %copy-done.1), custom_call_target="tpu_custom_call" | custom-call | tf_op jit(solution)/shard_map/local_forward/pallas_call | solution.py:652
  24.8 1.8 %local_forward.2 = (f32[256,384]{1,0:T(8,128)S(1)}, f32[256,128]{1,0:T(8,128)S(1)}, f32[256,128]{1,0:T(8,128)S(1)}) custom-call(s32[16]{0:T(128)S(1)} %concatenate.15.meta, bf16[256,768]{1,0:T(8,128)(2,1)S(1)} %copy-done.2, bf16[256,1536]{1,0:T(8,128)(2,1)S(1)} %copy-done.1), custom_call_target="tpu_custom_call" | custom-call | tf_op jit(solution)/shard_map/local_forward/pallas_call | solution.py:652
  26.8 2.2 %collective-permute-done.2.refs_1_ = bf16[32,1536]{1,0:T(8,128)(2,1)S(1)} collective-permute-done((bf16[32,1536]{1,0:T(8,128)(2,1)S(1)}, bf16[32,1536]{1,0:T(8,128)(2,1)S(1)}, u32[]{:S(2)}, u32[]{:S(2)}) %collective-permute-start.2) | collective-permute-done | bytes 98336 | tf_op jit(solution)/shard_map/ppermute | solution.py:670
  31.2 3.4 %remote_forward.1 = (bf16[256,768]{1,0:T(8,128)(2,1)S(1)}, f32[256,128]{1,0:T(8,128)S(1)}, bf16[80,1664]{1,0:T(8,128)(2,1)S(1)}) custom-call(s32[16]{0:T(128)S(1)} %concatenate.15.meta, bf16[256,768]{1,0:T(8,128)(2,1)S(1)} %copy-done.2, bf16[160,1536]{1,0:T(8,128)(2,1)S(1)} %pad_maximum_fusion.1.refs_0_, ...), custom_call_target="tpu_custom_call" | custom-call | tf_op jit(solution)/shard_map/remote_forward/pallas_call | solution.py:652
  35.1 2.9 %collective-permute-start.9 = (bf16[80,1664]{1,0:T(8,128)(2,1)S(1)}, bf16[80,1664]{1,0:T(8,128)(2,1)S(1)}, u32[]{:S(2)}, u32[]{:S(2)}) collective-permute-start(bf16[80,1664]{1,0:T(8,128)(2,1)S(1)} %get-tuple-element.106), channel_id=1, source_target_pairs={{0,2},{1,3},{2,0},{3,1},{4,6},{5,7},{6,4},{7,5},{8,10},{9,11},{10,... | collective-permute-start | bytes 798728 | tf_op jit(solution)/shard_map/ppermute | solution.py:665
  38.0 3.2 %local_backward.2 = (f32[256,384]{1,0:T(8,128)S(1)}, f32[256,384]{1,0:T(8,128)S(1)}, f32[256,384]{1,0:T(8,128)S(1)}) custom-call(s32[16]{0:T(128)S(1)} %concatenate.15.meta, bf16[256,768]{1,0:T(8,128)(2,1)S(1)} %copy-done.2, bf16[256,1536]{1,0:T(8,128)(2,1)S(1)} %copy-done.1, bf16[256,768]{1,0:T(8,128)(2,1)S(1)} %copy-done.3, ...), custom_call_target="tpu_custom_call" | custom-call | tf_op jit(solution)/shard_map/local_backward/pallas_call | solution.py:652
  41.2 2.3 %query_backward.1.refs_8_ = f32[256,768]{1,0:T(8,128)S(1)} custom-call(s32[16]{0:T(128)S(1)} %concatenate.15.meta, bf16[256,768]{1,0:T(8,128)(2,1)S(1)} %copy-done.2, bf16[256,768]{1,0:T(8,128)(2,1)S(1)} %copy-done.3, f32[256,128]{1,0:T(8,128)S(1)} %get-tuple-element.107.stat, bf16[160,1536]{1,0:T(8,128)(2,1)S(1)} %pad_maximum_fusion.1.refs_0_, ...), custom_call_target="tpu_custom_call" | custom-call | tf_op jit(solution)/shard_map/query_backward/pallas_call | solution.py:652
  47.2 3.2 %local_backward.3 = (f32[256,384]{1,0:T(8,128)S(1)}, f32[256,384]{1,0:T(8,128)S(1)}, f32[256,384]{1,0:T(8,128)S(1)}) custom-call(s32[16]{0:T(128)S(1)} %concatenate.15.meta, bf16[256,768]{1,0:T(8,128)(2,1)S(1)} %copy-done.2, bf16[256,1536]{1,0:T(8,128)(2,1)S(1)} %copy-done.1, bf16[256,768]{1,0:T(8,128)(2,1)S(1)} %copy-done.3, ...), custom_call_target="tpu_custom_call" | custom-call | tf_op jit(solution)/shard_map/local_backward/pallas_call | solution.py:652
  51.9 2.9 %collective-permute-done.11.refs_1_ = bf16[32,1664]{1,0:T(8,128)(2,1)S(1)} collective-permute-done((bf16[32,1664]{1,0:T(8,128)(2,1)S(1)}, bf16[32,1664]{1,0:T(8,128)(2,1)S(1)}, u32[]{:S(2)}, u32[]{:S(2)}) %collective-permute-start.11) | collective-permute-done | bytes 106528 | tf_op jit(solution)/shard_map/ppermute | solution.py:670
  56.8 2.9 %key_backward.1 = (bf16[256,2304]{1,0:T(8,128)(2,1)S(1)}, bf16[256,1536]{1,0:T(8,128)(2,1)S(1)}, bf16[256,1536]{1,0:T(8,128)(2,1)S(1)}) custom-call(s32[16]{0:T(128)S(1)} %concatenate.15.meta, bf16[256,1536]{1,0:T(8,128)(2,1)S(1)} %copy-done.1, bf16[160,1664]{1,0:T(8,128)(2,1)S(1)} %pad_maximum_fusion.refs_0_, ...), custom_call_target="tpu_custom_call" | custom-call | tf_op jit(solution)/shard_map/key_backward/pallas_call | solution.py:652
  62.2 2.3 %weight_grad.1 = (f32[768,384]{1,0:T(8,128)S(1)}, bf16[768,384]{1,0:T(8,128)(2,1)S(1)}, bf16[768,384]{1,0:T(8,128)(2,1)S(1)}, bf16[768,384]{1,0:T(8,128)(2,1)S(1)}) custom-call(s32[16]{0:T(128)S(1)} %concatenate.15.meta, bf16[256,1536]{1,0:T(8,128)(2,1)S(1)} %get-tuple-element.126.own, bf16[256,1536]{1,0:T(8,128)(2,1)S(1)} %collective-permute-done.18.other, ...), custom_call_target="tpu_custom_call" | custom-call | tf_op jit(solution)/shard_map/weight_grad/pallas_call | solution.py:652
  65.9 2.6 %collective-permute-start.20 = (bf16[768,384]{1,0:T(8,128)(2,1)S(1)}, bf16[768,384]{1,0:T(8,128)(2,1)S(1)}, u32[]{:S(2)}, u32[]{:S(2)}) collective-permute-start(bf16[768,384]{1,0:T(8,128)(2,1)S(1)} %get-tuple-element.138), channel_id=1, source_target_pairs={{0,64},{1,3},{2,66},{3,1},{4,68},{5,7},{6,70},{7,5},{8,72},{9,11},... | collective-permute-start | bytes 1769480 | tf_op jit(solution)/shard_map/ppermute | solution.py:704
  69.6 2.5 %token_grad.1 = (bf16[256,768]{1,0:T(8,128)(2,1)}, bf16[16,384]{1,0:T(8,128)(2,1)S(1)}) custom-call(bf16[256,2304]{1,0:T(8,128)(2,1)S(1)} %get-tuple-element.135.d_qkv, bf16[768,2304]{1,0:T(8,128)(2,1)S(1)} %copy-done, f32[256,768]{1,0:T(8,128)S(1)} %copy-done.5, f32[768]{0:T(1024)S(1)} %copy-done.9, bf16[256,768]{1,0:T(8,128)(2,1)S(1)} %copy-done.6), custom_call_target="tpu_custom_call" | custom-call | tf_op jit(solution)/shard_map/token_grad/pallas_call | solution.py:652
  74.9 7.5 %collective-permute-done.20.r2 = bf16[768,384]{1,0:T(8,128)(2,1)S(1)} collective-permute-done((bf16[768,384]{1,0:T(8,128)(2,1)S(1)}, bf16[768,384]{1,0:T(8,128)(2,1)S(1)}, u32[]{:S(2)}, u32[]{:S(2)}) %collective-permute-start.20) | collective-permute-done | bytes 589856 | tf_op jit(solution)/shard_map/ppermute | solution.py:704
  86.4 3.9 %collective-permute-done.22.r1 = bf16[208,384]{1,0:T(8,128)(2,1)S(1)} collective-permute-done((bf16[208,384]{1,0:T(8,128)(2,1)S(1)}, bf16[208,384]{1,0:T(8,128)(2,1)S(1)}, u32[]{:S(2)}, u32[]{:S(2)}) %collective-permute-start.22) | collective-permute-done | bytes 159776 | tf_op jit(solution)/shard_map/ppermute | solution.py:704
  91.6 2.3 %collective-permute-start.27 = (bf16[208,384]{1,0:T(8,128)(2,1)S(1)}, bf16[208,384]{1,0:T(8,128)(2,1)S(1)}, u32[]{:S(2)}, u32[]{:S(2)}) collective-permute-start(bf16[208,384]{1,0:T(8,128)(2,1)S(1)} %add_b.1.own), channel_id=1, source_target_pairs={{0,12},{1,97},{2,14},{3,99},{4,0},{5,101},{6,2},{7,103},{8,4},{9,1... | collective-permute-start | bytes 479240 | tf_op jit(solution)/shard_map/ppermute | solution.py:704
  94.9 2.8 %collective-permute-done.27.r3 = bf16[208,384]{1,0:T(8,128)(2,1)S(1)} collective-permute-done((bf16[208,384]{1,0:T(8,128)(2,1)S(1)}, bf16[208,384]{1,0:T(8,128)(2,1)S(1)}, u32[]{:S(2)}, u32[]{:S(2)}) %collective-permute-start.27) | collective-permute-done | bytes 159776 | tf_op jit(solution)/shard_map/ppermute | solution.py:704
  97.7 1.8 %collective-permute-done.26.r2 = bf16[208,384]{1,0:T(8,128)(2,1)S(1)} collective-permute-done((bf16[208,384]{1,0:T(8,128)(2,1)S(1)}, bf16[208,384]{1,0:T(8,128)(2,1)S(1)}, u32[]{:S(2)}, u32[]{:S(2)}) %collective-permute-start.26) | collective-permute-done | bytes 159776 | tf_op jit(solution)/shard_map/ppermute | solution.py:704
  99.5 1.9 %collective-permute-done.25.r1 = bf16[208,384]{1,0:T(8,128)(2,1)S(1)} collective-permute-done((bf16[208,384]{1,0:T(8,128)(2,1)S(1)}, bf16[208,384]{1,0:T(8,128)(2,1)S(1)}, u32[]{:S(2)}, u32[]{:S(2)}) %collective-permute-start.25) | collective-permute-done | bytes 159776 | tf_op jit(solution)/shard_map/ppermute | solution.py:704
  101.6 2.5 %collective-permute-start.30 = (bf16[208,384]{1,0:T(8,128)(2,1)S(1)}, bf16[208,384]{1,0:T(8,128)(2,1)S(1)}, u32[]{:S(2)}, u32[]{:S(2)}) collective-permute-start(bf16[208,384]{1,0:T(8,128)(2,1)S(1)} %add_c.1.own), channel_id=1, source_target_pairs={{0,18},{1,13},{2,16},{3,15},{4,22},{5,1},{6,20},{7,3},{8,26},{9,5}... | collective-permute-start | bytes 479240 | tf_op jit(solution)/shard_map/ppermute | solution.py:704
  104.7 3.3 %collective-permute-done.30.r3 = bf16[208,384]{1,0:T(8,128)(2,1)S(1)} collective-permute-done((bf16[208,384]{1,0:T(8,128)(2,1)S(1)}, bf16[208,384]{1,0:T(8,128)(2,1)S(1)}, u32[]{:S(2)}, u32[]{:S(2)}) %collective-permute-start.30) | collective-permute-done | bytes 159776 | tf_op jit(solution)/shard_map/ppermute | solution.py:704
  107.9 1.8 %collective-permute-done.29.r2 = bf16[208,384]{1,0:T(8,128)(2,1)S(1)} collective-permute-done((bf16[208,384]{1,0:T(8,128)(2,1)S(1)}, bf16[208,384]{1,0:T(8,128)(2,1)S(1)}, u32[]{:S(2)}, u32[]{:S(2)}) %collective-permute-start.29) | collective-permute-done | bytes 159776 | tf_op jit(solution)/shard_map/ppermute | solution.py:704
  112.0 3.7 %collective-permute-start.34 = (bf16[784,384]{1,0:T(8,128)(2,1)S(1)}, bf16[784,384]{1,0:T(8,128)(2,1)S(1)}, u32[]{:S(2)}, u32[]{:S(2)}) collective-permute-start(bf16[784,384]{1,0:T(8,128)(2,1)S(1)} %merge_b.1.refs_0_.refs_2_), channel_id=1, source_target_pairs={{0,1},{1,0},{2,3},{3,2},{4,5},{5,4},{6,7},{7,6},{8,9},{9,8},{10,11... | collective-permute-start | bytes 1806344 | tf_op jit(solution)/shard_map/ppermute | solution.py:665
  117.7 2.0 %finish.4 = (f32[768,2304]{1,0:T(8,128)}, f32[768,768]{1,0:T(8,128)}) custom-call(s32[16]{0:T(128)S(1)} %concatenate.15.meta, bf16[784,384]{1,0:T(8,128)(2,1)S(1)} %merge_b.1.refs_0_.refs_2_, bf16[784,384]{1,0:T(8,128)(2,1)S(1)} %collective-permute-done.34.refs_1_.refs_6_), custom_call_target="tpu_custom_call" | custom-call | tf_op jit(solution)/shard_map/finish/pallas_call | solution.py:631
  119.7 6.6 %collective-permute-done.33.refs_0_.refs_4_ = bf16[784,384]{1,0:T(8,128)(2,1)S(1)} collective-permute-done((bf16[784,384]{1,0:T(8,128)(2,1)S(1)}, bf16[784,384]{1,0:T(8,128)(2,1)S(1)}, u32[]{:S(2)}, u32[]{:S(2)}) %collective-permute-start.33) | collective-permute-done | bytes 602144 | tf_op jit(solution)/shard_map/ppermute | solution.py:704
  130.7 2.1 %collective-permute-done.31.refs_0_.refs_3_ = bf16[784,384]{1,0:T(8,128)(2,1)S(1)} collective-permute-done((bf16[784,384]{1,0:T(8,128)(2,1)S(1)}, bf16[784,384]{1,0:T(8,128)(2,1)S(1)}, u32[]{:S(2)}, u32[]{:S(2)}) %collective-permute-start.31) | collective-permute-done | bytes 602144 | tf_op jit(solution)/shard_map/ppermute | solution.py:704
  133.7 2.4 %finish.6 = (f32[768,2304]{1,0:T(8,128)}, f32[768,768]{1,0:T(8,128)}) custom-call(s32[16]{0:T(128)S(1)} %concatenate.15.meta, bf16[784,384]{1,0:T(8,128)(2,1)S(1)} %collective-permute-done.31.refs_0_.refs_3_, bf16[784,384]{1,0:T(8,128)(2,1)S(1)} %collective-permute-done.32.refs_1_.refs_5_, ...), custom_call_target="tpu_custom_call", output_to_operand_aliasing={{0}: (4, {}), {1}: (5, {})} | custom-call | tf_op jit(solution)/shard_map/finish/pallas_call | solution.py:631
  136.2 2.6 %finish.7 = (f32[768,2304]{1,0:T(8,128)}, f32[768,768]{1,0:T(8,128)}, f32[768]{0:T(1024)}, f32[768]{0:T(1024)}) custom-call(s32[16]{0:T(128)S(1)} %concatenate.15.meta, bf16[784,384]{1,0:T(8,128)(2,1)S(1)} %collective-permute-done.35.refs_0_.refs_7_, ...), custom_call_target="tpu_custom_call", output_to_operand_aliasing={{0}: (11, {}), {1}: (12, {})} | custom-call | tf_op jit(solution)/shard_map/finish/pallas_call | solution.py:631
  (101 shorter events, 41.1 us)
Async XLA Ops:
  5.6 10.8 %collective-permute-start.1 = (bf16[256,768]{1,0:T(8,128)(2,1)}, bf16[256,768]{1,0:T(8,128)(2,1)S(1)}, u32[]{:S(2)}, u32[]{:S(2)}) collective-permute-start(bf16[256,768]{1,0:T(8,128)(2,1)} %get-tuple-element.86.normed.norm_a), channel_id=1, source_target_pairs={{0,1},{1,0},{2,3},{3,2},{4,5},{5,4},{6,7},{7,6},{8,9},{9,8},{10,11... | collective-permute-start | bytes 1179656 | tf_op jit(solution)/shard_map/ppermute | solution.py:665
  7.1 9.3 %collective-permute-start = (bf16[80,1536]{1,0:T(8,128)(2,1)}, bf16[80,1536]{1,0:T(8,128)(2,1)S(1)}, u32[]{:S(2)}, u32[]{:S(2)}) collective-permute-start(bf16[80,1536]{1,0:T(8,128)(2,1)} %get-tuple-element.85), channel_id=1, source_target_pairs={{0,2},{1,3},{2,0},{3,1},{4,6},{5,7},{6,4},{7,5},{8,10},{9,11},{10,... | collective-permute-start | bytes 737288 | tf_op jit(solution)/shard_map/ppermute | solution.py:665
  16.5 12.5 %collective-permute-start.5 = (bf16[160,1536]{1,0:T(8,128)(2,1)S(1)}, bf16[160,1536]{1,0:T(8,128)(2,1)S(1)}, u32[]{:S(2)}, u32[]{:S(2)}) collective-permute-start(bf16[160,1536]{1,0:T(8,128)(2,1)S(1)} %pad_maximum_fusion.1.refs_0_), channel_id=1, source_target_pairs={{0,1},{1,0},{2,3},{3,2},{4,5},{5,4},{6,7},{7,6},{8,9},{9,8},{10,11... | collective-permute-start | bytes 1474568 | tf_op jit(solution)/shard_map/ppermute | solution.py:665
  17.4 9.3 %collective-permute-start.4 = (bf16[32,1536]{1,0:T(8,128)(2,1)S(1)}, bf16[32,1536]{1,0:T(8,128)(2,1)S(1)}, u32[]{:S(2)}, u32[]{:S(2)}) collective-permute-start(bf16[32,1536]{1,0:T(8,128)(2,1)S(1)} %pad_maximum_fusion.3), channel_id=1, source_target_pairs={{0,12},{1,13},{2,14},{3,15},{4,0},{5,1},{6,2},{7,3},{8,4},{9,5},{1... | collective-permute-start | bytes 294920 | tf_op jit(solution)/shard_map/ppermute | solution.py:670
  21.2 5.6 %collective-permute-start.3 = (bf16[32,1536]{1,0:T(8,128)(2,1)S(1)}, bf16[32,1536]{1,0:T(8,128)(2,1)S(1)}, u32[]{:S(2)}, u32[]{:S(2)}) collective-permute-start(bf16[32,1536]{1,0:T(8,128)(2,1)S(1)} %pad_maximum_fusion.3), channel_id=1, source_target_pairs={{0,8},{1,9},{2,10},{3,11},{4,12},{5,13},{6,14},{7,15},{8,0},{9,1},... | collective-permute-start | bytes 294920 | tf_op jit(solution)/shard_map/ppermute | solution.py:670
  21.2 7.8 %collective-permute-start.2 = (bf16[32,1536]{1,0:T(8,128)(2,1)S(1)}, bf16[32,1536]{1,0:T(8,128)(2,1)S(1)}, u32[]{:S(2)}, u32[]{:S(2)}) collective-permute-start(bf16[32,1536]{1,0:T(8,128)(2,1)S(1)} %pad_maximum_fusion.3), channel_id=1, source_target_pairs={{0,4},{1,5},{2,6},{3,7},{4,8},{5,9},{6,10},{7,11},{8,12},{9,13},{1... | collective-permute-start | bytes 294920 | tf_op jit(solution)/shard_map/ppermute | solution.py:670
  34.6 9.7 %collective-permute-start.10 = (bf16[256,768]{1,0:T(8,128)(2,1)S(1)}, bf16[256,768]{1,0:T(8,128)(2,1)S(1)}, u32[]{:S(2)}, u32[]{:S(2)}) collective-permute-start(bf16[256,768]{1,0:T(8,128)(2,1)S(1)} %get-tuple-element.133.att_a.att), channel_id=1, source_target_pairs={{0,1},{1,0},{2,3},{3,2},{4,5},{5,4},{6,7},{7,6},{8,9},{9,8},{10,11... | collective-permute-start | bytes 1179656 | tf_op jit(solution)/shard_map/ppermute | solution.py:665
  35.1 9.2 %collective-permute-start.9 = (bf16[80,1664]{1,0:T(8,128)(2,1)S(1)}, bf16[80,1664]{1,0:T(8,128)(2,1)S(1)}, u32[]{:S(2)}, u32[]{:S(2)}) collective-permute-start(bf16[80,1664]{1,0:T(8,128)(2,1)S(1)} %get-tuple-element.106), channel_id=1, source_target_pairs={{0,2},{1,3},{2,0},{3,1},{4,6},{5,7},{6,4},{7,5},{8,10},{9,11},{10,... | collective-permute-start | bytes 798728 | tf_op jit(solution)/shard_map/ppermute | solution.py:665
  44.4 10.4 %collective-permute-start.14 = (bf16[160,1664]{1,0:T(8,128)(2,1)S(1)}, bf16[160,1664]{1,0:T(8,128)(2,1)S(1)}, u32[]{:S(2)}, u32[]{:S(2)}) collective-permute-start(bf16[160,1664]{1,0:T(8,128)(2,1)S(1)} %pad_maximum_fusion.refs_0_), channel_id=1, source_target_pairs={{0,1},{1,0},{2,3},{3,2},{4,5},{5,4},{6,7},{7,6},{8,9},{9,8},{10,11... | collective-permute-start | bytes 1597448 | tf_op jit(solution)/shard_map/ppermute | solution.py:665
  45.6 4.9 %collective-permute-start.13 = (bf16[32,1664]{1,0:T(8,128)(2,1)S(1)}, bf16[32,1664]{1,0:T(8,128)(2,1)S(1)}, u32[]{:S(2)}, u32[]{:S(2)}) collective-permute-start(bf16[32,1664]{1,0:T(8,128)(2,1)S(1)} %pad_maximum_fusion.2), channel_id=1, source_target_pairs={{0,12},{1,13},{2,14},{3,15},{4,0},{5,1},{6,2},{7,3},{8,4},{9,5},{1... | collective-permute-start | bytes 319496 | tf_op jit(solution)/shard_map/ppermute | solution.py:670
  46.2 5.7 %collective-permute-start.12 = (bf16[32,1664]{1,0:T(8,128)(2,1)S(1)}, bf16[32,1664]{1,0:T(8,128)(2,1)S(1)}, u32[]{:S(2)}, u32[]{:S(2)}) collective-permute-start(bf16[32,1664]{1,0:T(8,128)(2,1)S(1)} %pad_maximum_fusion.2), channel_id=1, source_target_pairs={{0,8},{1,9},{2,10},{3,11},{4,12},{5,13},{6,14},{7,15},{8,0},{9,1},... | collective-permute-start | bytes 319496 | tf_op jit(solution)/shard_map/ppermute | solution.py:670
  47.2 7.5 %collective-permute-start.11 = (bf16[32,1664]{1,0:T(8,128)(2,1)S(1)}, bf16[32,1664]{1,0:T(8,128)(2,1)S(1)}, u32[]{:S(2)}, u32[]{:S(2)}) collective-permute-start(bf16[32,1664]{1,0:T(8,128)(2,1)S(1)} %pad_maximum_fusion.2), channel_id=1, source_target_pairs={{0,4},{1,5},{2,6},{3,7},{4,8},{5,9},{6,10},{7,11},{8,12},{9,13},{1... | collective-permute-start | bytes 319496 | tf_op jit(solution)/shard_map/ppermute | solution.py:670
  59.8 2.4 %collective-permute-start.18 = (bf16[256,1536]{1,0:T(8,128)(2,1)S(1)}, bf16[256,1536]{1,0:T(8,128)(2,1)S(1)}, u32[]{:S(2)}, u32[]{:S(2)}) collective-permute-start(bf16[256,1536]{1,0:T(8,128)(2,1)S(1)} %get-tuple-element.127), channel_id=1, source_target_pairs={{0,1},{1,0},{2,3},{3,2},{4,5},{5,4},{6,7},{7,6},{8,9},{9,8},{10,11... | collective-permute-start | bytes 2359304 | tf_op jit(solution)/shard_map/ppermute | solution.py:665
  64.5 10.4 %collective-permute-start.19 = (bf16[768,384]{1,0:T(8,128)(2,1)S(1)}, bf16[768,384]{1,0:T(8,128)(2,1)S(1)}, u32[]{:S(2)}, u32[]{:S(2)}) collective-permute-start(bf16[768,384]{1,0:T(8,128)(2,1)S(1)} %get-tuple-element.137), channel_id=1, source_target_pairs={{0,32},{1,17},{2,34},{3,19},{4,36},{5,21},{6,38},{7,23},{8,40},{9,... | collective-permute-start | bytes 1769480 | tf_op jit(solution)/shard_map/ppermute | solution.py:704
  65.9 16.5 %collective-permute-start.20 = (bf16[768,384]{1,0:T(8,128)(2,1)S(1)}, bf16[768,384]{1,0:T(8,128)(2,1)S(1)}, u32[]{:S(2)}, u32[]{:S(2)}) collective-permute-start(bf16[768,384]{1,0:T(8,128)(2,1)S(1)} %get-tuple-element.138), channel_id=1, source_target_pairs={{0,64},{1,3},{2,66},{3,1},{4,68},{5,7},{6,70},{7,5},{8,72},{9,11},... | collective-permute-start | bytes 1769480 | tf_op jit(solution)/shard_map/ppermute | solution.py:704
  68.5 13.9 %collective-permute-start.21 = (bf16[768,384]{1,0:T(8,128)(2,1)S(1)}, bf16[768,384]{1,0:T(8,128)(2,1)S(1)}, u32[]{:S(2)}, u32[]{:S(2)}) collective-permute-start(bf16[768,384]{1,0:T(8,128)(2,1)S(1)} %get-tuple-element.139), channel_id=1, source_target_pairs={{0,96},{1,19},{2,98},{3,17},{4,100},{5,23},{6,102},{7,21},{8,104},... | collective-permute-start | bytes 1769480 | tf_op jit(solution)/shard_map/ppermute | solution.py:704
  83.2 7.1 %collective-permute-start.22 = (bf16[208,384]{1,0:T(8,128)(2,1)S(1)}, bf16[208,384]{1,0:T(8,128)(2,1)S(1)}, u32[]{:S(2)}, u32[]{:S(2)}) collective-permute-start(bf16[208,384]{1,0:T(8,128)(2,1)S(1)} %get-tuple-element.145), channel_id=1, source_target_pairs={{0,16},{1,5},{2,18},{3,7},{4,20},{5,9},{6,22},{7,11},{8,24},{9,13}... | collective-permute-start | bytes 479240 | tf_op jit(solution)/shard_map/ppermute | solution.py:704
  83.3 7.0 %collective-permute-start.23 = (bf16[208,384]{1,0:T(8,128)(2,1)S(1)}, bf16[208,384]{1,0:T(8,128)(2,1)S(1)}, u32[]{:S(2)}, u32[]{:S(2)}) collective-permute-start(bf16[208,384]{1,0:T(8,128)(2,1)S(1)} %get-tuple-element.146), channel_id=1, source_target_pairs={{0,2},{1,9},{2,0},{3,11},{4,6},{5,13},{6,4},{7,15},{8,10},{9,1},{1... | collective-permute-start | bytes 479240 | tf_op jit(solution)/shard_map/ppermute | solution.py:704
  84.7 6.2 %collective-permute-start.24 = (bf16[208,384]{1,0:T(8,128)(2,1)S(1)}, bf16[208,384]{1,0:T(8,128)(2,1)S(1)}, u32[]{:S(2)}, u32[]{:S(2)}) collective-permute-start(bf16[208,384]{1,0:T(8,128)(2,1)S(1)} %get-tuple-element.147), channel_id=1, source_target_pairs={{0,18},{1,13},{2,16},{3,15},{4,22},{5,1},{6,20},{7,3},{8,26},{9,5}... | collective-permute-start | bytes 479240 | tf_op jit(solution)/shard_map/ppermute | solution.py:704
  91.6 6.2 %collective-permute-start.27 = (bf16[208,384]{1,0:T(8,128)(2,1)S(1)}, bf16[208,384]{1,0:T(8,128)(2,1)S(1)}, u32[]{:S(2)}, u32[]{:S(2)}) collective-permute-start(bf16[208,384]{1,0:T(8,128)(2,1)S(1)} %add_b.1.own), channel_id=1, source_target_pairs={{0,12},{1,97},{2,14},{3,99},{4,0},{5,101},{6,2},{7,103},{8,4},{9,1... | collective-permute-start | bytes 479240 | tf_op jit(solution)/shard_map/ppermute | solution.py:704
  93.8 5.7 %collective-permute-start.26 = (bf16[208,384]{1,0:T(8,128)(2,1)S(1)}, bf16[208,384]{1,0:T(8,128)(2,1)S(1)}, u32[]{:S(2)}, u32[]{:S(2)}) collective-permute-start(bf16[208,384]{1,0:T(8,128)(2,1)S(1)} %add_b.1.own), channel_id=1, source_target_pairs={{0,8},{1,65},{2,10},{3,67},{4,12},{5,69},{6,14},{7,71},{8,0},{9,73... | collective-permute-start | bytes 479240 | tf_op jit(solution)/shard_map/ppermute | solution.py:704
  94.4 7.0 %collective-permute-start.25 = (bf16[208,384]{1,0:T(8,128)(2,1)S(1)}, bf16[208,384]{1,0:T(8,128)(2,1)S(1)}, u32[]{:S(2)}, u32[]{:S(2)}) collective-permute-start(bf16[208,384]{1,0:T(8,128)(2,1)S(1)} %add_b.1.own), channel_id=1, source_target_pairs={{0,4},{1,33},{2,6},{3,35},{4,8},{5,37},{6,10},{7,39},{8,12},{9,41}... | collective-permute-start | bytes 479240 | tf_op jit(solution)/shard_map/ppermute | solution.py:704
  101.6 6.4 %collective-permute-start.30 = (bf16[208,384]{1,0:T(8,128)(2,1)S(1)}, bf16[208,384]{1,0:T(8,128)(2,1)S(1)}, u32[]{:S(2)}, u32[]{:S(2)}) collective-permute-start(bf16[208,384]{1,0:T(8,128)(2,1)S(1)} %add_c.1.own), channel_id=1, source_target_pairs={{0,18},{1,13},{2,16},{3,15},{4,22},{5,1},{6,20},{7,3},{8,26},{9,5}... | collective-permute-start | bytes 479240 | tf_op jit(solution)/shard_map/ppermute | solution.py:704
  104.0 5.7 %collective-permute-start.29 = (bf16[208,384]{1,0:T(8,128)(2,1)S(1)}, bf16[208,384]{1,0:T(8,128)(2,1)S(1)}, u32[]{:S(2)}, u32[]{:S(2)}) collective-permute-start(bf16[208,384]{1,0:T(8,128)(2,1)S(1)} %add_c.1.own), channel_id=1, source_target_pairs={{0,2},{1,9},{2,0},{3,11},{4,6},{5,13},{6,4},{7,15},{8,10},{9,1},{1... | collective-permute-start | bytes 479240 | tf_op jit(solution)/shard_map/ppermute | solution.py:704
  104.0 7.3 %collective-permute-start.28 = (bf16[208,384]{1,0:T(8,128)(2,1)S(1)}, bf16[208,384]{1,0:T(8,128)(2,1)S(1)}, u32[]{:S(2)}, u32[]{:S(2)}) collective-permute-start(bf16[208,384]{1,0:T(8,128)(2,1)S(1)} %add_c.1.own), channel_id=1, source_target_pairs={{0,16},{1,5},{2,18},{3,7},{4,20},{5,9},{6,22},{7,11},{8,24},{9,13}... | collective-permute-start | bytes 479240 | tf_op jit(solution)/shard_map/ppermute | solution.py:704
  112.0 5.7 %collective-permute-start.34 = (bf16[784,384]{1,0:T(8,128)(2,1)S(1)}, bf16[784,384]{1,0:T(8,128)(2,1)S(1)}, u32[]{:S(2)}, u32[]{:S(2)}) collective-permute-start(bf16[784,384]{1,0:T(8,128)(2,1)S(1)} %merge_b.1.refs_0_.refs_2_), channel_id=1, source_target_pairs={{0,1},{1,0},{2,3},{3,2},{4,5},{5,4},{6,7},{7,6},{8,9},{9,8},{10,11... | collective-permute-start | bytes 1806344 | tf_op jit(solution)/shard_map/ppermute | solution.py:665
  115.7 10.7 %collective-permute-start.33 = (bf16[784,384]{1,0:T(8,128)(2,1)S(1)}, bf16[784,384]{1,0:T(8,128)(2,1)S(1)}, u32[]{:S(2)}, u32[]{:S(2)}) collective-permute-start(bf16[784,384]{1,0:T(8,128)(2,1)S(1)} %merge_b.1.refs_0_.refs_2_), channel_id=1, source_target_pairs={{0,64},{1,3},{2,66},{3,1},{4,68},{5,7},{6,70},{7,5},{8,72},{9,11},... | collective-permute-start | bytes 1806344 | tf_op jit(solution)/shard_map/ppermute | solution.py:704
  116.2 14.5 %collective-permute-start.32 = (bf16[784,384]{1,0:T(8,128)(2,1)S(1)}, bf16[784,384]{1,0:T(8,128)(2,1)S(1)}, u32[]{:S(2)}, u32[]{:S(2)}) collective-permute-start(bf16[784,384]{1,0:T(8,128)(2,1)S(1)} %merge_b.1.refs_0_.refs_2_), channel_id=1, source_target_pairs={{0,96},{1,19},{2,98},{3,17},{4,100},{5,23},{6,102},{7,21},{8,104},... | collective-permute-start | bytes 1806344 | tf_op jit(solution)/shard_map/ppermute | solution.py:704
  117.1 15.7 %collective-permute-start.31 = (bf16[784,384]{1,0:T(8,128)(2,1)S(1)}, bf16[784,384]{1,0:T(8,128)(2,1)S(1)}, u32[]{:S(2)}, u32[]{:S(2)}) collective-permute-start(bf16[784,384]{1,0:T(8,128)(2,1)S(1)} %merge_b.1.refs_0_.refs_2_), channel_id=1, source_target_pairs={{0,32},{1,17},{2,34},{3,19},{4,36},{5,21},{6,38},{7,23},{8,40},{9,... | collective-permute-start | bytes 1806344 | tf_op jit(solution)/shard_map/ppermute | solution.py:704
  126.4 7.4 %collective-permute-start.37 = (bf16[784,384]{1,0:T(8,128)(2,1)S(1)}, bf16[784,384]{1,0:T(8,128)(2,1)S(1)}, u32[]{:S(2)}, u32[]{:S(2)}) collective-permute-start(bf16[784,384]{1,0:T(8,128)(2,1)S(1)} %collective-permute-done.33.refs_0_.refs_4_), channel_id=1, source_target_pairs={{0,1},{1,0},{2,3},{3,2},{4,5},{5,4},{6,7},{7,6},{8,9},{9,8},{10,11... | collective-permute-start | bytes 1806344 | tf_op jit(solution)/shard_map/ppermute | solution.py:665
  132.8 3.4 %collective-permute-start.35 = (bf16[784,384]{1,0:T(8,128)(2,1)S(1)}, bf16[784,384]{1,0:T(8,128)(2,1)S(1)}, u32[]{:S(2)}, u32[]{:S(2)}) collective-permute-start(bf16[784,384]{1,0:T(8,128)(2,1)S(1)} %collective-permute-done.31.refs_0_.refs_3_), channel_id=1, source_target_pairs={{0,1},{1,0},{2,3},{3,2},{4,5},{5,4},{6,7},{7,6},{8,9},{9,8},{10,11... | collective-permute-start | bytes 1806344 | tf_op jit(solution)/shard_map/ppermute | solution.py:665
  133.7 2.5 %collective-permute-start.36 = (bf16[784,384]{1,0:T(8,128)(2,1)S(1)}, bf16[784,384]{1,0:T(8,128)(2,1)S(1)}, u32[]{:S(2)}, u32[]{:S(2)}) collective-permute-start(bf16[784,384]{1,0:T(8,128)(2,1)S(1)} %collective-permute-done.32.refs_1_.refs_5_), channel_id=1, source_target_pairs={{0,1},{1,0},{2,3},{3,2},{4,5},{5,4},{6,7},{7,6},{8,9},{9,8},{10,11... | collective-permute-start | bytes 1806344 | tf_op jit(solution)/shard_map/ppermute | solution.py:665
  (17 other events, 105.6 us)

commit v5 on v4

--- a/solution.py
+++ b/solution.py
@@ -217,7 +217,8 @@
     return top, jnp.sum(shares, axis=1, keepdims=True), shares.astype(BF)
 
 
-def local_forward_kernel(meta, q_r, kv, o_o, top_o, sum_o, *, first):
+def local_forward_kernel(meta, q_r, kv, *refs, first):
+    o_o, top_o, sum_o = refs[-3:]
     bias = local_bias(meta)
     o_o[...] = jnp.zeros_like(o_o)
     lane = iota((T, 128), 1)
@@ -234,6 +235,27 @@
         o_o[:, s - base : s - base + w] += nn(shares, kv[:, D + s : D + s + w] * mask)
     top_o[...] = tops
     sum_o[...] = sums
+    if first:
+        mid_forward(meta, q_r, *refs[:-3])
+
+
+def mid_forward(meta, q_r, part, twin, mid_o, top_o, sum_o):
+    lane = iota((T, 128), 1)
+    row = iota((T, 128), 0)
+    got = (part, None, None, None, twin)
+    tops = jnp.full((T, 128), NEG, F32)
+    sums = jnp.zeros((T, 128), F32)
+    bias = mid_bias(meta)
+    for g in range(4):
+        s = group_window(g)
+        q = q_r[:, s : s + 256] * group_mask(g)
+        top, total, shares = soft(nt(q, mid_rows(got, s, 256)) * SCALE + bias)
+        here = lane == 4 * g + (row >> 6)
+        tops = jnp.where(here, top, tops)
+        sums = jnp.where(here, total, sums)
+        mid_o[g] = nn(shares, mid_rows(got, D + s, 256))
+    top_o[...] = tops
+    sum_o[...] = sums
 
 
 def mid_rows(got, lo, width):
@@ -263,25 +285,14 @@
 
 def remote_forward_kernel(meta, q_r, *refs):
     got = refs[:8]
-    o_1, top_1, sum_1, o_2, top_2, sum_2, d_att, pack, att_o, stat_o, send_o = refs[8:]
+    o_1, top_1, sum_1, mid_parts, top_m, sum_m, o_2, top_2, sum_2 = refs[8:17]
+    d_att, pack, att_o, stat_o, send_o = refs[17:]
     lane = iota((T, 128), 1)
     row = iota((T, 128), 0)
     top_l = jnp.where(lane < 8, top_1[...], top_2[...])
     sum_l = jnp.where(lane < 8, sum_1[...], sum_2[...])
-    tops_m = jnp.full((T, 128), NEG, F32)
-    sums_m = jnp.zeros((T, 128), F32)
-    mid = mid_bias(meta)
-    mid_parts = []
-    for g in range(4):
-        s = group_window(g)
-        mask = group_mask(g)
-        q = q_r[:, s : s + 256] * mask
-        scores = nt(q, mid_rows(got, s, 256)) * SCALE + mid
-        top, total, shares = soft(scores)
-        here = lane == 4 * g + (row >> 6)
-        tops_m = jnp.where(here, top, tops_m)
-        sums_m = jnp.where(here, total, sums_m)
-        mid_parts.append(nn(shares, mid_rows(got, D + s, 256)))
+    tops_m = top_m[...]
+    sums_m = sum_m[...]
     mask = far_mask()
     scores = nt(q_r[...] * mask, far_rows(got, 0, D)) * SCALE + far_bias(meta)
     top, total, shares = soft(scores)
@@ -353,7 +364,8 @@
     )
 
 
-def local_backward_kernel(meta, q_r, kv, d_att, stat, dq_o, dk_o, dv_o, *, first):
+def local_backward_kernel(meta, q_r, kv, d_att, stat, *refs, first):
+    dq_o, dk_o, dv_o = refs[-3:]
     bias = local_bias(meta)
     stat_t = stat[...].T
     dq_o[...] = jnp.zeros_like(dq_o)
@@ -374,6 +386,28 @@
         dk_o[:, t : t + w] += nn(ds, q)
         dv_o[:, t : t + w] += nn(shares.astype(BF), da)
         dq_o[:, t : t + w] += tn(ds, k)
+    if first:
+        mid_key_backward(meta, kv, *refs[:-3])
+
+
+def mid_key_backward(meta, kv, part, twin, dk_o, dv_o):
+    got = (part, None, None, None, twin)
+    stat_t = joined_stats(mid_rows(got, 2 * D, 128))
+    dk_o[...] = jnp.zeros_like(dk_o)
+    dv_o[...] = jnp.zeros_like(dv_o)
+    bias = mid_bias(meta)
+    for g in range(4):
+        s = group_window(g)
+        mask = group_mask(g)
+        mask_f = mask.astype(F32)
+        q = mid_rows(got, s, 256)
+        da = mid_rows(got, D + s, 256)
+        scores = nt(kv[:, s : s + 256] * mask, q) * SCALE + bias
+        shares = jnp.exp(scores - spread_mid(stat_t, 4 * g))
+        d_shares = nt(kv[:, D + s : D + s + 256] * mask, da)
+        ds = (shares * (d_shares - spread_mid(stat_t, HEADS + 4 * g))).astype(BF)
+        dk_o[:, s : s + 256] += nn(ds, q) * mask_f
+        dv_o[:, s : s + 256] += nn(shares.astype(BF), da) * mask_f
 
 
 def query_backward_kernel(meta, q_r, d_att, stat, *refs):
@@ -421,27 +455,10 @@
 
 def key_backward_kernel(meta, kv, *refs):
     got = refs[:8]
-    dq_r, dq_1, dk_1, dv_1, dq_2, dk_2, dv_2, cot = refs[8:16]
-    all_o, kept_o, sent_o, dk_s, dv_s = refs[16:]
-    half = D // 2
-    dk_s[:, :half] = dk_1[...]
-    dk_s[:, half:] = dk_2[...]
-    dv_s[:, :half] = dv_1[...]
-    dv_s[:, half:] = dv_2[...]
-    stat_t = joined_stats(mid_rows(got, 2 * D, 128))
-    mid = mid_bias(meta)
-    for g in range(4):
-        s = group_window(g)
-        mask = group_mask(g)
-        mask_f = mask.astype(F32)
-        q = mid_rows(got, s, 256)
-        da = mid_rows(got, D + s, 256)
-        scores = nt(kv[:, s : s + 256] * mask, q) * SCALE + mid
-        shares = jnp.exp(scores - spread_mid(stat_t, 4 * g))
-        d_shares = nt(kv[:, D + s : D + s + 256] * mask, da)
-        ds = (shares * (d_shares - spread_mid(stat_t, HEADS + 4 * g))).astype(BF)
-        dk_s[:, s : s + 256] += nn(ds, q) * mask_f
-        dv_s[:, s : s + 256] += nn(shares.astype(BF), da) * mask_f
+    dq_r, dq_1, dk_1, dv_1, dk_m, dv_m, dq_2, dk_2, dv_2, cot = refs[8:18]
+    all_o, kept_o, sent_o, dk_s, dv_s = refs[18:]
+    dk_s[...] = jnp.concatenate([dk_1[...], dk_2[...]], axis=1) + dk_m[...]
+    dv_s[...] = jnp.concatenate([dv_1[...], dv_2[...]], axis=1) + dv_m[...]
     stat_t = joined_stats(far_rows(got, 2 * D, 128))
     mask = far_mask()
     mask_f = mask.astype(F32)
@@ -793,20 +810,23 @@
     far, q = after(far, q)
     part = join(kv_pack[:64], from_y[:64], far)
     twin = swap_seq(part, 1)
-    tops = [
-        call(
-            functools.partial(local_forward_kernel, first=first),
-            [((T, D // 2), F32), ((T, 128), F32), ((T, 128), F32)],
-            meta, q, kv, smem=1, name="local_forward",
-        )
-        for first in (0, 8)
-    ]
-    *from_z, twin, _, _ = after(*from_z, twin, tops[0][0], tops[1][0])
+    stat_shape = ((T, 128), F32)
+    out_1 = call(
+        functools.partial(local_forward_kernel, first=0),
+        [((T, D // 2), F32), stat_shape, stat_shape],
+        meta, q, kv, smem=1, name="local_forward",
+    )
+    out_2 = call(
+        functools.partial(local_forward_kernel, first=8),
+        [((4, T, 256), F32), stat_shape, stat_shape, ((T, D // 2), F32), stat_shape, stat_shape],
+        meta, q, kv, part, twin, smem=1, name="local_forward",
+    )
+    *from_z, _, _ = after(*from_z, out_1[0], out_2[0])
     got_kv = (part, *from_z, twin, *[swap_seq(rows, 1) for rows in from_z])
     att, stat, pack = call(
         remote_forward_kernel,
         [((T, D), BF), ((T, 128), F32), ((80, 2 * D + 128), BF)],
-        meta, q, *got_kv, *tops[0], *tops[1], d_att, qd_pack,
+        meta, q, *got_kv, *out_1, *out_2, d_att, qd_pack,
         smem=1, name="remote_forward",
     )
     from_y = swap_seq(pack, 2)
@@ -828,10 +848,10 @@
     twin = swap_seq(part, 1)
     grads_2 = call(
         functools.partial(local_backward_kernel, first=8),
-        [((T, D // 2), F32)] * 3,
-        meta, q, kv, d_att, stat, smem=1, name="local_backward",
-    )
-    *from_z, twin, _ = after(*from_z, twin, grads_2[0])
+        [((T, D), F32)] * 2 + [((T, D // 2), F32)] * 3,
+        meta, q, kv, d_att, stat, part, twin, smem=1, name="local_backward",
+    )
+    *from_z, _ = after(*from_z, grads_2[0])
     got_qd = (part, *from_z, twin, *[swap_seq(rows, 1) for rows in from_z])
     d_qkv, own, sent = call(
         key_backward_kernel,

time: 139 us -> 138 us (level)
  waiting for transfers between devices: 47.6 us -> 44.6 us
  starting transfers between devices: 41.4 us -> 42.8 us
    ppermute x6, waiting for transfers between devices: 6.67 us -> 3.86 us  [shift(): lax.ppermute(block, 'seq', [(i, (i + 4 * d) % 16) for i in range(16)])]
  transfers between devices with their start and end apart: 38 -> 38, of which waited for: 27 -> 25; matrix products, arithmetic and copies ran while one was open for 1% -> 1% of each run, Pallas kernels for 20% -> 21%
where the time goes in v5:
time: 138 us
  Pallas kernels  45.9 us (33%)
  waiting for transfers between devices  44.6 us (32%)
  starting transfers between devices  42.8 us (31%)
  local copies, waits for them, and re-layouts  2.97 us (2%)
    pallas_call x17, Pallas kernels, call(): pl.pallas_call(kernel, grid=(1,) if windows else (), out_shape=[jax.Shape...  37.2 us
    ppermute x15, waiting for transfers between devices, hop(): return lax.ppermute(block, AXES, ring_route(stage, d))  36.7 us
    ppermute x17, starting transfers between devices, swap_seq(): return lax.ppermute(block, 'seq', [(i, i ^ code) for i in range(16)])  18.7 us
    ppermute x15, starting transfers between devices, hop(): return lax.ppermute(block, AXES, ring_route(stage, d))  17.2 us
    pallas_call x4, Pallas kernels, finish(): pl.pallas_call(functools.partial(finish_kernel, marks=marks, first=first,...  8.72 us
    ppermute x6, starting transfers between devices, shift(): lax.ppermute(block, 'seq', [(i, (i + 4 * d) % 16) for i in range(16)])  6.92 us
    ppermute x17, waiting for transfers between devices, swap_seq(): return lax.ppermute(block, 'seq', [(i, i ^ code) for i in range(16)])  4.03 us
    ppermute x6, waiting for transfers between devices, shift(): lax.ppermute(block, 'seq', [(i, (i + 4 * d) % 16) for i in range(16)])  3.86 us
  transfers between devices with their start and end apart: 38, of which 25 were waited for; matrix products, arithmetic and copies ran while one was open for 1% of the time, Pallas kernels for 21%

profile of v5, /device:TPU:1, one launch (start us, length us, event | category | flops | bytes accessed | tf_op | source)
XLA Modules:
  0.0 137.5 jit_solution(2537529637165925354)
XLA Ops:
  0.6 4.9 %keys.1 = (f32[256,768]{1,0:T(8,128)}, bf16[256,768]{1,0:T(8,128)(2,1)}, bf16[256,1536]{1,0:T(8,128)(2,1)}, bf16[80,1536]{1,0:T(8,128)(2,1)}) custom-call(bf16[256,768]{1,0:T(8,128)(2,1)} %bitcast.13, s32[2,256]{1,0:T(2,128)} %bitcast.15, bf16[256,1152]{1,0:T(8,128)(2,1)} %constant.18.clone.table_h, f32[768]{0:T(1024)} %gain.3, f32[768]{0:T(1024)} %bias.1, ...), custom_call_target="tpu_custom_call" | custom-call | tf_op jit(solution)/shard_map/keys/pallas_call | solution.py:669
  7.1 3.0 %collective-permute-start = (bf16[80,1536]{1,0:T(8,128)(2,1)}, bf16[80,1536]{1,0:T(8,128)(2,1)S(1)}, u32[]{:S(2)}, u32[]{:S(2)}) collective-permute-start(bf16[80,1536]{1,0:T(8,128)(2,1)} %get-tuple-element.88), channel_id=1, source_target_pairs={{0,2},{1,3},{2,0},{3,1},{4,6},{5,7},{6,4},{7,5},{8,10},{9,11},{10,... | collective-permute-start | bytes 737288 | tf_op jit(solution)/shard_map/ppermute | solution.py:682
  11.9 3.8 %queries.1 = (bf16[256,768]{1,0:T(8,128)(2,1)}, bf16[256,768]{1,0:T(8,128)(2,1)}, bf16[256,768]{1,0:T(8,128)(2,1)}, bf16[80,1536]{1,0:T(8,128)(2,1)}) custom-call(bf16[256,768]{1,0:T(8,128)(2,1)} %get-tuple-element.89.normed.norm_a, bf16[768,2304]{1,0:T(8,128)(2,1)} %w_qkv.3, bf16[768,768]{1,0:T(8,128)(2,1)} %w_out.3, bf16[256,768]{1,0:T(8,128)(2,1)} %bitcast.14), custom_call_target="tpu_custom_call" | custom-call | tf_op jit(solution)/shard_map/queries/pallas_call | solution.py:669
  17.4 3.8 %collective-permute-start.4 = (bf16[32,1536]{1,0:T(8,128)(2,1)S(1)}, bf16[32,1536]{1,0:T(8,128)(2,1)S(1)}, u32[]{:S(2)}, u32[]{:S(2)}) collective-permute-start(bf16[32,1536]{1,0:T(8,128)(2,1)S(1)} %pad_maximum_fusion.3), channel_id=1, source_target_pairs={{0,12},{1,13},{2,14},{3,15},{4,0},{5,1},{6,2},{7,3},{8,4},{9,5},{1... | collective-permute-start | bytes 294920 | tf_op jit(solution)/shard_map/ppermute | solution.py:687
  24.8 2.5 %local_forward.3 = (f32[4,256,256]{2,1,0:T(8,128)S(1)}, f32[256,128]{1,0:T(8,128)S(1)}, f32[256,128]{1,0:T(8,128)S(1)}, f32[256,384]{1,0:T(8,128)S(1)}, f32[256,128]{1,0:T(8,128)S(1)}, /*index=5*/f32[256,128]{1,0:T(8,128)S(1)}) custom-call(s32[16]{0:T(128)S(1)} %concatenate.15.meta, bf16[256,768]{1,0:T(8,128)(2,1)S(1)} %copy-done.2, ...), custom_call_target="tpu_custom_call" | custom-call | tf_op jit(solution)/shard_map/local_forward/pallas_call | solution.py:669
  31.2 2.8 %remote_forward.1 = (bf16[256,768]{1,0:T(8,128)(2,1)S(1)}, f32[256,128]{1,0:T(8,128)S(1)}, bf16[80,1664]{1,0:T(8,128)(2,1)S(1)}) custom-call(s32[16]{0:T(128)S(1)} %concatenate.15.meta, bf16[256,768]{1,0:T(8,128)(2,1)S(1)} %copy-done.2, bf16[160,1536]{1,0:T(8,128)(2,1)S(1)} %pad_maximum_fusion.1.refs_0_, ...), custom_call_target="tpu_custom_call" | custom-call | tf_op jit(solution)/shard_map/remote_forward/pallas_call | solution.py:669
  34.4 2.9 %collective-permute-start.9 = (bf16[80,1664]{1,0:T(8,128)(2,1)S(1)}, bf16[80,1664]{1,0:T(8,128)(2,1)S(1)}, u32[]{:S(2)}, u32[]{:S(2)}) collective-permute-start(bf16[80,1664]{1,0:T(8,128)(2,1)S(1)} %get-tuple-element.111), channel_id=1, source_target_pairs={{0,2},{1,3},{2,0},{3,1},{4,6},{5,7},{6,4},{7,5},{8,10},{9,11},{10,... | collective-permute-start | bytes 798728 | tf_op jit(solution)/shard_map/ppermute | solution.py:682
  37.4 3.2 %local_backward.2 = (f32[256,384]{1,0:T(8,128)S(1)}, f32[256,384]{1,0:T(8,128)S(1)}, f32[256,384]{1,0:T(8,128)S(1)}) custom-call(s32[16]{0:T(128)S(1)} %concatenate.15.meta, bf16[256,768]{1,0:T(8,128)(2,1)S(1)} %copy-done.2, bf16[256,1536]{1,0:T(8,128)(2,1)S(1)} %copy-done.1, bf16[256,768]{1,0:T(8,128)(2,1)S(1)} %copy-done.3, ...), custom_call_target="tpu_custom_call" | custom-call | tf_op jit(solution)/shard_map/local_backward/pallas_call | solution.py:669
  40.6 2.3 %query_backward.1.refs_8_ = f32[256,768]{1,0:T(8,128)S(1)} custom-call(s32[16]{0:T(128)S(1)} %concatenate.15.meta, bf16[256,768]{1,0:T(8,128)(2,1)S(1)} %copy-done.2, bf16[256,768]{1,0:T(8,128)(2,1)S(1)} %copy-done.3, f32[256,128]{1,0:T(8,128)S(1)} %get-tuple-element.112.stat, bf16[160,1536]{1,0:T(8,128)(2,1)S(1)} %pad_maximum_fusion.1.refs_0_, ...), custom_call_target="tpu_custom_call" | custom-call | tf_op jit(solution)/shard_map/query_backward/pallas_call | solution.py:669
  47.3 4.2 %local_backward.3 = (f32[256,768]{1,0:T(8,128)S(1)}, f32[256,768]{1,0:T(8,128)S(1)}, f32[256,384]{1,0:T(8,128)S(1)}, f32[256,384]{1,0:T(8,128)S(1)}, f32[256,384]{1,0:T(8,128)S(1)}) custom-call(s32[16]{0:T(128)S(1)} %concatenate.15.meta, bf16[256,768]{1,0:T(8,128)(2,1)S(1)} %copy-done.2, bf16[256,1536]{1,0:T(8,128)(2,1)S(1)} %copy-done.1, ...), custom_call_target="tpu_custom_call" | custom-call | tf_op jit(solution)/shard_map/local_backward/pallas_call | solution.py:669
  51.6 2.3 %collective-permute-done.11.refs_1_ = bf16[32,1664]{1,0:T(8,128)(2,1)S(1)} collective-permute-done((bf16[32,1664]{1,0:T(8,128)(2,1)S(1)}, bf16[32,1664]{1,0:T(8,128)(2,1)S(1)}, u32[]{:S(2)}, u32[]{:S(2)}) %collective-permute-start.11) | collective-permute-done | bytes 106528 | tf_op jit(solution)/shard_map/ppermute | solution.py:687
  56.2 1.8 %key_backward.1 = (bf16[256,2304]{1,0:T(8,128)(2,1)S(1)}, bf16[256,1536]{1,0:T(8,128)(2,1)S(1)}, bf16[256,1536]{1,0:T(8,128)(2,1)S(1)}) custom-call(s32[16]{0:T(128)S(1)} %concatenate.15.meta, bf16[256,1536]{1,0:T(8,128)(2,1)S(1)} %copy-done.1, bf16[160,1664]{1,0:T(8,128)(2,1)S(1)} %pad_maximum_fusion.refs_0_, ...), custom_call_target="tpu_custom_call" | custom-call | tf_op jit(solution)/shard_map/key_backward/pallas_call | solution.py:669
  60.4 2.3 %weight_grad.1 = (f32[768,384]{1,0:T(8,128)S(1)}, bf16[768,384]{1,0:T(8,128)(2,1)S(1)}, bf16[768,384]{1,0:T(8,128)(2,1)S(1)}, bf16[768,384]{1,0:T(8,128)(2,1)S(1)}) custom-call(s32[16]{0:T(128)S(1)} %concatenate.15.meta, bf16[256,1536]{1,0:T(8,128)(2,1)S(1)} %get-tuple-element.132.own, bf16[256,1536]{1,0:T(8,128)(2,1)S(1)} %collective-permute-done.18.other, ...), custom_call_target="tpu_custom_call" | custom-call | tf_op jit(solution)/shard_map/weight_grad/pallas_call | solution.py:669
  64.1 2.6 %collective-permute-start.20 = (bf16[768,384]{1,0:T(8,128)(2,1)S(1)}, bf16[768,384]{1,0:T(8,128)(2,1)S(1)}, u32[]{:S(2)}, u32[]{:S(2)}) collective-permute-start(bf16[768,384]{1,0:T(8,128)(2,1)S(1)} %get-tuple-element.144), channel_id=1, source_target_pairs={{0,64},{1,3},{2,66},{3,1},{4,68},{5,7},{6,70},{7,5},{8,72},{9,11},... | collective-permute-start | bytes 1769480 | tf_op jit(solution)/shard_map/ppermute | solution.py:721
  67.8 2.5 %token_grad.1 = (bf16[256,768]{1,0:T(8,128)(2,1)}, bf16[16,384]{1,0:T(8,128)(2,1)S(1)}) custom-call(bf16[256,2304]{1,0:T(8,128)(2,1)S(1)} %get-tuple-element.141.d_qkv, bf16[768,2304]{1,0:T(8,128)(2,1)S(1)} %copy-done, f32[256,768]{1,0:T(8,128)S(1)} %copy-done.5, f32[768]{0:T(1024)S(1)} %copy-done.9, bf16[256,768]{1,0:T(8,128)(2,1)S(1)} %copy-done.6), custom_call_target="tpu_custom_call" | custom-call | tf_op jit(solution)/shard_map/token_grad/pallas_call | solution.py:669
  73.1 7.5 %collective-permute-done.20.r2 = bf16[768,384]{1,0:T(8,128)(2,1)S(1)} collective-permute-done((bf16[768,384]{1,0:T(8,128)(2,1)S(1)}, bf16[768,384]{1,0:T(8,128)(2,1)S(1)}, u32[]{:S(2)}, u32[]{:S(2)}) %collective-permute-start.20) | collective-permute-done | bytes 589856 | tf_op jit(solution)/shard_map/ppermute | solution.py:721
  83.2 1.9 %collective-permute-start.24 = (bf16[208,384]{1,0:T(8,128)(2,1)S(1)}, bf16[208,384]{1,0:T(8,128)(2,1)S(1)}, u32[]{:S(2)}, u32[]{:S(2)}) collective-permute-start(bf16[208,384]{1,0:T(8,128)(2,1)S(1)} %get-tuple-element.153), channel_id=1, source_target_pairs={{0,18},{1,13},{2,16},{3,15},{4,22},{5,1},{6,20},{7,3},{8,26},{9,5}... | collective-permute-start | bytes 479240 | tf_op jit(solution)/shard_map/ppermute | solution.py:721
  85.1 3.5 %collective-permute-done.22.r1 = bf16[208,384]{1,0:T(8,128)(2,1)S(1)} collective-permute-done((bf16[208,384]{1,0:T(8,128)(2,1)S(1)}, bf16[208,384]{1,0:T(8,128)(2,1)S(1)}, u32[]{:S(2)}, u32[]{:S(2)}) %collective-permute-start.22) | collective-permute-done | bytes 159776 | tf_op jit(solution)/shard_map/ppermute | solution.py:721
  89.8 2.2 %collective-permute-start.27 = (bf16[208,384]{1,0:T(8,128)(2,1)S(1)}, bf16[208,384]{1,0:T(8,128)(2,1)S(1)}, u32[]{:S(2)}, u32[]{:S(2)}) collective-permute-start(bf16[208,384]{1,0:T(8,128)(2,1)S(1)} %add_b.1.own), channel_id=1, source_target_pairs={{0,12},{1,97},{2,14},{3,99},{4,0},{5,101},{6,2},{7,103},{8,4},{9,1... | collective-permute-start | bytes 479240 | tf_op jit(solution)/shard_map/ppermute | solution.py:721
  93.2 2.8 %collective-permute-done.27.r3 = bf16[208,384]{1,0:T(8,128)(2,1)S(1)} collective-permute-done((bf16[208,384]{1,0:T(8,128)(2,1)S(1)}, bf16[208,384]{1,0:T(8,128)(2,1)S(1)}, u32[]{:S(2)}, u32[]{:S(2)}) %collective-permute-start.27) | collective-permute-done | bytes 159776 | tf_op jit(solution)/shard_map/ppermute | solution.py:721
  96.0 1.8 %collective-permute-done.26.r2 = bf16[208,384]{1,0:T(8,128)(2,1)S(1)} collective-permute-done((bf16[208,384]{1,0:T(8,128)(2,1)S(1)}, bf16[208,384]{1,0:T(8,128)(2,1)S(1)}, u32[]{:S(2)}, u32[]{:S(2)}) %collective-permute-start.26) | collective-permute-done | bytes 159776 | tf_op jit(solution)/shard_map/ppermute | solution.py:721
  97.8 1.9 %collective-permute-done.25.r1 = bf16[208,384]{1,0:T(8,128)(2,1)S(1)} collective-permute-done((bf16[208,384]{1,0:T(8,128)(2,1)S(1)}, bf16[208,384]{1,0:T(8,128)(2,1)S(1)}, u32[]{:S(2)}, u32[]{:S(2)}) %collective-permute-start.25) | collective-permute-done | bytes 159776 | tf_op jit(solution)/shard_map/ppermute | solution.py:721
  99.8 2.5 %collective-permute-start.30 = (bf16[208,384]{1,0:T(8,128)(2,1)S(1)}, bf16[208,384]{1,0:T(8,128)(2,1)S(1)}, u32[]{:S(2)}, u32[]{:S(2)}) collective-permute-start(bf16[208,384]{1,0:T(8,128)(2,1)S(1)} %add_c.1.own), channel_id=1, source_target_pairs={{0,18},{1,13},{2,16},{3,15},{4,22},{5,1},{6,20},{7,3},{8,26},{9,5}... | collective-permute-start | bytes 479240 | tf_op jit(solution)/shard_map/ppermute | solution.py:721
  102.9 3.3 %collective-permute-done.30.r3 = bf16[208,384]{1,0:T(8,128)(2,1)S(1)} collective-permute-done((bf16[208,384]{1,0:T(8,128)(2,1)S(1)}, bf16[208,384]{1,0:T(8,128)(2,1)S(1)}, u32[]{:S(2)}, u32[]{:S(2)}) %collective-permute-start.30) | collective-permute-done | bytes 159776 | tf_op jit(solution)/shard_map/ppermute | solution.py:721
  106.2 1.8 %collective-permute-done.29.r2 = bf16[208,384]{1,0:T(8,128)(2,1)S(1)} collective-permute-done((bf16[208,384]{1,0:T(8,128)(2,1)S(1)}, bf16[208,384]{1,0:T(8,128)(2,1)S(1)}, u32[]{:S(2)}, u32[]{:S(2)}) %collective-permute-start.29) | collective-permute-done | bytes 159776 | tf_op jit(solution)/shard_map/ppermute | solution.py:721
  108.0 1.9 %collective-permute-done.28.r1 = bf16[208,384]{1,0:T(8,128)(2,1)S(1)} collective-permute-done((bf16[208,384]{1,0:T(8,128)(2,1)S(1)}, bf16[208,384]{1,0:T(8,128)(2,1)S(1)}, u32[]{:S(2)}, u32[]{:S(2)}) %collective-permute-start.28) | collective-permute-done | bytes 159776 | tf_op jit(solution)/shard_map/ppermute | solution.py:721
  110.5 3.6 %collective-permute-start.34 = (bf16[784,384]{1,0:T(8,128)(2,1)S(1)}, bf16[784,384]{1,0:T(8,128)(2,1)S(1)}, u32[]{:S(2)}, u32[]{:S(2)}) collective-permute-start(bf16[784,384]{1,0:T(8,128)(2,1)S(1)} %merge_b.1.refs_0_.refs_2_), channel_id=1, source_target_pairs={{0,1},{1,0},{2,3},{3,2},{4,5},{5,4},{6,7},{7,6},{8,9},{9,8},{10,11... | collective-permute-start | bytes 1806344 | tf_op jit(solution)/shard_map/ppermute | solution.py:682
  116.2 2.0 %finish.4 = (f32[768,2304]{1,0:T(8,128)}, f32[768,768]{1,0:T(8,128)}) custom-call(s32[16]{0:T(128)S(1)} %concatenate.15.meta, bf16[784,384]{1,0:T(8,128)(2,1)S(1)} %merge_b.1.refs_0_.refs_2_, bf16[784,384]{1,0:T(8,128)(2,1)S(1)} %collective-permute-done.34.refs_1_.refs_6_), custom_call_target="tpu_custom_call" | custom-call | tf_op jit(solution)/shard_map/finish/pallas_call | solution.py:648
  118.2 6.6 %collective-permute-done.33.refs_0_.refs_4_ = bf16[784,384]{1,0:T(8,128)(2,1)S(1)} collective-permute-done((bf16[784,384]{1,0:T(8,128)(2,1)S(1)}, bf16[784,384]{1,0:T(8,128)(2,1)S(1)}, u32[]{:S(2)}, u32[]{:S(2)}) %collective-permute-start.33) | collective-permute-done | bytes 602144 | tf_op jit(solution)/shard_map/ppermute | solution.py:721
  129.2 2.1 %collective-permute-done.31.refs_0_.refs_3_ = bf16[784,384]{1,0:T(8,128)(2,1)S(1)} collective-permute-done((bf16[784,384]{1,0:T(8,128)(2,1)S(1)}, bf16[784,384]{1,0:T(8,128)(2,1)S(1)}, u32[]{:S(2)}, u32[]{:S(2)}) %collective-permute-start.31) | collective-permute-done | bytes 602144 | tf_op jit(solution)/shard_map/ppermute | solution.py:721
  132.2 2.4 %finish.6 = (f32[768,2304]{1,0:T(8,128)}, f32[768,768]{1,0:T(8,128)}) custom-call(s32[16]{0:T(128)S(1)} %concatenate.15.meta, bf16[784,384]{1,0:T(8,128)(2,1)S(1)} %collective-permute-done.31.refs_0_.refs_3_, bf16[784,384]{1,0:T(8,128)(2,1)S(1)} %collective-permute-done.32.refs_1_.refs_5_, ...), custom_call_target="tpu_custom_call", output_to_operand_aliasing={{0}: (4, {}), {1}: (5, {})} | custom-call | tf_op jit(solution)/shard_map/finish/pallas_call | solution.py:648
  134.7 2.6 %finish.7 = (f32[768,2304]{1,0:T(8,128)}, f32[768,768]{1,0:T(8,128)}, f32[768]{0:T(1024)}, f32[768]{0:T(1024)}) custom-call(s32[16]{0:T(128)S(1)} %concatenate.15.meta, bf16[784,384]{1,0:T(8,128)(2,1)S(1)} %collective-permute-done.35.refs_0_.refs_7_, ...), custom_call_target="tpu_custom_call", output_to_operand_aliasing={{0}: (11, {}), {1}: (12, {})} | custom-call | tf_op jit(solution)/shard_map/finish/pallas_call | solution.py:648
  (101 shorter events, 40.9 us)
Async XLA Ops:
  5.6 10.8 %collective-permute-start.1 = (bf16[256,768]{1,0:T(8,128)(2,1)}, bf16[256,768]{1,0:T(8,128)(2,1)S(1)}, u32[]{:S(2)}, u32[]{:S(2)}) collective-permute-start(bf16[256,768]{1,0:T(8,128)(2,1)} %get-tuple-element.89.normed.norm_a), channel_id=1, source_target_pairs={{0,1},{1,0},{2,3},{3,2},{4,5},{5,4},{6,7},{7,6},{8,9},{9,8},{10,11... | collective-permute-start | bytes 1179656 | tf_op jit(solution)/shard_map/ppermute | solution.py:682
  7.1 9.3 %collective-permute-start = (bf16[80,1536]{1,0:T(8,128)(2,1)}, bf16[80,1536]{1,0:T(8,128)(2,1)S(1)}, u32[]{:S(2)}, u32[]{:S(2)}) collective-permute-start(bf16[80,1536]{1,0:T(8,128)(2,1)} %get-tuple-element.88), channel_id=1, source_target_pairs={{0,2},{1,3},{2,0},{3,1},{4,6},{5,7},{6,4},{7,5},{8,10},{9,11},{10,... | collective-permute-start | bytes 737288 | tf_op jit(solution)/shard_map/ppermute | solution.py:682
  16.5 8.3 %collective-permute-start.5 = (bf16[160,1536]{1,0:T(8,128)(2,1)S(1)}, bf16[160,1536]{1,0:T(8,128)(2,1)S(1)}, u32[]{:S(2)}, u32[]{:S(2)}) collective-permute-start(bf16[160,1536]{1,0:T(8,128)(2,1)S(1)} %pad_maximum_fusion.1.refs_0_), channel_id=1, source_target_pairs={{0,1},{1,0},{2,3},{3,2},{4,5},{5,4},{6,7},{7,6},{8,9},{9,8},{10,11... | collective-permute-start | bytes 1474568 | tf_op jit(solution)/shard_map/ppermute | solution.py:682
  17.4 10.0 %collective-permute-start.4 = (bf16[32,1536]{1,0:T(8,128)(2,1)S(1)}, bf16[32,1536]{1,0:T(8,128)(2,1)S(1)}, u32[]{:S(2)}, u32[]{:S(2)}) collective-permute-start(bf16[32,1536]{1,0:T(8,128)(2,1)S(1)} %pad_maximum_fusion.3), channel_id=1, source_target_pairs={{0,12},{1,13},{2,14},{3,15},{4,0},{5,1},{6,2},{7,3},{8,4},{9,5},{1... | collective-permute-start | bytes 294920 | tf_op jit(solution)/shard_map/ppermute | solution.py:687
  21.2 6.2 %collective-permute-start.3 = (bf16[32,1536]{1,0:T(8,128)(2,1)S(1)}, bf16[32,1536]{1,0:T(8,128)(2,1)S(1)}, u32[]{:S(2)}, u32[]{:S(2)}) collective-permute-start(bf16[32,1536]{1,0:T(8,128)(2,1)S(1)} %pad_maximum_fusion.3), channel_id=1, source_target_pairs={{0,8},{1,9},{2,10},{3,11},{4,12},{5,13},{6,14},{7,15},{8,0},{9,1},... | collective-permute-start | bytes 294920 | tf_op jit(solution)/shard_map/ppermute | solution.py:687
  21.2 7.8 %collective-permute-start.2 = (bf16[32,1536]{1,0:T(8,128)(2,1)S(1)}, bf16[32,1536]{1,0:T(8,128)(2,1)S(1)}, u32[]{:S(2)}, u32[]{:S(2)}) collective-permute-start(bf16[32,1536]{1,0:T(8,128)(2,1)S(1)} %pad_maximum_fusion.3), channel_id=1, source_target_pairs={{0,4},{1,5},{2,6},{3,7},{4,8},{5,9},{6,10},{7,11},{8,12},{9,13},{1... | collective-permute-start | bytes 294920 | tf_op jit(solution)/shard_map/ppermute | solution.py:687
  34.0 9.7 %collective-permute-start.10 = (bf16[256,768]{1,0:T(8,128)(2,1)S(1)}, bf16[256,768]{1,0:T(8,128)(2,1)S(1)}, u32[]{:S(2)}, u32[]{:S(2)}) collective-permute-start(bf16[256,768]{1,0:T(8,128)(2,1)S(1)} %get-tuple-element.139.att_a.att), channel_id=1, source_target_pairs={{0,1},{1,0},{2,3},{3,2},{4,5},{5,4},{6,7},{7,6},{8,9},{9,8},{10,11... | collective-permute-start | bytes 1179656 | tf_op jit(solution)/shard_map/ppermute | solution.py:682
  34.4 9.2 %collective-permute-start.9 = (bf16[80,1664]{1,0:T(8,128)(2,1)S(1)}, bf16[80,1664]{1,0:T(8,128)(2,1)S(1)}, u32[]{:S(2)}, u32[]{:S(2)}) collective-permute-start(bf16[80,1664]{1,0:T(8,128)(2,1)S(1)} %get-tuple-element.111), channel_id=1, source_target_pairs={{0,2},{1,3},{2,0},{3,1},{4,6},{5,7},{6,4},{7,5},{8,10},{9,11},{10,... | collective-permute-start | bytes 798728 | tf_op jit(solution)/shard_map/ppermute | solution.py:682
  43.8 3.6 %collective-permute-start.14 = (bf16[160,1664]{1,0:T(8,128)(2,1)S(1)}, bf16[160,1664]{1,0:T(8,128)(2,1)S(1)}, u32[]{:S(2)}, u32[]{:S(2)}) collective-permute-start(bf16[160,1664]{1,0:T(8,128)(2,1)S(1)} %pad_maximum_fusion.refs_0_), channel_id=1, source_target_pairs={{0,1},{1,0},{2,3},{3,2},{4,5},{5,4},{6,7},{7,6},{8,9},{9,8},{10,11... | collective-permute-start | bytes 1597448 | tf_op jit(solution)/shard_map/ppermute | solution.py:682
  44.9 6.6 %collective-permute-start.13 = (bf16[32,1664]{1,0:T(8,128)(2,1)S(1)}, bf16[32,1664]{1,0:T(8,128)(2,1)S(1)}, u32[]{:S(2)}, u32[]{:S(2)}) collective-permute-start(bf16[32,1664]{1,0:T(8,128)(2,1)S(1)} %pad_maximum_fusion.2), channel_id=1, source_target_pairs={{0,12},{1,13},{2,14},{3,15},{4,0},{5,1},{6,2},{7,3},{8,4},{9,5},{1... | collective-permute-start | bytes 319496 | tf_op jit(solution)/shard_map/ppermute | solution.py:687
  45.6 6.0 %collective-permute-start.12 = (bf16[32,1664]{1,0:T(8,128)(2,1)S(1)}, bf16[32,1664]{1,0:T(8,128)(2,1)S(1)}, u32[]{:S(2)}, u32[]{:S(2)}) collective-permute-start(bf16[32,1664]{1,0:T(8,128)(2,1)S(1)} %pad_maximum_fusion.2), channel_id=1, source_target_pairs={{0,8},{1,9},{2,10},{3,11},{4,12},{5,13},{6,14},{7,15},{8,0},{9,1},... | collective-permute-start | bytes 319496 | tf_op jit(solution)/shard_map/ppermute | solution.py:687
  47.3 6.5 %collective-permute-start.11 = (bf16[32,1664]{1,0:T(8,128)(2,1)S(1)}, bf16[32,1664]{1,0:T(8,128)(2,1)S(1)}, u32[]{:S(2)}, u32[]{:S(2)}) collective-permute-start(bf16[32,1664]{1,0:T(8,128)(2,1)S(1)} %pad_maximum_fusion.2), channel_id=1, source_target_pairs={{0,4},{1,5},{2,6},{3,7},{4,8},{5,9},{6,10},{7,11},{8,12},{9,13},{1... | collective-permute-start | bytes 319496 | tf_op jit(solution)/shard_map/ppermute | solution.py:687
  58.0 2.4 %collective-permute-start.18 = (bf16[256,1536]{1,0:T(8,128)(2,1)S(1)}, bf16[256,1536]{1,0:T(8,128)(2,1)S(1)}, u32[]{:S(2)}, u32[]{:S(2)}) collective-permute-start(bf16[256,1536]{1,0:T(8,128)(2,1)S(1)} %get-tuple-element.133), channel_id=1, source_target_pairs={{0,1},{1,0},{2,3},{3,2},{4,5},{5,4},{6,7},{7,6},{8,9},{9,8},{10,11... | collective-permute-start | bytes 2359304 | tf_op jit(solution)/shard_map/ppermute | solution.py:682
  62.8 10.4 %collective-permute-start.19 = (bf16[768,384]{1,0:T(8,128)(2,1)S(1)}, bf16[768,384]{1,0:T(8,128)(2,1)S(1)}, u32[]{:S(2)}, u32[]{:S(2)}) collective-permute-start(bf16[768,384]{1,0:T(8,128)(2,1)S(1)} %get-tuple-element.143), channel_id=1, source_target_pairs={{0,32},{1,17},{2,34},{3,19},{4,36},{5,21},{6,38},{7,23},{8,40},{9,... | collective-permute-start | bytes 1769480 | tf_op jit(solution)/shard_map/ppermute | solution.py:721
  64.1 16.5 %collective-permute-start.20 = (bf16[768,384]{1,0:T(8,128)(2,1)S(1)}, bf16[768,384]{1,0:T(8,128)(2,1)S(1)}, u32[]{:S(2)}, u32[]{:S(2)}) collective-permute-start(bf16[768,384]{1,0:T(8,128)(2,1)S(1)} %get-tuple-element.144), channel_id=1, source_target_pairs={{0,64},{1,3},{2,66},{3,1},{4,68},{5,7},{6,70},{7,5},{8,72},{9,11},... | collective-permute-start | bytes 1769480 | tf_op jit(solution)/shard_map/ppermute | solution.py:721
  66.7 13.9 %collective-permute-start.21 = (bf16[768,384]{1,0:T(8,128)(2,1)S(1)}, bf16[768,384]{1,0:T(8,128)(2,1)S(1)}, u32[]{:S(2)}, u32[]{:S(2)}) collective-permute-start(bf16[768,384]{1,0:T(8,128)(2,1)S(1)} %get-tuple-element.145), channel_id=1, source_target_pairs={{0,96},{1,19},{2,98},{3,17},{4,100},{5,23},{6,102},{7,21},{8,104},... | collective-permute-start | bytes 1769480 | tf_op jit(solution)/shard_map/ppermute | solution.py:721
  81.5 7.1 %collective-permute-start.22 = (bf16[208,384]{1,0:T(8,128)(2,1)S(1)}, bf16[208,384]{1,0:T(8,128)(2,1)S(1)}, u32[]{:S(2)}, u32[]{:S(2)}) collective-permute-start(bf16[208,384]{1,0:T(8,128)(2,1)S(1)} %get-tuple-element.151), channel_id=1, source_target_pairs={{0,16},{1,5},{2,18},{3,7},{4,20},{5,9},{6,22},{7,11},{8,24},{9,13}... | collective-permute-start | bytes 479240 | tf_op jit(solution)/shard_map/ppermute | solution.py:721
  81.8 6.8 %collective-permute-start.23 = (bf16[208,384]{1,0:T(8,128)(2,1)S(1)}, bf16[208,384]{1,0:T(8,128)(2,1)S(1)}, u32[]{:S(2)}, u32[]{:S(2)}) collective-permute-start(bf16[208,384]{1,0:T(8,128)(2,1)S(1)} %get-tuple-element.152), channel_id=1, source_target_pairs={{0,2},{1,9},{2,0},{3,11},{4,6},{5,13},{6,4},{7,15},{8,10},{9,1},{1... | collective-permute-start | bytes 479240 | tf_op jit(solution)/shard_map/ppermute | solution.py:721
  83.2 5.9 %collective-permute-start.24 = (bf16[208,384]{1,0:T(8,128)(2,1)S(1)}, bf16[208,384]{1,0:T(8,128)(2,1)S(1)}, u32[]{:S(2)}, u32[]{:S(2)}) collective-permute-start(bf16[208,384]{1,0:T(8,128)(2,1)S(1)} %get-tuple-element.153), channel_id=1, source_target_pairs={{0,18},{1,13},{2,16},{3,15},{4,22},{5,1},{6,20},{7,3},{8,26},{9,5}... | collective-permute-start | bytes 479240 | tf_op jit(solution)/shard_map/ppermute | solution.py:721
  89.8 6.2 %collective-permute-start.27 = (bf16[208,384]{1,0:T(8,128)(2,1)S(1)}, bf16[208,384]{1,0:T(8,128)(2,1)S(1)}, u32[]{:S(2)}, u32[]{:S(2)}) collective-permute-start(bf16[208,384]{1,0:T(8,128)(2,1)S(1)} %add_b.1.own), channel_id=1, source_target_pairs={{0,12},{1,97},{2,14},{3,99},{4,0},{5,101},{6,2},{7,103},{8,4},{9,1... | collective-permute-start | bytes 479240 | tf_op jit(solution)/shard_map/ppermute | solution.py:721
  92.1 5.7 %collective-permute-start.26 = (bf16[208,384]{1,0:T(8,128)(2,1)S(1)}, bf16[208,384]{1,0:T(8,128)(2,1)S(1)}, u32[]{:S(2)}, u32[]{:S(2)}) collective-permute-start(bf16[208,384]{1,0:T(8,128)(2,1)S(1)} %add_b.1.own), channel_id=1, source_target_pairs={{0,8},{1,65},{2,10},{3,67},{4,12},{5,69},{6,14},{7,71},{8,0},{9,73... | collective-permute-start | bytes 479240 | tf_op jit(solution)/shard_map/ppermute | solution.py:721
  92.7 7.0 %collective-permute-start.25 = (bf16[208,384]{1,0:T(8,128)(2,1)S(1)}, bf16[208,384]{1,0:T(8,128)(2,1)S(1)}, u32[]{:S(2)}, u32[]{:S(2)}) collective-permute-start(bf16[208,384]{1,0:T(8,128)(2,1)S(1)} %add_b.1.own), channel_id=1, source_target_pairs={{0,4},{1,33},{2,6},{3,35},{4,8},{5,37},{6,10},{7,39},{8,12},{9,41}... | collective-permute-start | bytes 479240 | tf_op jit(solution)/shard_map/ppermute | solution.py:721
  99.8 6.4 %collective-permute-start.30 = (bf16[208,384]{1,0:T(8,128)(2,1)S(1)}, bf16[208,384]{1,0:T(8,128)(2,1)S(1)}, u32[]{:S(2)}, u32[]{:S(2)}) collective-permute-start(bf16[208,384]{1,0:T(8,128)(2,1)S(1)} %add_c.1.own), channel_id=1, source_target_pairs={{0,18},{1,13},{2,16},{3,15},{4,22},{5,1},{6,20},{7,3},{8,26},{9,5}... | collective-permute-start | bytes 479240 | tf_op jit(solution)/shard_map/ppermute | solution.py:721
  102.3 5.7 %collective-permute-start.29 = (bf16[208,384]{1,0:T(8,128)(2,1)S(1)}, bf16[208,384]{1,0:T(8,128)(2,1)S(1)}, u32[]{:S(2)}, u32[]{:S(2)}) collective-permute-start(bf16[208,384]{1,0:T(8,128)(2,1)S(1)} %add_c.1.own), channel_id=1, source_target_pairs={{0,2},{1,9},{2,0},{3,11},{4,6},{5,13},{6,4},{7,15},{8,10},{9,1},{1... | collective-permute-start | bytes 479240 | tf_op jit(solution)/shard_map/ppermute | solution.py:721
  102.6 7.3 %collective-permute-start.28 = (bf16[208,384]{1,0:T(8,128)(2,1)S(1)}, bf16[208,384]{1,0:T(8,128)(2,1)S(1)}, u32[]{:S(2)}, u32[]{:S(2)}) collective-permute-start(bf16[208,384]{1,0:T(8,128)(2,1)S(1)} %add_c.1.own), channel_id=1, source_target_pairs={{0,16},{1,5},{2,18},{3,7},{4,20},{5,9},{6,22},{7,11},{8,24},{9,13}... | collective-permute-start | bytes 479240 | tf_op jit(solution)/shard_map/ppermute | solution.py:721
  110.5 5.7 %collective-permute-start.34 = (bf16[784,384]{1,0:T(8,128)(2,1)S(1)}, bf16[784,384]{1,0:T(8,128)(2,1)S(1)}, u32[]{:S(2)}, u32[]{:S(2)}) collective-permute-start(bf16[784,384]{1,0:T(8,128)(2,1)S(1)} %merge_b.1.refs_0_.refs_2_), channel_id=1, source_target_pairs={{0,1},{1,0},{2,3},{3,2},{4,5},{5,4},{6,7},{7,6},{8,9},{9,8},{10,11... | collective-permute-start | bytes 1806344 | tf_op jit(solution)/shard_map/ppermute | solution.py:682
  114.1 10.7 %collective-permute-start.33 = (bf16[784,384]{1,0:T(8,128)(2,1)S(1)}, bf16[784,384]{1,0:T(8,128)(2,1)S(1)}, u32[]{:S(2)}, u32[]{:S(2)}) collective-permute-start(bf16[784,384]{1,0:T(8,128)(2,1)S(1)} %merge_b.1.refs_0_.refs_2_), channel_id=1, source_target_pairs={{0,64},{1,3},{2,66},{3,1},{4,68},{5,7},{6,70},{7,5},{8,72},{9,11},... | collective-permute-start | bytes 1806344 | tf_op jit(solution)/shard_map/ppermute | solution.py:721
  114.7 14.5 %collective-permute-start.32 = (bf16[784,384]{1,0:T(8,128)(2,1)S(1)}, bf16[784,384]{1,0:T(8,128)(2,1)S(1)}, u32[]{:S(2)}, u32[]{:S(2)}) collective-permute-start(bf16[784,384]{1,0:T(8,128)(2,1)S(1)} %merge_b.1.refs_0_.refs_2_), channel_id=1, source_target_pairs={{0,96},{1,19},{2,98},{3,17},{4,100},{5,23},{6,102},{7,21},{8,104},... | collective-permute-start | bytes 1806344 | tf_op jit(solution)/shard_map/ppermute | solution.py:721
  115.6 15.7 %collective-permute-start.31 = (bf16[784,384]{1,0:T(8,128)(2,1)S(1)}, bf16[784,384]{1,0:T(8,128)(2,1)S(1)}, u32[]{:S(2)}, u32[]{:S(2)}) collective-permute-start(bf16[784,384]{1,0:T(8,128)(2,1)S(1)} %merge_b.1.refs_0_.refs_2_), channel_id=1, source_target_pairs={{0,32},{1,17},{2,34},{3,19},{4,36},{5,21},{6,38},{7,23},{8,40},{9,... | collective-permute-start | bytes 1806344 | tf_op jit(solution)/shard_map/ppermute | solution.py:721
  124.9 7.4 %collective-permute-start.37 = (bf16[784,384]{1,0:T(8,128)(2,1)S(1)}, bf16[784,384]{1,0:T(8,128)(2,1)S(1)}, u32[]{:S(2)}, u32[]{:S(2)}) collective-permute-start(bf16[784,384]{1,0:T(8,128)(2,1)S(1)} %collective-permute-done.33.refs_0_.refs_4_), channel_id=1, source_target_pairs={{0,1},{1,0},{2,3},{3,2},{4,5},{5,4},{6,7},{7,6},{8,9},{9,8},{10,11... | collective-permute-start | bytes 1806344 | tf_op jit(solution)/shard_map/ppermute | solution.py:682
  131.3 3.4 %collective-permute-start.35 = (bf16[784,384]{1,0:T(8,128)(2,1)S(1)}, bf16[784,384]{1,0:T(8,128)(2,1)S(1)}, u32[]{:S(2)}, u32[]{:S(2)}) collective-permute-start(bf16[784,384]{1,0:T(8,128)(2,1)S(1)} %collective-permute-done.31.refs_0_.refs_3_), channel_id=1, source_target_pairs={{0,1},{1,0},{2,3},{3,2},{4,5},{5,4},{6,7},{7,6},{8,9},{9,8},{10,11... | collective-permute-start | bytes 1806344 | tf_op jit(solution)/shard_map/ppermute | solution.py:682
  132.2 2.5 %collective-permute-start.36 = (bf16[784,384]{1,0:T(8,128)(2,1)S(1)}, bf16[784,384]{1,0:T(8,128)(2,1)S(1)}, u32[]{:S(2)}, u32[]{:S(2)}) collective-permute-start(bf16[784,384]{1,0:T(8,128)(2,1)S(1)} %collective-permute-done.32.refs_1_.refs_5_), channel_id=1, source_target_pairs={{0,1},{1,0},{2,3},{3,2},{4,5},{5,4},{6,7},{7,6},{8,9},{9,8},{10,11... | collective-permute-start | bytes 1806344 | tf_op jit(solution)/shard_map/ppermute | solution.py:682
  (17 other events, 103.5 us)

commit v6 on v5

--- a/solution.py
+++ b/solution.py
@@ -765,8 +765,9 @@
     outs = finish(meta, [(ring[2], 0, 2, 0)], (first, outs[1]))
     ring[1], ring[3], *outs = after(ring[1], ring[3], *outs)
     twin[1], twin[3] = swap_seq(ring[1], 1), swap_seq(ring[3], 1)
-    outs = finish(meta, [(ring[1], 0, 1, 0), (ring[3], 0, 3, 0), (twin[2], 1, 2, 0)], outs)
-    return finish(meta, [(twin[1], 1, 1, 0), (twin[3], 1, 3, 0)], outs, ring + twin)
+    pieces = [(ring[1], 0, 1, 0), (ring[3], 0, 3, 0), (twin[2], 1, 2, 0)]
+    pieces += [(twin[1], 1, 1, 0), (twin[3], 1, 3, 0)]
+    return finish(meta, pieces, outs, ring + twin)
 
 
 def position_table():

time: 138 us -> 140 us (1.014)
  waiting for transfers between devices: 44.6 us -> 51.3 us
  starting transfers between devices: 42.8 us -> 40.3 us
    ppermute x17, waiting for transfers between devices: 4.03 us -> 7.02 us  [swap_seq(): return lax.ppermute(block, 'seq', [(i, i ^ code) for i in range(16)])]
    ppermute x6, waiting for transfers between devices: 3.86 us -> 6.12 us  [shift(): lax.ppermute(block, 'seq', [(i, (i + 4 * d) % 16) for i in range(16)])]
    ppermute x15, waiting for transfers between devices: 36.7 us -> 38.2 us  [hop(): return lax.ppermute(block, AXES, ring_route(stage, d))]
    pallas_call x4 -> x3, Pallas kernels: 8.72 us -> 7.48 us  [finish(): pl.pallas_call(functools.partial(finish_kernel, marks=marks, first=first,...]
  transfers between devices with their start and end apart: 38 -> 38, of which waited for: 25 -> 30; matrix products, arithmetic and copies ran while one was open for 1% -> 1% of each run, Pallas kernels for 21% -> 19%
where the time goes in v6:
time: 140 us; the launch traced here: 139 us
  waiting for transfers between devices  51.3 us (37%)
  Pallas kernels  44.6 us (32%)
  starting transfers between devices  40.3 us (29%)
  local copies, waits for them, and re-layouts  1.96 us (1%)
    ppermute x15, waiting for transfers between devices, hop(): return lax.ppermute(block, AXES, ring_route(stage, d))  38.2 us
    pallas_call x17, Pallas kernels, call(): pl.pallas_call(kernel, grid=(1,) if windows else (), out_shape=[jax.Shape...  37.1 us
    ppermute x17, starting transfers between devices, swap_seq(): return lax.ppermute(block, 'seq', [(i, i ^ code) for i in range(16)])  18 us
    ppermute x15, starting transfers between devices, hop(): return lax.ppermute(block, AXES, ring_route(stage, d))  16.3 us
    pallas_call x3, Pallas kernels, finish(): pl.pallas_call(functools.partial(finish_kernel, marks=marks, first=first,...  7.48 us
    ppermute x17, waiting for transfers between devices, swap_seq(): return lax.ppermute(block, 'seq', [(i, i ^ code) for i in range(16)])  7.02 us
    ppermute x6, waiting for transfers between devices, shift(): lax.ppermute(block, 'seq', [(i, (i + 4 * d) % 16) for i in range(16)])  6.12 us
    ppermute x6, starting transfers between devices, shift(): lax.ppermute(block, 'seq', [(i, (i + 4 * d) % 16) for i in range(16)])  6.02 us
  transfers between devices with their start and end apart: 38, of which 30 were waited for; matrix products, arithmetic and copies ran while one was open for 1% of the time, Pallas kernels for 19%

profile of v6, /device:TPU:1, one launch (start us, length us, event | category | flops | bytes accessed | tf_op | source)
XLA Modules:
  0.0 139.4 jit_solution(399702225756708235)
XLA Ops:
  0.6 4.9 %keys.1 = (f32[256,768]{1,0:T(8,128)}, bf16[256,768]{1,0:T(8,128)(2,1)}, bf16[256,1536]{1,0:T(8,128)(2,1)}, bf16[80,1536]{1,0:T(8,128)(2,1)}) custom-call(bf16[256,768]{1,0:T(8,128)(2,1)} %bitcast.13, s32[2,256]{1,0:T(2,128)} %bitcast.15, bf16[256,1152]{1,0:T(8,128)(2,1)} %constant.18.clone.table_h, f32[768]{0:T(1024)} %gain.3, f32[768]{0:T(1024)} %bias.1, ...), custom_call_target="tpu_custom_call" | custom-call | tf_op jit(solution)/shard_map/keys/pallas_call | solution.py:669
  7.1 3.0 %collective-permute-start = (bf16[80,1536]{1,0:T(8,128)(2,1)}, bf16[80,1536]{1,0:T(8,128)(2,1)S(1)}, u32[]{:S(2)}, u32[]{:S(2)}) collective-permute-start(bf16[80,1536]{1,0:T(8,128)(2,1)} %get-tuple-element.86), channel_id=1, source_target_pairs={{0,2},{1,3},{2,0},{3,1},{4,6},{5,7},{6,4},{7,5},{8,10},{9,11},{10,... | collective-permute-start | bytes 737288 | tf_op jit(solution)/shard_map/ppermute | solution.py:682
  11.9 3.7 %queries.1 = (bf16[256,768]{1,0:T(8,128)(2,1)}, bf16[256,768]{1,0:T(8,128)(2,1)}, bf16[256,768]{1,0:T(8,128)(2,1)}, bf16[80,1536]{1,0:T(8,128)(2,1)}) custom-call(bf16[256,768]{1,0:T(8,128)(2,1)} %get-tuple-element.87.normed.norm_a, bf16[768,2304]{1,0:T(8,128)(2,1)} %w_qkv.3, bf16[768,768]{1,0:T(8,128)(2,1)} %w_out.3, bf16[256,768]{1,0:T(8,128)(2,1)} %bitcast.14), custom_call_target="tpu_custom_call" | custom-call | tf_op jit(solution)/shard_map/queries/pallas_call | solution.py:669
  17.4 3.8 %collective-permute-start.4 = (bf16[32,1536]{1,0:T(8,128)(2,1)S(1)}, bf16[32,1536]{1,0:T(8,128)(2,1)S(1)}, u32[]{:S(2)}, u32[]{:S(2)}) collective-permute-start(bf16[32,1536]{1,0:T(8,128)(2,1)S(1)} %pad_maximum_fusion.3), channel_id=1, source_target_pairs={{0,12},{1,13},{2,14},{3,15},{4,0},{5,1},{6,2},{7,3},{8,4},{9,5},{1... | collective-permute-start | bytes 294920 | tf_op jit(solution)/shard_map/ppermute | solution.py:687
  22.0 1.8 %local_forward.2 = (f32[256,384]{1,0:T(8,128)S(1)}, f32[256,128]{1,0:T(8,128)S(1)}, f32[256,128]{1,0:T(8,128)S(1)}) custom-call(s32[16]{0:T(128)S(1)} %concatenate.15.meta, bf16[256,768]{1,0:T(8,128)(2,1)S(1)} %copy-done.2, bf16[256,1536]{1,0:T(8,128)(2,1)S(1)} %copy-done.1), custom_call_target="tpu_custom_call" | custom-call | tf_op jit(solution)/shard_map/local_forward/pallas_call | solution.py:669
  23.8 2.5 %local_forward.3 = (f32[4,256,256]{2,1,0:T(8,128)S(1)}, f32[256,128]{1,0:T(8,128)S(1)}, f32[256,128]{1,0:T(8,128)S(1)}, f32[256,384]{1,0:T(8,128)S(1)}, f32[256,128]{1,0:T(8,128)S(1)}, /*index=5*/f32[256,128]{1,0:T(8,128)S(1)}) custom-call(s32[16]{0:T(128)S(1)} %concatenate.15.meta, bf16[256,768]{1,0:T(8,128)(2,1)S(1)} %copy-done.2, ...), custom_call_target="tpu_custom_call" | custom-call | tf_op jit(solution)/shard_map/local_forward/pallas_call | solution.py:669
  26.8 2.2 %collective-permute-done.2.refs_1_ = bf16[32,1536]{1,0:T(8,128)(2,1)S(1)} collective-permute-done((bf16[32,1536]{1,0:T(8,128)(2,1)S(1)}, bf16[32,1536]{1,0:T(8,128)(2,1)S(1)}, u32[]{:S(2)}, u32[]{:S(2)}) %collective-permute-start.2) | collective-permute-done | bytes 98336 | tf_op jit(solution)/shard_map/ppermute | solution.py:687
  31.2 2.8 %remote_forward.1 = (bf16[256,768]{1,0:T(8,128)(2,1)S(1)}, f32[256,128]{1,0:T(8,128)S(1)}, bf16[80,1664]{1,0:T(8,128)(2,1)S(1)}) custom-call(s32[16]{0:T(128)S(1)} %concatenate.15.meta, bf16[256,768]{1,0:T(8,128)(2,1)S(1)} %copy-done.2, bf16[160,1536]{1,0:T(8,128)(2,1)S(1)} %pad_maximum_fusion.1.refs_0_, ...), custom_call_target="tpu_custom_call" | custom-call | tf_op jit(solution)/shard_map/remote_forward/pallas_call | solution.py:669
  34.4 2.9 %collective-permute-start.9 = (bf16[80,1664]{1,0:T(8,128)(2,1)S(1)}, bf16[80,1664]{1,0:T(8,128)(2,1)S(1)}, u32[]{:S(2)}, u32[]{:S(2)}) collective-permute-start(bf16[80,1664]{1,0:T(8,128)(2,1)S(1)} %get-tuple-element.109), channel_id=1, source_target_pairs={{0,2},{1,3},{2,0},{3,1},{4,6},{5,7},{6,4},{7,5},{8,10},{9,11},{10,... | collective-permute-start | bytes 798728 | tf_op jit(solution)/shard_map/ppermute | solution.py:682
  37.4 3.2 %local_backward.2 = (f32[256,384]{1,0:T(8,128)S(1)}, f32[256,384]{1,0:T(8,128)S(1)}, f32[256,384]{1,0:T(8,128)S(1)}) custom-call(s32[16]{0:T(128)S(1)} %concatenate.15.meta, bf16[256,768]{1,0:T(8,128)(2,1)S(1)} %copy-done.2, bf16[256,1536]{1,0:T(8,128)(2,1)S(1)} %copy-done.1, bf16[256,768]{1,0:T(8,128)(2,1)S(1)} %copy-done.3, ...), custom_call_target="tpu_custom_call" | custom-call | tf_op jit(solution)/shard_map/local_backward/pallas_call | solution.py:669
  40.5 2.3 %query_backward.1.refs_8_ = f32[256,768]{1,0:T(8,128)S(1)} custom-call(s32[16]{0:T(128)S(1)} %concatenate.15.meta, bf16[256,768]{1,0:T(8,128)(2,1)S(1)} %copy-done.2, bf16[256,768]{1,0:T(8,128)(2,1)S(1)} %copy-done.3, f32[256,128]{1,0:T(8,128)S(1)} %get-tuple-element.110.stat, bf16[160,1536]{1,0:T(8,128)(2,1)S(1)} %pad_maximum_fusion.1.refs_0_, ...), custom_call_target="tpu_custom_call" | custom-call | tf_op jit(solution)/shard_map/query_backward/pallas_call | solution.py:669
  46.5 4.2 %local_backward.3 = (f32[256,768]{1,0:T(8,128)S(1)}, f32[256,768]{1,0:T(8,128)S(1)}, f32[256,384]{1,0:T(8,128)S(1)}, f32[256,384]{1,0:T(8,128)S(1)}, f32[256,384]{1,0:T(8,128)S(1)}) custom-call(s32[16]{0:T(128)S(1)} %concatenate.15.meta, bf16[256,768]{1,0:T(8,128)(2,1)S(1)} %copy-done.2, bf16[256,1536]{1,0:T(8,128)(2,1)S(1)} %copy-done.1, ...), custom_call_target="tpu_custom_call" | custom-call | tf_op jit(solution)/shard_map/local_backward/pallas_call | solution.py:669
  51.3 3.0 %collective-permute-done.11.refs_1_ = bf16[32,1664]{1,0:T(8,128)(2,1)S(1)} collective-permute-done((bf16[32,1664]{1,0:T(8,128)(2,1)S(1)}, bf16[32,1664]{1,0:T(8,128)(2,1)S(1)}, u32[]{:S(2)}, u32[]{:S(2)}) %collective-permute-start.11) | collective-permute-done | bytes 106528 | tf_op jit(solution)/shard_map/ppermute | solution.py:687
  56.2 1.8 %key_backward.1 = (bf16[256,2304]{1,0:T(8,128)(2,1)S(1)}, bf16[256,1536]{1,0:T(8,128)(2,1)S(1)}, bf16[256,1536]{1,0:T(8,128)(2,1)S(1)}) custom-call(s32[16]{0:T(128)S(1)} %concatenate.15.meta, bf16[256,1536]{1,0:T(8,128)(2,1)S(1)} %copy-done.1, bf16[160,1664]{1,0:T(8,128)(2,1)S(1)} %pad_maximum_fusion.refs_0_, ...), custom_call_target="tpu_custom_call" | custom-call | tf_op jit(solution)/shard_map/key_backward/pallas_call | solution.py:669
  60.4 2.3 %weight_grad.1 = (f32[768,384]{1,0:T(8,128)S(1)}, bf16[768,384]{1,0:T(8,128)(2,1)S(1)}, bf16[768,384]{1,0:T(8,128)(2,1)S(1)}, bf16[768,384]{1,0:T(8,128)(2,1)S(1)}) custom-call(s32[16]{0:T(128)S(1)} %concatenate.15.meta, bf16[256,1536]{1,0:T(8,128)(2,1)S(1)} %get-tuple-element.130.own, bf16[256,1536]{1,0:T(8,128)(2,1)S(1)} %collective-permute-done.18.other, ...), custom_call_target="tpu_custom_call" | custom-call | tf_op jit(solution)/shard_map/weight_grad/pallas_call | solution.py:669
  64.1 2.6 %collective-permute-start.20 = (bf16[768,384]{1,0:T(8,128)(2,1)S(1)}, bf16[768,384]{1,0:T(8,128)(2,1)S(1)}, u32[]{:S(2)}, u32[]{:S(2)}) collective-permute-start(bf16[768,384]{1,0:T(8,128)(2,1)S(1)} %get-tuple-element.142), channel_id=1, source_target_pairs={{0,64},{1,3},{2,66},{3,1},{4,68},{5,7},{6,70},{7,5},{8,72},{9,11},... | collective-permute-start | bytes 1769480 | tf_op jit(solution)/shard_map/ppermute | solution.py:721
  67.8 2.5 %token_grad.1 = (bf16[256,768]{1,0:T(8,128)(2,1)}, bf16[16,384]{1,0:T(8,128)(2,1)S(1)}) custom-call(bf16[256,2304]{1,0:T(8,128)(2,1)S(1)} %get-tuple-element.139.d_qkv, bf16[768,2304]{1,0:T(8,128)(2,1)S(1)} %copy-done, f32[256,768]{1,0:T(8,128)S(1)} %copy-done.5, f32[768]{0:T(1024)S(1)} %copy-done.9, bf16[256,768]{1,0:T(8,128)(2,1)S(1)} %copy-done.6), custom_call_target="tpu_custom_call" | custom-call | tf_op jit(solution)/shard_map/token_grad/pallas_call | solution.py:669
  73.1 7.5 %collective-permute-done.20.r2 = bf16[768,384]{1,0:T(8,128)(2,1)S(1)} collective-permute-done((bf16[768,384]{1,0:T(8,128)(2,1)S(1)}, bf16[768,384]{1,0:T(8,128)(2,1)S(1)}, u32[]{:S(2)}, u32[]{:S(2)}) %collective-permute-start.20) | collective-permute-done | bytes 589856 | tf_op jit(solution)/shard_map/ppermute | solution.py:721
  84.4 4.2 %collective-permute-done.22.r1 = bf16[208,384]{1,0:T(8,128)(2,1)S(1)} collective-permute-done((bf16[208,384]{1,0:T(8,128)(2,1)S(1)}, bf16[208,384]{1,0:T(8,128)(2,1)S(1)}, u32[]{:S(2)}, u32[]{:S(2)}) %collective-permute-start.22) | collective-permute-done | bytes 159776 | tf_op jit(solution)/shard_map/ppermute | solution.py:721
  89.9 2.2 %collective-permute-start.27 = (bf16[208,384]{1,0:T(8,128)(2,1)S(1)}, bf16[208,384]{1,0:T(8,128)(2,1)S(1)}, u32[]{:S(2)}, u32[]{:S(2)}) collective-permute-start(bf16[208,384]{1,0:T(8,128)(2,1)S(1)} %add_b.1.own), channel_id=1, source_target_pairs={{0,12},{1,97},{2,14},{3,99},{4,0},{5,101},{6,2},{7,103},{8,4},{9,1... | collective-permute-start | bytes 479240 | tf_op jit(solution)/shard_map/ppermute | solution.py:721
  93.2 2.8 %collective-permute-done.27.r3 = bf16[208,384]{1,0:T(8,128)(2,1)S(1)} collective-permute-done((bf16[208,384]{1,0:T(8,128)(2,1)S(1)}, bf16[208,384]{1,0:T(8,128)(2,1)S(1)}, u32[]{:S(2)}, u32[]{:S(2)}) %collective-permute-start.27) | collective-permute-done | bytes 159776 | tf_op jit(solution)/shard_map/ppermute | solution.py:721
  96.0 1.8 %collective-permute-done.26.r2 = bf16[208,384]{1,0:T(8,128)(2,1)S(1)} collective-permute-done((bf16[208,384]{1,0:T(8,128)(2,1)S(1)}, bf16[208,384]{1,0:T(8,128)(2,1)S(1)}, u32[]{:S(2)}, u32[]{:S(2)}) %collective-permute-start.26) | collective-permute-done | bytes 159776 | tf_op jit(solution)/shard_map/ppermute | solution.py:721
  97.8 1.9 %collective-permute-done.25.r1 = bf16[208,384]{1,0:T(8,128)(2,1)S(1)} collective-permute-done((bf16[208,384]{1,0:T(8,128)(2,1)S(1)}, bf16[208,384]{1,0:T(8,128)(2,1)S(1)}, u32[]{:S(2)}, u32[]{:S(2)}) %collective-permute-start.25) | collective-permute-done | bytes 159776 | tf_op jit(solution)/shard_map/ppermute | solution.py:721
  99.9 2.3 %collective-permute-start.30 = (bf16[208,384]{1,0:T(8,128)(2,1)S(1)}, bf16[208,384]{1,0:T(8,128)(2,1)S(1)}, u32[]{:S(2)}, u32[]{:S(2)}) collective-permute-start(bf16[208,384]{1,0:T(8,128)(2,1)S(1)} %add_c.1.own), channel_id=1, source_target_pairs={{0,18},{1,13},{2,16},{3,15},{4,22},{5,1},{6,20},{7,3},{8,26},{9,5}... | collective-permute-start | bytes 479240 | tf_op jit(solution)/shard_map/ppermute | solution.py:721
  102.8 3.3 %collective-permute-done.30.r3 = bf16[208,384]{1,0:T(8,128)(2,1)S(1)} collective-permute-done((bf16[208,384]{1,0:T(8,128)(2,1)S(1)}, bf16[208,384]{1,0:T(8,128)(2,1)S(1)}, u32[]{:S(2)}, u32[]{:S(2)}) %collective-permute-start.30) | collective-permute-done | bytes 159776 | tf_op jit(solution)/shard_map/ppermute | solution.py:721
  106.1 1.8 %collective-permute-done.29.r2 = bf16[208,384]{1,0:T(8,128)(2,1)S(1)} collective-permute-done((bf16[208,384]{1,0:T(8,128)(2,1)S(1)}, bf16[208,384]{1,0:T(8,128)(2,1)S(1)}, u32[]{:S(2)}, u32[]{:S(2)}) %collective-permute-start.29) | collective-permute-done | bytes 159776 | tf_op jit(solution)/shard_map/ppermute | solution.py:721
  110.1 3.8 %collective-permute-start.34 = (bf16[784,384]{1,0:T(8,128)(2,1)S(1)}, bf16[784,384]{1,0:T(8,128)(2,1)S(1)}, u32[]{:S(2)}, u32[]{:S(2)}) collective-permute-start(bf16[784,384]{1,0:T(8,128)(2,1)S(1)} %merge_b.1.refs_0_.refs_5_), channel_id=1, source_target_pairs={{0,1},{1,0},{2,3},{3,2},{4,5},{5,4},{6,7},{7,6},{8,9},{9,8},{10,11... | collective-permute-start | bytes 1806344 | tf_op jit(solution)/shard_map/ppermute | solution.py:682
  116.0 2.0 %finish.3 = (f32[768,2304]{1,0:T(8,128)}, f32[768,768]{1,0:T(8,128)}) custom-call(s32[16]{0:T(128)S(1)} %concatenate.15.meta, bf16[784,384]{1,0:T(8,128)(2,1)S(1)} %merge_b.1.refs_0_.refs_5_, bf16[784,384]{1,0:T(8,128)(2,1)S(1)} %collective-permute-done.34.refs_1_.refs_9_), custom_call_target="tpu_custom_call" | custom-call | tf_op jit(solution)/shard_map/finish/pallas_call | solution.py:648
  118.0 6.6 %collective-permute-done.33.refs_0_.refs_7_ = bf16[784,384]{1,0:T(8,128)(2,1)S(1)} collective-permute-done((bf16[784,384]{1,0:T(8,128)(2,1)S(1)}, bf16[784,384]{1,0:T(8,128)(2,1)S(1)}, u32[]{:S(2)}, u32[]{:S(2)}) %collective-permute-start.33) | collective-permute-done | bytes 602144 | tf_op jit(solution)/shard_map/ppermute | solution.py:721
  126.3 2.7 %collective-permute-done.32.refs_1_.refs_8_ = bf16[784,384]{1,0:T(8,128)(2,1)S(1)} collective-permute-done((bf16[784,384]{1,0:T(8,128)(2,1)S(1)}, bf16[784,384]{1,0:T(8,128)(2,1)S(1)}, u32[]{:S(2)}, u32[]{:S(2)}) %collective-permute-start.32) | collective-permute-done | bytes 602144 | tf_op jit(solution)/shard_map/ppermute | solution.py:721
  129.0 2.1 %collective-permute-done.31.refs_0_.refs_6_ = bf16[784,384]{1,0:T(8,128)(2,1)S(1)} collective-permute-done((bf16[784,384]{1,0:T(8,128)(2,1)S(1)}, bf16[784,384]{1,0:T(8,128)(2,1)S(1)}, u32[]{:S(2)}, u32[]{:S(2)}) %collective-permute-start.31) | collective-permute-done | bytes 602144 | tf_op jit(solution)/shard_map/ppermute | solution.py:721
  135.4 3.8 %finish.5 = (f32[768,2304]{1,0:T(8,128)}, f32[768,768]{1,0:T(8,128)}, f32[768]{0:T(1024)}, f32[768]{0:T(1024)}) custom-call(s32[16]{0:T(128)S(1)} %concatenate.15.meta, bf16[784,384]{1,0:T(8,128)(2,1)S(1)} %collective-permute-done.31.refs_0_.refs_6_, ...), custom_call_target="tpu_custom_call", output_to_operand_aliasing={{0}: (14, {}), {1}: (15, {})} | custom-call | tf_op jit(solution)/shard_map/finish/pallas_call | solution.py:648
  (100 shorter events, 39.7 us)
Async XLA Ops:
  5.6 10.8 %collective-permute-start.1 = (bf16[256,768]{1,0:T(8,128)(2,1)}, bf16[256,768]{1,0:T(8,128)(2,1)S(1)}, u32[]{:S(2)}, u32[]{:S(2)}) collective-permute-start(bf16[256,768]{1,0:T(8,128)(2,1)} %get-tuple-element.87.normed.norm_a), channel_id=1, source_target_pairs={{0,1},{1,0},{2,3},{3,2},{4,5},{5,4},{6,7},{7,6},{8,9},{9,8},{10,11... | collective-permute-start | bytes 1179656 | tf_op jit(solution)/shard_map/ppermute | solution.py:682
  7.1 9.3 %collective-permute-start = (bf16[80,1536]{1,0:T(8,128)(2,1)}, bf16[80,1536]{1,0:T(8,128)(2,1)S(1)}, u32[]{:S(2)}, u32[]{:S(2)}) collective-permute-start(bf16[80,1536]{1,0:T(8,128)(2,1)} %get-tuple-element.86), channel_id=1, source_target_pairs={{0,2},{1,3},{2,0},{3,1},{4,6},{5,7},{6,4},{7,5},{8,10},{9,11},{10,... | collective-permute-start | bytes 737288 | tf_op jit(solution)/shard_map/ppermute | solution.py:682
  16.5 7.4 %collective-permute-start.5 = (bf16[160,1536]{1,0:T(8,128)(2,1)S(1)}, bf16[160,1536]{1,0:T(8,128)(2,1)S(1)}, u32[]{:S(2)}, u32[]{:S(2)}) collective-permute-start(bf16[160,1536]{1,0:T(8,128)(2,1)S(1)} %pad_maximum_fusion.1.refs_0_), channel_id=1, source_target_pairs={{0,1},{1,0},{2,3},{3,2},{4,5},{5,4},{6,7},{7,6},{8,9},{9,8},{10,11... | collective-permute-start | bytes 1474568 | tf_op jit(solution)/shard_map/ppermute | solution.py:682
  17.4 9.0 %collective-permute-start.4 = (bf16[32,1536]{1,0:T(8,128)(2,1)S(1)}, bf16[32,1536]{1,0:T(8,128)(2,1)S(1)}, u32[]{:S(2)}, u32[]{:S(2)}) collective-permute-start(bf16[32,1536]{1,0:T(8,128)(2,1)S(1)} %pad_maximum_fusion.3), channel_id=1, source_target_pairs={{0,12},{1,13},{2,14},{3,15},{4,0},{5,1},{6,2},{7,3},{8,4},{9,5},{1... | collective-permute-start | bytes 294920 | tf_op jit(solution)/shard_map/ppermute | solution.py:687
  21.2 5.6 %collective-permute-start.3 = (bf16[32,1536]{1,0:T(8,128)(2,1)S(1)}, bf16[32,1536]{1,0:T(8,128)(2,1)S(1)}, u32[]{:S(2)}, u32[]{:S(2)}) collective-permute-start(bf16[32,1536]{1,0:T(8,128)(2,1)S(1)} %pad_maximum_fusion.3), channel_id=1, source_target_pairs={{0,8},{1,9},{2,10},{3,11},{4,12},{5,13},{6,14},{7,15},{8,0},{9,1},... | collective-permute-start | bytes 294920 | tf_op jit(solution)/shard_map/ppermute | solution.py:687
  21.2 7.8 %collective-permute-start.2 = (bf16[32,1536]{1,0:T(8,128)(2,1)S(1)}, bf16[32,1536]{1,0:T(8,128)(2,1)S(1)}, u32[]{:S(2)}, u32[]{:S(2)}) collective-permute-start(bf16[32,1536]{1,0:T(8,128)(2,1)S(1)} %pad_maximum_fusion.3), channel_id=1, source_target_pairs={{0,4},{1,5},{2,6},{3,7},{4,8},{5,9},{6,10},{7,11},{8,12},{9,13},{1... | collective-permute-start | bytes 294920 | tf_op jit(solution)/shard_map/ppermute | solution.py:687
  34.0 9.7 %collective-permute-start.10 = (bf16[256,768]{1,0:T(8,128)(2,1)S(1)}, bf16[256,768]{1,0:T(8,128)(2,1)S(1)}, u32[]{:S(2)}, u32[]{:S(2)}) collective-permute-start(bf16[256,768]{1,0:T(8,128)(2,1)S(1)} %get-tuple-element.137.att_a.att), channel_id=1, source_target_pairs={{0,1},{1,0},{2,3},{3,2},{4,5},{5,4},{6,7},{7,6},{8,9},{9,8},{10,11... | collective-permute-start | bytes 1179656 | tf_op jit(solution)/shard_map/ppermute | solution.py:682
  34.4 9.2 %collective-permute-start.9 = (bf16[80,1664]{1,0:T(8,128)(2,1)S(1)}, bf16[80,1664]{1,0:T(8,128)(2,1)S(1)}, u32[]{:S(2)}, u32[]{:S(2)}) collective-permute-start(bf16[80,1664]{1,0:T(8,128)(2,1)S(1)} %get-tuple-element.109), channel_id=1, source_target_pairs={{0,2},{1,3},{2,0},{3,1},{4,6},{5,7},{6,4},{7,5},{8,10},{9,11},{10,... | collective-permute-start | bytes 798728 | tf_op jit(solution)/shard_map/ppermute | solution.py:682
  43.7 2.7 %collective-permute-start.14 = (bf16[160,1664]{1,0:T(8,128)(2,1)S(1)}, bf16[160,1664]{1,0:T(8,128)(2,1)S(1)}, u32[]{:S(2)}, u32[]{:S(2)}) collective-permute-start(bf16[160,1664]{1,0:T(8,128)(2,1)S(1)} %pad_maximum_fusion.refs_0_), channel_id=1, source_target_pairs={{0,1},{1,0},{2,3},{3,2},{4,5},{5,4},{6,7},{7,6},{8,9},{9,8},{10,11... | collective-permute-start | bytes 1597448 | tf_op jit(solution)/shard_map/ppermute | solution.py:682
  44.9 5.8 %collective-permute-start.13 = (bf16[32,1664]{1,0:T(8,128)(2,1)S(1)}, bf16[32,1664]{1,0:T(8,128)(2,1)S(1)}, u32[]{:S(2)}, u32[]{:S(2)}) collective-permute-start(bf16[32,1664]{1,0:T(8,128)(2,1)S(1)} %pad_maximum_fusion.2), channel_id=1, source_target_pairs={{0,12},{1,13},{2,14},{3,15},{4,0},{5,1},{6,2},{7,3},{8,4},{9,5},{1... | collective-permute-start | bytes 319496 | tf_op jit(solution)/shard_map/ppermute | solution.py:687
  45.6 5.7 %collective-permute-start.12 = (bf16[32,1664]{1,0:T(8,128)(2,1)S(1)}, bf16[32,1664]{1,0:T(8,128)(2,1)S(1)}, u32[]{:S(2)}, u32[]{:S(2)}) collective-permute-start(bf16[32,1664]{1,0:T(8,128)(2,1)S(1)} %pad_maximum_fusion.2), channel_id=1, source_target_pairs={{0,8},{1,9},{2,10},{3,11},{4,12},{5,13},{6,14},{7,15},{8,0},{9,1},... | collective-permute-start | bytes 319496 | tf_op jit(solution)/shard_map/ppermute | solution.py:687
  46.3 7.9 %collective-permute-start.11 = (bf16[32,1664]{1,0:T(8,128)(2,1)S(1)}, bf16[32,1664]{1,0:T(8,128)(2,1)S(1)}, u32[]{:S(2)}, u32[]{:S(2)}) collective-permute-start(bf16[32,1664]{1,0:T(8,128)(2,1)S(1)} %pad_maximum_fusion.2), channel_id=1, source_target_pairs={{0,4},{1,5},{2,6},{3,7},{4,8},{5,9},{6,10},{7,11},{8,12},{9,13},{1... | collective-permute-start | bytes 319496 | tf_op jit(solution)/shard_map/ppermute | solution.py:687
  58.0 2.4 %collective-permute-start.18 = (bf16[256,1536]{1,0:T(8,128)(2,1)S(1)}, bf16[256,1536]{1,0:T(8,128)(2,1)S(1)}, u32[]{:S(2)}, u32[]{:S(2)}) collective-permute-start(bf16[256,1536]{1,0:T(8,128)(2,1)S(1)} %get-tuple-element.131), channel_id=1, source_target_pairs={{0,1},{1,0},{2,3},{3,2},{4,5},{5,4},{6,7},{7,6},{8,9},{9,8},{10,11... | collective-permute-start | bytes 2359304 | tf_op jit(solution)/shard_map/ppermute | solution.py:682
  62.8 10.4 %collective-permute-start.19 = (bf16[768,384]{1,0:T(8,128)(2,1)S(1)}, bf16[768,384]{1,0:T(8,128)(2,1)S(1)}, u32[]{:S(2)}, u32[]{:S(2)}) collective-permute-start(bf16[768,384]{1,0:T(8,128)(2,1)S(1)} %get-tuple-element.141), channel_id=1, source_target_pairs={{0,32},{1,17},{2,34},{3,19},{4,36},{5,21},{6,38},{7,23},{8,40},{9,... | collective-permute-start | bytes 1769480 | tf_op jit(solution)/shard_map/ppermute | solution.py:721
  64.1 16.5 %collective-permute-start.20 = (bf16[768,384]{1,0:T(8,128)(2,1)S(1)}, bf16[768,384]{1,0:T(8,128)(2,1)S(1)}, u32[]{:S(2)}, u32[]{:S(2)}) collective-permute-start(bf16[768,384]{1,0:T(8,128)(2,1)S(1)} %get-tuple-element.142), channel_id=1, source_target_pairs={{0,64},{1,3},{2,66},{3,1},{4,68},{5,7},{6,70},{7,5},{8,72},{9,11},... | collective-permute-start | bytes 1769480 | tf_op jit(solution)/shard_map/ppermute | solution.py:721
  66.7 13.9 %collective-permute-start.21 = (bf16[768,384]{1,0:T(8,128)(2,1)S(1)}, bf16[768,384]{1,0:T(8,128)(2,1)S(1)}, u32[]{:S(2)}, u32[]{:S(2)}) collective-permute-start(bf16[768,384]{1,0:T(8,128)(2,1)S(1)} %get-tuple-element.143), channel_id=1, source_target_pairs={{0,96},{1,19},{2,98},{3,17},{4,100},{5,23},{6,102},{7,21},{8,104},... | collective-permute-start | bytes 1769480 | tf_op jit(solution)/shard_map/ppermute | solution.py:721
  81.5 7.1 %collective-permute-start.22 = (bf16[208,384]{1,0:T(8,128)(2,1)S(1)}, bf16[208,384]{1,0:T(8,128)(2,1)S(1)}, u32[]{:S(2)}, u32[]{:S(2)}) collective-permute-start(bf16[208,384]{1,0:T(8,128)(2,1)S(1)} %get-tuple-element.149), channel_id=1, source_target_pairs={{0,16},{1,5},{2,18},{3,7},{4,20},{5,9},{6,22},{7,11},{8,24},{9,13}... | collective-permute-start | bytes 479240 | tf_op jit(solution)/shard_map/ppermute | solution.py:721
  81.5 7.0 %collective-permute-start.23 = (bf16[208,384]{1,0:T(8,128)(2,1)S(1)}, bf16[208,384]{1,0:T(8,128)(2,1)S(1)}, u32[]{:S(2)}, u32[]{:S(2)}) collective-permute-start(bf16[208,384]{1,0:T(8,128)(2,1)S(1)} %get-tuple-element.150), channel_id=1, source_target_pairs={{0,2},{1,9},{2,0},{3,11},{4,6},{5,13},{6,4},{7,15},{8,10},{9,1},{1... | collective-permute-start | bytes 479240 | tf_op jit(solution)/shard_map/ppermute | solution.py:721
  83.0 6.2 %collective-permute-start.24 = (bf16[208,384]{1,0:T(8,128)(2,1)S(1)}, bf16[208,384]{1,0:T(8,128)(2,1)S(1)}, u32[]{:S(2)}, u32[]{:S(2)}) collective-permute-start(bf16[208,384]{1,0:T(8,128)(2,1)S(1)} %get-tuple-element.151), channel_id=1, source_target_pairs={{0,18},{1,13},{2,16},{3,15},{4,22},{5,1},{6,20},{7,3},{8,26},{9,5}... | collective-permute-start | bytes 479240 | tf_op jit(solution)/shard_map/ppermute | solution.py:721
  89.9 6.2 %collective-permute-start.27 = (bf16[208,384]{1,0:T(8,128)(2,1)S(1)}, bf16[208,384]{1,0:T(8,128)(2,1)S(1)}, u32[]{:S(2)}, u32[]{:S(2)}) collective-permute-start(bf16[208,384]{1,0:T(8,128)(2,1)S(1)} %add_b.1.own), channel_id=1, source_target_pairs={{0,12},{1,97},{2,14},{3,99},{4,0},{5,101},{6,2},{7,103},{8,4},{9,1... | collective-permute-start | bytes 479240 | tf_op jit(solution)/shard_map/ppermute | solution.py:721
  92.1 5.7 %collective-permute-start.26 = (bf16[208,384]{1,0:T(8,128)(2,1)S(1)}, bf16[208,384]{1,0:T(8,128)(2,1)S(1)}, u32[]{:S(2)}, u32[]{:S(2)}) collective-permute-start(bf16[208,384]{1,0:T(8,128)(2,1)S(1)} %add_b.1.own), channel_id=1, source_target_pairs={{0,8},{1,65},{2,10},{3,67},{4,12},{5,69},{6,14},{7,71},{8,0},{9,73... | collective-permute-start | bytes 479240 | tf_op jit(solution)/shard_map/ppermute | solution.py:721
  92.7 7.0 %collective-permute-start.25 = (bf16[208,384]{1,0:T(8,128)(2,1)S(1)}, bf16[208,384]{1,0:T(8,128)(2,1)S(1)}, u32[]{:S(2)}, u32[]{:S(2)}) collective-permute-start(bf16[208,384]{1,0:T(8,128)(2,1)S(1)} %add_b.1.own), channel_id=1, source_target_pairs={{0,4},{1,33},{2,6},{3,35},{4,8},{5,37},{6,10},{7,39},{8,12},{9,41}... | collective-permute-start | bytes 479240 | tf_op jit(solution)/shard_map/ppermute | solution.py:721
  99.9 6.2 %collective-permute-start.30 = (bf16[208,384]{1,0:T(8,128)(2,1)S(1)}, bf16[208,384]{1,0:T(8,128)(2,1)S(1)}, u32[]{:S(2)}, u32[]{:S(2)}) collective-permute-start(bf16[208,384]{1,0:T(8,128)(2,1)S(1)} %add_c.1.own), channel_id=1, source_target_pairs={{0,18},{1,13},{2,16},{3,15},{4,22},{5,1},{6,20},{7,3},{8,26},{9,5}... | collective-permute-start | bytes 479240 | tf_op jit(solution)/shard_map/ppermute | solution.py:721
  102.1 5.7 %collective-permute-start.29 = (bf16[208,384]{1,0:T(8,128)(2,1)S(1)}, bf16[208,384]{1,0:T(8,128)(2,1)S(1)}, u32[]{:S(2)}, u32[]{:S(2)}) collective-permute-start(bf16[208,384]{1,0:T(8,128)(2,1)S(1)} %add_c.1.own), channel_id=1, source_target_pairs={{0,2},{1,9},{2,0},{3,11},{4,6},{5,13},{6,4},{7,15},{8,10},{9,1},{1... | collective-permute-start | bytes 479240 | tf_op jit(solution)/shard_map/ppermute | solution.py:721
  102.1 7.3 %collective-permute-start.28 = (bf16[208,384]{1,0:T(8,128)(2,1)S(1)}, bf16[208,384]{1,0:T(8,128)(2,1)S(1)}, u32[]{:S(2)}, u32[]{:S(2)}) collective-permute-start(bf16[208,384]{1,0:T(8,128)(2,1)S(1)} %add_c.1.own), channel_id=1, source_target_pairs={{0,16},{1,5},{2,18},{3,7},{4,20},{5,9},{6,22},{7,11},{8,24},{9,13}... | collective-permute-start | bytes 479240 | tf_op jit(solution)/shard_map/ppermute | solution.py:721
  110.1 5.9 %collective-permute-start.34 = (bf16[784,384]{1,0:T(8,128)(2,1)S(1)}, bf16[784,384]{1,0:T(8,128)(2,1)S(1)}, u32[]{:S(2)}, u32[]{:S(2)}) collective-permute-start(bf16[784,384]{1,0:T(8,128)(2,1)S(1)} %merge_b.1.refs_0_.refs_5_), channel_id=1, source_target_pairs={{0,1},{1,0},{2,3},{3,2},{4,5},{5,4},{6,7},{7,6},{8,9},{9,8},{10,11... | collective-permute-start | bytes 1806344 | tf_op jit(solution)/shard_map/ppermute | solution.py:682
  113.9 10.7 %collective-permute-start.33 = (bf16[784,384]{1,0:T(8,128)(2,1)S(1)}, bf16[784,384]{1,0:T(8,128)(2,1)S(1)}, u32[]{:S(2)}, u32[]{:S(2)}) collective-permute-start(bf16[784,384]{1,0:T(8,128)(2,1)S(1)} %merge_b.1.refs_0_.refs_5_), channel_id=1, source_target_pairs={{0,64},{1,3},{2,66},{3,1},{4,68},{5,7},{6,70},{7,5},{8,72},{9,11},... | collective-permute-start | bytes 1806344 | tf_op jit(solution)/shard_map/ppermute | solution.py:721
  114.5 14.5 %collective-permute-start.32 = (bf16[784,384]{1,0:T(8,128)(2,1)S(1)}, bf16[784,384]{1,0:T(8,128)(2,1)S(1)}, u32[]{:S(2)}, u32[]{:S(2)}) collective-permute-start(bf16[784,384]{1,0:T(8,128)(2,1)S(1)} %merge_b.1.refs_0_.refs_5_), channel_id=1, source_target_pairs={{0,96},{1,19},{2,98},{3,17},{4,100},{5,23},{6,102},{7,21},{8,104},... | collective-permute-start | bytes 1806344 | tf_op jit(solution)/shard_map/ppermute | solution.py:721
  115.4 15.7 %collective-permute-start.31 = (bf16[784,384]{1,0:T(8,128)(2,1)S(1)}, bf16[784,384]{1,0:T(8,128)(2,1)S(1)}, u32[]{:S(2)}, u32[]{:S(2)}) collective-permute-start(bf16[784,384]{1,0:T(8,128)(2,1)S(1)} %merge_b.1.refs_0_.refs_5_), channel_id=1, source_target_pairs={{0,32},{1,17},{2,34},{3,19},{4,36},{5,21},{6,38},{7,23},{8,40},{9,... | collective-permute-start | bytes 1806344 | tf_op jit(solution)/shard_map/ppermute | solution.py:721
  131.0 2.6 %collective-permute-start.36 = (bf16[784,384]{1,0:T(8,128)(2,1)S(1)}, bf16[784,384]{1,0:T(8,128)(2,1)S(1)}, u32[]{:S(2)}, u32[]{:S(2)}) collective-permute-start(bf16[784,384]{1,0:T(8,128)(2,1)S(1)} %collective-permute-done.31.refs_0_.refs_6_), channel_id=1, source_target_pairs={{0,1},{1,0},{2,3},{3,2},{4,5},{5,4},{6,7},{7,6},{8,9},{9,8},{10,11... | collective-permute-start | bytes 1806344 | tf_op jit(solution)/shard_map/ppermute | solution.py:682
  132.0 2.5 %collective-permute-start.37 = (bf16[784,384]{1,0:T(8,128)(2,1)S(1)}, bf16[784,384]{1,0:T(8,128)(2,1)S(1)}, u32[]{:S(2)}, u32[]{:S(2)}) collective-permute-start(bf16[784,384]{1,0:T(8,128)(2,1)S(1)} %collective-permute-done.32.refs_1_.refs_8_), channel_id=1, source_target_pairs={{0,1},{1,0},{2,3},{3,2},{4,5},{5,4},{6,7},{7,6},{8,9},{9,8},{10,11... | collective-permute-start | bytes 1806344 | tf_op jit(solution)/shard_map/ppermute | solution.py:682
  132.0 3.4 %collective-permute-start.35 = (bf16[784,384]{1,0:T(8,128)(2,1)S(1)}, bf16[784,384]{1,0:T(8,128)(2,1)S(1)}, u32[]{:S(2)}, u32[]{:S(2)}) collective-permute-start(bf16[784,384]{1,0:T(8,128)(2,1)S(1)} %collective-permute-done.33.refs_0_.refs_7_), channel_id=1, source_target_pairs={{0,1},{1,0},{2,3},{3,2},{4,5},{5,4},{6,7},{7,6},{8,9},{9,8},{10,11... | collective-permute-start | bytes 1806344 | tf_op jit(solution)/shard_map/ppermute | solution.py:682
  (17 other events, 87.7 us)
